TPU v7x, 128 devices: a whole 4x4x4 slice. The times are simulated.
128 devices in a mesh: wide: 8 (over z_hi, y), seq: 16 (over z_lo, x, core).
Axes of the slice: x: 4, y: 4, z: 4 (z_hi: 2, z_lo: 2; z = z_hi * 2 + z_lo), core: 2. Of those that a mesh axis runs over, the one named last changes fastest.
Arguments:
- tokens: bfloat16 [98304, 512], P(('wide', 'seq')), may hold values from -6 to 6
- user_ids: int32 [98304], P(('wide', 'seq')), may hold values from 0 to 31, never falling along the last dimension, each value on 1 to 6144 neighbouring positions
- in_gain: float32 [512], replicated, may hold values from 0.5 to 1.5
- out_gain: float32 [512], replicated, may hold values from 0.5 to 1.5
- w_in: bfloat16 [512, 2048], replicated, may hold values from -0.25 to 0.25
- w_out: bfloat16 [512, 512], replicated, may hold values from -0.25 to 0.25
- cotangent: bfloat16 [98304, 512], P(('wide', 'seq')), may hold values from -6 to 6
Outputs:
- layer_out: bfloat16 [98304, 512], P(('wide', 'seq'))
- grad_tokens: bfloat16 [98304, 512], P(('wide', 'seq'))
- grad_w_in: float32 [512, 2048], replicated
- grad_w_out: float32 [512, 512], replicated
Inputs may be any that keep to these rules, and one draw needn't show every extreme that they name: `user_ids`: never falling along the pack; each user holds 1 to 6144 consecutive events, one exactly 6144, and every user number occurs.
All inputs are finite; a program needn't handle non-finite values.
Results may differ from a plain program's by a relative error of at most 0.0084.
Values may be sent and summed in bfloat16 or wider, within the bound.
No kernel may reach another device: no remote copies, remote signals or barrier semaphores. Data moves between devices by JAX's collectives and lax.ppermute only.
A program may use at most 192 MiB of HBM per device.

v0:
```python
import jax
import jax.numpy as jnp
from jax import lax
from jax.sharding import PartitionSpec as P

HEADS = 4
HEAD_DIM = 128
SPAN = 2


epsilon = 1e-05


def shifted(value, axis, steps):
    count = lax.axis_size(axis)
    first, last = (max(0, -steps), min(count, count - steps))
    return lax.ppermute(value, axis, [(source, source + steps) for source in range(first, last)])


def layer_norm(values, gain):
    center = values - jnp.mean(values, axis=1, keepdims=True)
    inverse = lax.rsqrt(jnp.mean(center * center, axis=1, keepdims=True) + epsilon)
    normed = center * inverse
    return (normed * gain, normed, inverse)


def norm_backward(upstream, normed, inverse, gain):
    scaled_grad = upstream * gain
    first = jnp.mean(scaled_grad, axis=1, keepdims=True)
    second = jnp.mean(scaled_grad * normed, axis=1, keepdims=True)
    return (scaled_grad - first - normed * second) * inverse


def split_heads(matrix):
    return matrix.reshape(matrix.shape[0], HEADS, HEAD_DIM)


def pair_scores(query, keys):
    scores = jnp.einsum(
        "rhd,chd->hrc", split_heads(query), split_heads(keys), preferred_element_type=jnp.float32
    )
    return scores * HEAD_DIM ** (-0.5)


def pair_output(query, keys, values, key_mask):
    scores = pair_scores(query, keys)
    weights = jnp.where(key_mask[None], scores * jax.nn.sigmoid(scores), 0.0).astype(jnp.bfloat16)
    mixed = jnp.einsum(
        "hrc,chd->rhd", weights, split_heads(values), preferred_element_type=jnp.float32
    )
    return mixed.reshape(query.shape[0], -1)


def score_grads(query, keys, values, key_mask, grad_attn):
    scores = pair_scores(query, keys)
    logistic = jax.nn.sigmoid(scores)
    weights = jnp.where(key_mask[None], scores * logistic, 0.0).astype(jnp.bfloat16)
    grad_weights = jnp.einsum(
        "rhd,chd->hrc",
        split_heads(grad_attn),
        split_heads(values),
        preferred_element_type=jnp.float32,
    )
    slope = logistic * (1.0 + scores * (1.0 - logistic))
    grad_scores = (
        jnp.where(key_mask[None], grad_weights * slope, 0.0) * HEAD_DIM ** (-0.5)
    ).astype(jnp.bfloat16)
    return (weights, grad_scores)


def pair_backward(query, keys, values, key_mask, grad_attn):
    weights, grad_scores = score_grads(query, keys, values, key_mask, grad_attn)
    grad_query = jnp.einsum(
        "hrc,chd->rhd", grad_scores, split_heads(keys), preferred_element_type=jnp.float32
    )
    grad_keys = jnp.einsum(
        "hrc,rhd->chd", grad_scores, split_heads(query), preferred_element_type=jnp.float32
    )
    grad_values = jnp.einsum(
        "hrc,rhd->chd", weights, split_heads(grad_attn), preferred_element_type=jnp.float32
    )
    return (
        grad_query.reshape(query.shape),
        grad_keys.reshape(keys.shape),
        grad_values.reshape(values.shape),
    )


def on_device(tokens, user_ids, in_gain, out_gain, w_in, w_out, cotangent):
    local_rows, model_width = tokens.shape
    as_float = tokens.astype(jnp.float32)
    scaled_in, normed_in, inverse_in = layer_norm(as_float, in_gain)
    normed_tokens = scaled_in.astype(jnp.bfloat16)
    preact = jnp.dot(normed_tokens, w_in, preferred_element_type=jnp.float32)
    logistic = jax.nn.sigmoid(preact)
    projected = (preact * logistic).astype(jnp.bfloat16)
    u_part = projected[:, :model_width]
    query = projected[:, model_width : 2 * model_width]
    keys = projected[:, 2 * model_width : 3 * model_width]
    values = projected[:, 3 * model_width :]
    key_values = projected[:, 2 * model_width :]
    positions = jnp.arange(local_rows, dtype=jnp.int32)
    local_mask = (user_ids[:, None] == user_ids[None, :]) & (
        positions[None, :] <= positions[:, None]
    )
    arrived = []
    for distance in range(1, SPAN + 1):
        arrived.append(shifted((key_values, user_ids), ("wide", "seq"), distance))
    remote_inputs = []
    for offset, (remote_pair, remote_ids) in enumerate(arrived):
        distance = offset + 1
        in_window = positions[None, :] > positions[:, None] - (SPAN - distance) * local_rows
        remote_mask = (user_ids[:, None] == remote_ids[None, :]) & in_window
        remote_inputs.append(
            (remote_pair[:, :model_width], remote_pair[:, model_width:], remote_mask)
        )
    mixed = pair_output(query, keys, values, local_mask)
    for remote_keys, remote_values, remote_mask in remote_inputs:
        mixed = mixed + pair_output(query, remote_keys, remote_values, remote_mask)
    scaled_out, normed_out, inverse_out = layer_norm(mixed, out_gain)
    u_float = u_part.astype(jnp.float32)
    gated = (scaled_out * u_float).astype(jnp.bfloat16)
    layer_out = (as_float + jnp.dot(gated, w_out, preferred_element_type=jnp.float32)).astype(
        jnp.bfloat16
    )
    grad_gated = jnp.einsum("re,de->rd", cotangent, w_out, preferred_element_type=jnp.float32)
    grad_u = grad_gated * scaled_out
    grad_attn = norm_backward(grad_gated * u_float, normed_out, inverse_out, out_gain).astype(
        jnp.bfloat16
    )
    grad_query, grad_keys, grad_values = pair_backward(query, keys, values, local_mask, grad_attn)
    grad_pairs = jnp.concatenate([grad_keys, grad_values], axis=1)
    partials = []
    for remote_keys, remote_values, remote_mask in remote_inputs:
        query_term, keys_term, values_term = pair_backward(
            query, remote_keys, remote_values, remote_mask, grad_attn
        )
        grad_query = grad_query + query_term
        partials.append(jnp.concatenate([keys_term, values_term], axis=1))
    for distance in range(1, SPAN + 1):
        grad_pairs = grad_pairs + shifted(
            partials[distance - 1].astype(jnp.bfloat16), ("wide", "seq"), -distance
        ).astype(jnp.float32)
    grad_proj = jnp.concatenate([grad_u, grad_query, grad_pairs], axis=1)
    grad_preact = (grad_proj * logistic * (1.0 + preact * (1.0 - logistic))).astype(jnp.bfloat16)
    local_w_in = jnp.einsum(
        "rd,rf->df", normed_tokens, grad_preact, preferred_element_type=jnp.float32
    )
    local_w_out = jnp.einsum("rd,re->de", gated, cotangent, preferred_element_type=jnp.float32)
    grad_w_in, grad_w_out = lax.psum((local_w_in, local_w_out), ("wide", "seq"))
    grad_normed = jnp.einsum("rf,df->rd", grad_preact, w_in, preferred_element_type=jnp.float32)
    grad_tokens = (
        cotangent.astype(jnp.float32) + norm_backward(grad_normed, normed_in, inverse_in, in_gain)
    ).astype(jnp.bfloat16)
    return (layer_out, grad_tokens, grad_w_in, grad_w_out)


def solution(mesh):
    placed = (
        P(("wide", "seq"), None),
        P(("wide", "seq")),
        P(),
        P(),
        P(),
        P(),
        P(("wide", "seq"), None),
    )
    return jax.shard_map(
        on_device,
        mesh=mesh,
        in_specs=placed,
        out_specs=(P(("wide", "seq"), None), P(("wide", "seq"), None), P(), P()),
        check_vma=False,
    )
```

profile of v0, /device:TPU:39, one launch (start us, length us, event | category | flops | bytes accessed | tf_op | source)
XLA Modules:
  0.0 419.0 jit_solution(17932485386486492964)
XLA Ops:
  7.2 2.8 collective-permute-start.3
  10.0 4.0 collective-permute-start.1
  16.8 6.2 %multiply_convert_fusion.3 = (bf16[768,2048]{1,0:T(8,128)(2,1)S(1)}, f32[768,2048]{1,0:T(8,128)}) fusion(bf16[512,2048]{1,0:T(8,128)(2,1)S(1)} %copy-done, bf16[768,512]{1,0:T(8,128)(2,1)} %param.7, f32[512]{0:T(512)} %param.9, f32[768]{0:T(1024)S(1)} %add_rsqrt_fusion.1, f32[768]{0:T(1024)S(1)} %broadcast_multiply_fusion.5), kind=kOutput, calls=%fused_computation.12 | convolution fusion | flops 1620443136 | bytes 12328960 | tf_op jit(solution)/shard_map/dot_general | solution.py:94
  24.4 3.2 collective-permute-start.2
  27.7 2.7 collective-permute-start
  34.4 2.6 fusion.5
  37.0 7.4 %select_convert_fusion.2 = (bf16[4,768,768]{2,1,0:T(8,128)(2,1)S(1)}, f32[4,768,768]{2,1,0:T(8,128)}) fusion(pred[768,768]{1,0:T(8,128)(4,1)S(1)} %get-tuple-element.21, bf16[768,4,128]{0,2,1:T(8,128)(2,1)S(1)} %bitcast.100, bf16[768,4,128]{0,2,1:T(8,128)(2,1)} %bitcast.122), kind=kOutput, calls=%fused_computation.7 | convolution fusion | flops 620494848 | bytes 16318464 | tf_op jit(solution)/shard_map/rhd,chd->hrc/dot_general | solution.py:39
  44.5 2.9 fusion.26
  47.4 14.9 %collective-permute-done.2 = bf16[768,1024]{1,0:T(8,128)(2,1)} collective-permute-done((bf16[768,1024]{1,0:T(8,128)(2,1)}, bf16[768,1024]{1,0:T(8,128)(2,1)}, u32[]{:S(2)}, u32[]{:S(2)}) %collective-permute-start.2) | collective-permute-done | bytes 1572896 | tf_op jit(solution)/shard_map/ppermute | solution.py:17
  62.2 2.7 slice_bitcast_fusion
  64.9 2.3 copy.59
  67.3 11.1 %collective-permute-done = bf16[768,1024]{1,0:T(8,128)(2,1)} collective-permute-done((bf16[768,1024]{1,0:T(8,128)(2,1)}, bf16[768,1024]{1,0:T(8,128)(2,1)}, u32[]{:S(2)}, u32[]{:S(2)}) %collective-permute-start) | collective-permute-done | bytes 1572896 | tf_op jit(solution)/shard_map/ppermute | solution.py:17
  78.4 2.7 slice_bitcast_fusion.1
  81.1 2.3 copy.58
  83.4 7.4 %select_convert_fusion = (bf16[4,768,768]{2,1,0:T(8,128)(2,1)S(1)}, f32[4,768,768]{2,1,0:T(8,128)}) fusion(pred[768,768]{1,0:T(8,128)(4,1)} %get-tuple-element.20, bf16[768,4,128]{0,2,1:T(8,128)(2,1)S(1)} %bitcast.101, bf16[768,4,128]{0,2,1:T(8,128)(2,1)} %bitcast.124), kind=kOutput, calls=%fused_computation.3 | convolution fusion | flops 620494848 | bytes 16318464 | tf_op jit(solution)/shard_map/rhd,chd->hrc/dot_general | solution.py:39
  90.8 6.3 %select_convert_fusion.1 = (bf16[4,768,768]{2,1,0:T(8,128)(2,1)S(1)}, f32[4,768,768]{2,1,0:T(8,128)}) fusion(pred[768,768]{1,0:T(8,128)(4,1)S(1)} %copy-done.31, bf16[768,4,128]{0,2,1:T(8,128)(2,1)S(1)} %bitcast.102, bf16[768,4,128]{0,2,1:T(8,128)(2,1)S(1)} %bitcast.126), kind=kOutput, calls=%fused_computation.5 | convolution fusion | flops 620494848 | bytes 16318464 | tf_op jit(solution)/shard_map/rhd,chd->hrc/dot_general | solution.py:39
  103.6 3.0 copy.48
  106.6 3.1 fusion.35
  109.7 3.1 multiply_convert_fusion.4
  112.8 2.3 copy.60
  115.2 4.4 %convolution_convert_fusion = bf16[4,128,768]{2,1,0:T(8,128)(2,1)} fusion(bf16[768,4,128]{0,2,1:T(8,128)(2,1)} %bitcast.106, bf16[4,768,768]{2,1,0:T(8,128)(2,1)} %copy-done.1), kind=kOutput, calls=%fused_computation.52 | convolution fusion | flops 604372992 | bytes 6291456 | tf_op jit(solution)/shard_map/hrc,rhd->chd/dot_general | solution.py:79
  123.4 9.6 %multiply_convert_fusion = bf16[4,768,768]{2,1,0:T(8,128)(2,1)} fusion(f32[4,768,768]{2,1,0:T(8,128)} %get-tuple-element.30, pred[768,768]{1,0:T(8,128)(4,1)S(1)} %copy-done.33, bf16[768,4,128]{0,2,1:T(8,128)(2,1)S(1)} %bitcast.109, bf16[96,4,8,128]{3,2,1,0:T(8,128)(2,1)S(1)} %copy-done.21), kind=kOutput, calls=%fused_computation | convolution fusion | flops 632291328 | bytes 16318464 | tf_op jit(solution)/shard_map/rhd,chd->hrc/dot_general | solution.py:58
  133.0 7.3 %multiply_convert_fusion.1 = bf16[4,768,768]{2,1,0:T(8,128)(2,1)} fusion(f32[4,768,768]{2,1,0:T(8,128)S(1)} %bitcast.131, pred[768,768]{1,0:T(8,128)(4,1)S(1)} %copy-done.32, bf16[768,4,128]{0,2,1:T(8,128)(2,1)S(1)} %bitcast.110, bf16[96,4,8,128]{3,2,1,0:T(8,128)(2,1)S(1)} %copy-done.23), kind=kOutput, calls=%fused_computation.1 | convolution fusion | flops 632291328 | bytes 16318464 | tf_op jit(solution)/shard_map/rhd,chd->hrc/dot_general | solution.py:58
  140.4 7.1 %multiply_convert_fusion.2 = bf16[4,768,768]{2,1,0:T(8,128)(2,1)} fusion(f32[4,768,768]{2,1,0:T(8,128)S(1)} %bitcast.129, pred[768,768]{1,0:T(8,128)(4,1)S(1)} %copy-done.30, bf16[768,4,128]{0,2,1:T(8,128)(2,1)S(1)} %bitcast.111, bf16[96,4,8,128]{3,2,1,0:T(8,128)(2,1)S(1)} %copy-done.15), kind=kOutput, calls=%fused_computation.2 | convolution fusion | flops 632291328 | bytes 16318464 | tf_op jit(solution)/shard_map/rhd,chd->hrc/dot_general | solution.py:58
  147.5 3.1 copy.51
  150.5 2.3 copy.53
  152.8 2.3 copy.55
  155.1 4.3 %fusion.44 = f32[4,128,768]{2,1,0:T(8,128)} fusion(bf16[768,4,128]{0,2,1:T(8,128)(2,1)S(1)} %bitcast.103, bf16[4,768,768]{2,1,0:T(8,128)(2,1)} %multiply_convert_fusion.2), kind=kOutput, calls=%fused_computation.89 | convolution fusion | flops 603979776 | bytes 7077888 | tf_op jit(solution)/shard_map/hrc,rhd->chd/dot_general | solution.py:76
  159.4 3.2 copy.50
  162.6 4.2 convolution_convert_fusion.3
  168.4 2.4 copy.54
  170.8 2.3 copy.52
  173.2 2.8 pad_maximum_fusion
  176.0 3.5 collective-permute-start.4
  180.9 3.1 collective-permute-start.5
  184.1 3.9 fusion.42
  189.8 2.8 add_add_fusion
  192.5 3.1 copy.49
  195.7 2.8 fusion.46
  198.5 16.7 %collective-permute-done.4 = bf16[768,1024]{1,0:T(8,128)(2,1)} collective-permute-done((bf16[768,1024]{1,0:T(8,128)(2,1)}, bf16[768,1024]{1,0:T(8,128)(2,1)}, u32[]{:S(2)}, u32[]{:S(2)}) %collective-permute-start.4) | collective-permute-done | bytes 1572896 | tf_op jit(solution)/shard_map/ppermute | solution.py:17
  215.2 7.7 %collective-permute-done.5 = bf16[768,1024]{1,0:T(8,128)(2,1)} collective-permute-done((bf16[768,1024]{1,0:T(8,128)(2,1)}, bf16[768,1024]{1,0:T(8,128)(2,1)}, u32[]{:S(2)}, u32[]{:S(2)}) %collective-permute-start.5) | collective-permute-done | bytes 1572896 | tf_op jit(solution)/shard_map/ppermute | solution.py:17
  222.9 3.1 fusion.2
  226.1 4.3 %fusion.1 = bf16[768,2048]{1,0:T(8,128)(2,1)S(1)} fusion(f32[768,1024]{1,0:T(8,128)S(1)} %fusion.2, f32[768,512]{1,0:T(8,128)S(1)} %copy-done.12, f32[768,512]{1,0:T(8,128)S(1)} %copy-done.13, f32[768,2048]{1,0:T(8,128)} %get-tuple-element.24), kind=kLoop, calls=%fused_computation.11 | loop fusion | flops 17301504 | bytes 15728640 | tf_op jit(solution)/shard_map/convert_element_type | solution.py:145
  232.0 4.0 fusion.36
  236.1 2.7 fusion.20
  238.8 3.9 fusion.40
  244.2 161.9 %all-reduce.3.cloned.1.call-done = (f32[512,2048]{1,0:T(8,128)}, f32[512,512]{1,0:T(8,128)}) async-done(((f32[512,2048]{1,0:T(8,128)}, f32[512,512]{1,0:T(8,128)}), (f32[512,2048]{1,0:T(8,128)}, f32[512,512]{1,0:T(8,128)})) %all-reduce.3.cloned.1.call-update) | async-done | bytes 5242896 | tf_op jit(solution)/shard_map/psum | solution.py:150
  406.1 4.8 %copy.92 = f32[512,2048]{1,0:T(8,128)} copy(f32[512,2048]{1,0:T(8,128)} %get-tuple-element.39) | data formatting | bytes 8388608
  (141 shorter events, 27.3 us)
Async XLA Ops:
  7.2 9.7 %copy-start = (bf16[512,2048]{1,0:T(8,128)(2,1)S(1)}, bf16[512,2048]{1,0:T(8,128)(2,1)}, u32[]{:S(2)}) copy-start(bf16[512,2048]{1,0:T(8,128)(2,1)} %param.11) | copy-start | bytes 6291460
  7.2 398.9 %all-reduce.3.cloned.1.call-start = ((), (), s32[]{:S(2)}) async-start(), calls=%async_computation | async-start | bytes 10485760 | tf_op jit(solution)/shard_map/psum | solution.py:150
  7.2 27.1 %collective-permute-start.3 = (s32[768]{0:T(1024)}, s32[768]{0:T(1024)S(1)}, u32[]{:S(2)}, u32[]{:S(2)}) collective-permute-start(s32[768]{0:T(1024)} %param.8), channel_id=1, source_target_pairs={{0,2},{1,3},{2,4},{3,5},{4,6},{5,7},{6,8},{7,9},{8,10},{9,11},{10,... | collective-permute-start | bytes 9224 | tf_op jit(solution)/shard_map/ppermute | solution.py:17
  10.0 24.3 %collective-permute-start.1 = (s32[768]{0:T(1024)}, s32[768]{0:T(1024)S(1)}, u32[]{:S(2)}, u32[]{:S(2)}) collective-permute-start(s32[768]{0:T(1024)} %param.8), channel_id=1, source_target_pairs={{0,1},{1,2},{2,3},{3,4},{4,5},{5,6},{6,7},{7,8},{8,9},{9,10},{10,1... | collective-permute-start | bytes 9224 | tf_op jit(solution)/shard_map/ppermute | solution.py:17
  23.0 8.8 %copy-start.8 = (bf16[768,2048]{1,0:T(8,128)(2,1)}, bf16[768,2048]{1,0:T(8,128)(2,1)S(1)}, u32[]{:S(2)}) copy-start(bf16[768,2048]{1,0:T(8,128)(2,1)S(1)} %get-tuple-element.23) | copy-start | bytes 9437188
  24.4 10.0 %copy-start.35 = (s32[768]{0:T(1024)S(1)}, s32[768]{0:T(1024)}, u32[]{:S(2)}) copy-start(s32[768]{0:T(1024)} %param.8) | copy-start | bytes 9220
  24.4 37.8 %collective-permute-start.2 = (bf16[768,1024]{1,0:T(8,128)(2,1)}, bf16[768,1024]{1,0:T(8,128)(2,1)}, u32[]{:S(2)}, u32[]{:S(2)}) collective-permute-start(bf16[768,1024]{1,0:T(8,128)(2,1)} %slice.39), channel_id=1, source_target_pairs={{0,2},{1,3},{2,4},{3,5},{4,6},{5,7},{6,8},{7,9},{8,10},{9,11},{10,... | collective-permute-start | bytes 4718600 | tf_op jit(solution)/shard_map/ppermute | solution.py:17
  27.7 50.7 %collective-permute-start = (bf16[768,1024]{1,0:T(8,128)(2,1)}, bf16[768,1024]{1,0:T(8,128)(2,1)}, u32[]{:S(2)}, u32[]{:S(2)}) collective-permute-start(bf16[768,1024]{1,0:T(8,128)(2,1)} %slice.39), channel_id=1, source_target_pairs={{0,1},{1,2},{2,3},{3,4},{4,5},{5,6},{6,7},{7,8},{8,9},{9,10},{10,1... | collective-permute-start | bytes 4718600 | tf_op jit(solution)/shard_map/ppermute | solution.py:17
  37.0 7.4 %copy-start.29 = (pred[768,768]{1,0:T(8,128)(4,1)}, pred[768,768]{1,0:T(8,128)(4,1)S(1)}, u32[]{:S(2)}) copy-start(pred[768,768]{1,0:T(8,128)(4,1)S(1)} %get-tuple-element.21) | copy-start | bytes 1769476
  37.0 7.4 %copy-start.14 = (bf16[96,4,8,128]{3,2,1,0:T(8,128)(2,1)S(1)}, bf16[96,4,8,128]{3,2,1,0:T(8,128)(2,1)}, u32[]{:S(2)}) copy-start(bf16[96,4,8,128]{3,2,1,0:T(8,128)(2,1)} %get-tuple-element.13) | copy-start | bytes 2359300
  83.4 7.4 %copy-start.18 = (bf16[768,512]{0,1:T(8,128)(2,1)S(1)}, bf16[768,512]{0,1:T(8,128)(2,1)}, u32[]{:S(2)}) copy-start(bf16[768,512]{0,1:T(8,128)(2,1)} %copy.58) | copy-start | bytes 2359300
  83.4 7.4 %copy-start.31 = (pred[768,768]{1,0:T(8,128)(4,1)S(1)}, pred[768,768]{1,0:T(8,128)(4,1)}, u32[]{:S(2)}) copy-start(pred[768,768]{1,0:T(8,128)(4,1)} %get-tuple-element.22) | copy-start | bytes 1769476
  90.8 8.7 %copy-start.1 = (bf16[4,768,768]{2,1,0:T(8,128)(2,1)}, bf16[4,768,768]{2,1,0:T(8,128)(2,1)S(1)}, u32[]{:S(2)}) copy-start(bf16[4,768,768]{2,1,0:T(8,128)(2,1)S(1)} %get-tuple-element.29) | copy-start | bytes 14155780
  90.8 6.3 %copy-start.22 = (bf16[96,4,8,128]{3,2,1,0:T(8,128)(2,1)S(1)}, bf16[96,4,8,128]{3,2,1,0:T(8,128)(2,1)}, u32[]{:S(2)}) copy-start(bf16[96,4,8,128]{3,2,1,0:T(8,128)(2,1)} %get-tuple-element.18) | copy-start | bytes 2359300
  102.2 4.4 %copy-start.36 = (f32[512]{0:T(512)S(1)}, f32[512]{0:T(512)}, u32[]{:S(2)}) copy-start(f32[512]{0:T(512)} %param.10) | copy-start | bytes 6148
  112.8 6.8 %slice-start.4 = ((s8[4718592]{0:T(1024)(128)(4,1)}), s8[524288]{0:T(1024)(128)(4,1)S(1)}, s32[]{:S(2)}) async-start(s8[4718592]{0:T(1024)(128)(4,1)} %bitcast.96), calls=%async_computation.5 | async-start | bytes 1048576
  115.2 4.4 %slice-start.5 = ((s8[4718592]{0:T(1024)(128)(4,1)}), s8[4194304]{0:T(1024)(128)(4,1)S(1)}, s32[]{:S(2)}) async-start(s8[4718592]{0:T(1024)(128)(4,1)} %bitcast.96), calls=%async_computation.6 | async-start | bytes 8388608
  115.2 4.4 %copy-start.3 = (bf16[768,512]{0,1:T(8,128)(2,1)S(1)}, bf16[768,512]{0,1:T(8,128)(2,1)}, u32[]{:S(2)}) copy-start(bf16[768,512]{0,1:T(8,128)(2,1)} %copy.60) | copy-start | bytes 2359300
  115.2 6.2 %slice-start.8 = ((s8[4718592]{0:T(1024)(128)(4,1)}), s8[4194304]{0:T(1024)(128)(4,1)S(1)}, s32[]{:S(2)}) async-start(s8[4718592]{0:T(1024)(128)(4,1)} %bitcast.112), calls=%async_computation.9 | async-start | bytes 8388608
  121.3 11.6 %slice-start.13 = ((s8[9437184]{0:T(1024)(128)(4,1)}), s8[4194304]{0:T(1024)(128)(4,1)S(1)}, s32[]{:S(2)}) async-start(s8[9437184]{0:T(1024)(128)(4,1)} %bitcast.130), calls=%async_computation.14 | async-start | bytes 8388608
  123.3 9.6 %copy-start.23 = (bf16[96,4,8,128]{3,2,1,0:T(8,128)(2,1)S(1)}, bf16[96,4,8,128]{3,2,1,0:T(8,128)(2,1)}, u32[]{:S(2)}) copy-start(bf16[96,4,8,128]{3,2,1,0:T(8,128)(2,1)} %get-tuple-element.18) | copy-start | bytes 2359300
  123.3 9.6 %copy-start.32 = (pred[768,768]{1,0:T(8,128)(4,1)S(1)}, pred[768,768]{1,0:T(8,128)(4,1)}, u32[]{:S(2)}) copy-start(pred[768,768]{1,0:T(8,128)(4,1)} %get-tuple-element.22) | copy-start | bytes 1769476
  123.3 9.6 %slice-start.14 = ((s8[9437184]{0:T(1024)(128)(4,1)}), s8[4194304]{0:T(1024)(128)(4,1)S(1)}, s32[]{:S(2)}) async-start(s8[9437184]{0:T(1024)(128)(4,1)} %bitcast.130), calls=%async_computation.15 | async-start | bytes 8388608
  123.3 9.6 %slice-start.15 = ((s8[9437184]{0:T(1024)(128)(4,1)}), s8[1048576]{0:T(1024)(128)(4,1)S(1)}, s32[]{:S(2)}) async-start(s8[9437184]{0:T(1024)(128)(4,1)} %bitcast.130), calls=%async_computation.16 | async-start | bytes 2097152
  123.3 17.0 %slice-start.10 = ((s8[9437184]{0:T(1024)(128)(4,1)}), s8[4194304]{0:T(1024)(128)(4,1)S(1)}, s32[]{:S(2)}) async-start(s8[9437184]{0:T(1024)(128)(4,1)} %bitcast.128), calls=%async_computation.11 | async-start | bytes 8388608
  123.4 17.0 %slice-start.11 = ((s8[9437184]{0:T(1024)(128)(4,1)}), s8[4194304]{0:T(1024)(128)(4,1)S(1)}, s32[]{:S(2)}) async-start(s8[9437184]{0:T(1024)(128)(4,1)} %bitcast.128), calls=%async_computation.12 | async-start | bytes 8388608
  133.0 7.4 %copy-start.15 = (bf16[96,4,8,128]{3,2,1,0:T(8,128)(2,1)S(1)}, bf16[96,4,8,128]{3,2,1,0:T(8,128)(2,1)}, u32[]{:S(2)}) copy-start(bf16[96,4,8,128]{3,2,1,0:T(8,128)(2,1)} %get-tuple-element.13) | copy-start | bytes 2359300
  133.0 7.4 %copy-start.30 = (pred[768,768]{1,0:T(8,128)(4,1)S(1)}, pred[768,768]{1,0:T(8,128)(4,1)}, u32[]{:S(2)}) copy-start(pred[768,768]{1,0:T(8,128)(4,1)} %copy-done.29) | copy-start | bytes 1769476
  133.0 7.4 %slice-start.12 = ((s8[9437184]{0:T(1024)(128)(4,1)}), s8[1048576]{0:T(1024)(128)(4,1)S(1)}, s32[]{:S(2)}) async-start(s8[9437184]{0:T(1024)(128)(4,1)} %bitcast.128), calls=%async_computation.13 | async-start | bytes 2097152
  159.4 7.3 %slice-start = ((s8[4718592]{0:T(1024)(128)(4,1)}), s8[524288]{0:T(1024)(128)(4,1)S(1)}, s32[]{:S(2)}) async-start(s8[4718592]{0:T(1024)(128)(4,1)} %bitcast.92), calls=%async_computation.1 | async-start | bytes 1048576
  162.6 4.2 slice-start.1
  168.4 11.1 %copy-start.24 = (bf16[768,512]{1,0:T(8,128)(2,1)S(1)}, bf16[768,512]{1,0:T(8,128)(2,1)}, u32[]{:S(2)}) copy-start(bf16[768,512]{1,0:T(8,128)(2,1)} %copy.55) | copy-start | bytes 2359300
  170.8 17.2 %slice-start.6 = ((s8[4718592]{0:T(1024)(128)(4,1)}), s8[524288]{0:T(1024)(128)(4,1)S(1)}, s32[]{:S(2)}) async-start(s8[4718592]{0:T(1024)(128)(4,1)} %bitcast.98), calls=%async_computation.7 | async-start | bytes 1048576
  173.2 6.4 %copy-start.25 = (bf16[768,512]{1,0:T(8,128)(2,1)S(1)}, bf16[768,512]{1,0:T(8,128)(2,1)}, u32[]{:S(2)}) copy-start(bf16[768,512]{1,0:T(8,128)(2,1)} %copy.54) | copy-start | bytes 2359300
  173.2 10.9 %copy-start.16 = (bf16[768,512]{0,1:T(8,128)(2,1)S(1)}, bf16[768,512]{0,1:T(8,128)(2,1)}, u32[]{:S(2)}) copy-start(bf16[768,512]{0,1:T(8,128)(2,1)} %copy.57) | copy-start | bytes 2359300
  176.0 12.1 %slice-start.7 = ((s8[4718592]{0:T(1024)(128)(4,1)}), s8[4194304]{0:T(1024)(128)(4,1)S(1)}, s32[]{:S(2)}) async-start(s8[4718592]{0:T(1024)(128)(4,1)} %bitcast.98), calls=%async_computation.8 | async-start | bytes 8388608
  176.0 39.2 %collective-permute-start.4 = (bf16[768,1024]{1,0:T(8,128)(2,1)}, bf16[768,1024]{1,0:T(8,128)(2,1)}, u32[]{:S(2)}, u32[]{:S(2)}) collective-permute-start(bf16[768,1024]{1,0:T(8,128)(2,1)} %pad_maximum_fusion), channel_id=1, source_target_pairs={{1,0},{2,1},{3,2},{4,3},{5,4},{6,5},{7,6},{8,7},{9,8},{10,9},{11,1... | collective-permute-start | bytes 4718600 | tf_op jit(solution)/shard_map/ppermute | solution.py:17
  179.6 10.2 %slice-start.2 = ((s8[4718592]{0:T(1024)(128)(4,1)}), s8[4194304]{0:T(1024)(128)(4,1)S(1)}, s32[]{:S(2)}) async-start(s8[4718592]{0:T(1024)(128)(4,1)} %bitcast.94), calls=%async_computation.3 | async-start | bytes 8388608
  180.9 7.1 %copy-start.19 = (bf16[768,512]{0,1:T(8,128)(2,1)S(1)}, bf16[768,512]{0,1:T(8,128)(2,1)}, u32[]{:S(2)}) copy-start(bf16[768,512]{0,1:T(8,128)(2,1)} %copy.58) | copy-start | bytes 2359300
  180.9 8.8 %slice-start.3 = ((s8[4718592]{0:T(1024)(128)(4,1)}), s8[524288]{0:T(1024)(128)(4,1)S(1)}, s32[]{:S(2)}) async-start(s8[4718592]{0:T(1024)(128)(4,1)} %bitcast.94), calls=%async_computation.4 | async-start | bytes 1048576
  180.9 41.9 %collective-permute-start.5 = (bf16[768,1024]{1,0:T(8,128)(2,1)}, bf16[768,1024]{1,0:T(8,128)(2,1)}, u32[]{:S(2)}, u32[]{:S(2)}) collective-permute-start(bf16[768,1024]{1,0:T(8,128)(2,1)} %pad_maximum_fusion.1), channel_id=1, source_target_pairs={{2,0},{3,1},{4,2},{5,3},{6,4},{7,5},{8,6},{9,7},{10,8},{11,9},{12,... | collective-permute-start | bytes 4718600 | tf_op jit(solution)/shard_map/ppermute | solution.py:17
  195.7 27.2 %copy-start.10 = (f32[768,512]{1,0:T(8,128)S(1)}, f32[768,512]{1,0:T(8,128)}, u32[]{:S(2)}) copy-start(f32[768,512]{1,0:T(8,128)} %copy.51) | copy-start | bytes 4718596
  198.5 27.5 %copy-start.12 = (f32[768,512]{1,0:T(8,128)S(1)}, f32[768,512]{1,0:T(8,128)}, u32[]{:S(2)}) copy-start(f32[768,512]{1,0:T(8,128)} %copy.49) | copy-start | bytes 4718596
  198.5 27.5 %copy-start.13 = (f32[768,512]{1,0:T(8,128)S(1)}, f32[768,512]{1,0:T(8,128)}, u32[]{:S(2)}) copy-start(f32[768,512]{1,0:T(8,128)} %get-tuple-element.12) | copy-start | bytes 4718596
  226.0 6.0 %copy-start.6 = (bf16[768,512]{1,0:T(8,128)(2,1)S(1)}, bf16[768,512]{1,0:T(8,128)(2,1)}, u32[]{:S(2)}) copy-start(bf16[768,512]{1,0:T(8,128)(2,1)} %param.7) | copy-start | bytes 2359300
  226.1 6.0 %copy-start.34 = (f32[512]{0:T(512)S(1)}, f32[512]{0:T(512)}, u32[]{:S(2)}) copy-start(f32[512]{0:T(512)} %param.9) | copy-start | bytes 6148
  238.8 4.0 copy-start.27
  406.1 4.8 %copy-start.28 = (f32[512,512]{1,0:T(8,128)S(1)}, f32[512,512]{1,0:T(8,128)}, u32[]{:S(2)}) copy-start(f32[512,512]{1,0:T(8,128)} %get-tuple-element.40) | copy-start | bytes 3145732
  (12 other events, 27.6 us)
Sparse Core Ops, SparseCore 0:
  236.2 169.8 all-reduce.2
where the time goes:
time: 426 us; the launch traced here: 419 us
  waiting for transfers between devices  212 us (50%)
  matrix products  101 us (24%)
  local copies, waits for them, and re-layouts  49.7 us (12%)
  other arithmetic  21.9 us (5%)
  starting transfers between devices  19.4 us (5%)
  between operations  14.9 us (3%)
    psum x1, waiting for transfers between devices, on_device(): grad_w_in, grad_w_out = lax.psum((local_w_in, local_w_out), ('wide', 'seq'))  162 us
    ppermute x6, waiting for transfers between devices, shifted(): lax.ppermute(value, axis, [(source, source + steps) for source in range(f...  50.4 us
    dot_general x3, matrix products, score_grads(): jnp.einsum('rhd,chd->hrc', split_heads(grad_attn), split_heads(values), p...  24 us
    dot_general x3, matrix products, pair_scores(): jnp.einsum('rhd,chd->hrc', split_heads(query), split_heads(keys), preferr...  21.1 us
    ppermute x6, starting transfers between devices, shifted(): lax.ppermute(value, axis, [(source, source + steps) for source in range(f...  19.4 us
    unnamed x111, local copies, waits for them, and re-layouts  17.1 us
    dot_general x3, matrix products, pair_backward(): jnp.einsum('hrc,rhd->chd', grad_scores, split_heads(query), preferred_ele...  10.1 us
    reshape x5, local copies, waits for them, and re-layouts, split_heads(): return matrix.reshape(matrix.shape[0], HEADS, HEAD_DIM)  9.53 us
  transfers between devices with their start and end apart: 7, of which 5 were waited for; matrix products, arithmetic and copies ran while one was open for 13% of the time, Pallas kernels for 0%

commit v1 on v0

v1 whole, which is shorter than its diff:
```python
import jax
import jax.numpy as jnp
from jax import lax
from jax.experimental import pallas as pl
from jax.experimental.pallas import tpu as pltpu
from jax.sharding import Mesh
from jax.sharding import PartitionSpec as P

HEADS = 4
HEAD_DIM = 128
ROWS = 768
WIDTH = 512
WINDOW_ROWS = 3 * ROWS
HALO = 2 * ROWS
TILE = 256
TILES = ROWS // TILE
SPREAD = 7
HALF_SCALE = 0.5 * HEAD_DIM ** (-0.5)
EPSILON = 1e-05
BLOCKS = 5 * HEADS
HALF_BLOCKS = BLOCKS // 2

ALL = ("z_hi", "y", "z_lo", "x", "core")
CHIPS = ("z_hi", "y", "z_lo", "x")
MIB = 1024 * 1024

f32 = jnp.float32
bf16 = jnp.bfloat16


def dot(left, right):
    return lax.dot_general(left, right, (((1,), (0,)), ((), ())), preferred_element_type=f32)


def dot_nt(left, right):
    return lax.dot_general(left, right, (((1,), (1,)), ((), ())), preferred_element_type=f32)


def layer_norm_rows(values):
    center = values - jnp.mean(values, axis=1, keepdims=True)
    inverse = lax.rsqrt(jnp.mean(center * center, axis=1, keepdims=True) + EPSILON)
    return center * inverse, inverse


def silu_and_slope(value):
    half = 0.5 * value
    tanh = jnp.tanh(half)
    silu = half + half * tanh
    slope = 0.5 * ((1.0 + tanh) + silu * (1.0 - tanh))
    return silu, slope


def project_kv(normed, w_kv, normed_t, kv, kv_t, kv_slope):
    normed_t[...] = normed.T
    for block in range(2 * HEADS):
        silu, slope = silu_and_slope(dot(normed, w_kv[:, pl.ds(block * HEAD_DIM, HEAD_DIM)]))
        silu = silu.astype(bf16)
        kv[block] = silu
        kv_t[block] = silu.T
        kv_slope[block] = slope.astype(bf16)


def own_kernel(
    tokens, in_gain, w_uq_t, w_kv, w_out, cotangent,
    normed_t, kv, kv_t, kv_slope, uq_t, uq_slope_t, grad_gated_t,
):
    normed, _ = layer_norm_rows(tokens[...].astype(f32))
    normed = (normed * in_gain[...]).astype(bf16)
    project_kv(normed, w_kv, normed_t, kv, kv_t, kv_slope)
    for block in range(2 * HEADS):
        columns = pl.ds(block * HEAD_DIM, HEAD_DIM)
        silu, slope = silu_and_slope(dot_nt(w_uq_t[columns, :], normed))
        uq_t[block] = silu.astype(bf16)
        uq_slope_t[block] = slope.astype(bf16)
    grad_gated_t[...] = dot_nt(w_out[...], cotangent[...])


def whole(shape, buffers=1):
    return pl.BlockSpec(shape, lambda *_: (0,) * len(shape), pipeline_mode=pl.Buffered(buffers))


def window_specs(at):
    blocks = 2 * HEADS
    return [
        pl.BlockSpec((WIDTH, ROWS), lambda i: (0, at(i))),
        pl.BlockSpec((blocks, ROWS, HEAD_DIM), lambda i: (0, at(i), 0)),
        pl.BlockSpec((blocks, HEAD_DIM, ROWS), lambda i: (0, 0, at(i))),
        pl.BlockSpec((blocks, ROWS, HEAD_DIM), lambda i: (0, at(i), 0)),
    ]


WINDOW_SHAPES = (
    jax.ShapeDtypeStruct((WIDTH, WINDOW_ROWS), bf16),
    jax.ShapeDtypeStruct((2 * HEADS, WINDOW_ROWS, HEAD_DIM), bf16),
    jax.ShapeDtypeStruct((2 * HEADS, HEAD_DIM, WINDOW_ROWS), bf16),
    jax.ShapeDtypeStruct((2 * HEADS, WINDOW_ROWS, HEAD_DIM), bf16),
)


def own_call(tokens, in_gain, w_uq_t, w_kv, w_out, cotangent):
    blocks = 2 * HEADS
    operands = (tokens, in_gain, w_uq_t, w_kv, w_out, cotangent)
    extra = ((blocks, HEAD_DIM, ROWS), (blocks, HEAD_DIM, ROWS), (WIDTH, ROWS))
    return pl.pallas_call(
        own_kernel,
        grid=(1,),
        in_specs=[whole(operand.shape) for operand in operands],
        out_specs=window_specs(lambda i: 2) + [whole(shape) for shape in extra],
        out_shape=WINDOW_SHAPES
        + (
            jax.ShapeDtypeStruct(extra[0], bf16),
            jax.ShapeDtypeStruct(extra[1], bf16),
            jax.ShapeDtypeStruct(extra[2], f32),
        ),
        compiler_params=pltpu.CompilerParams(vmem_limit_bytes=40 * MIB),
        cost_estimate=pl.CostEstimate(
            flops=2 * ROWS * WIDTH * 5 * WIDTH, bytes_accessed=12 * MIB, transcendentals=ROWS * 4 * WIDTH
        ),
        name="own_projection",
    )(*operands)


def halo_kernel(far, near_a, near_b, in_gain, w_kv, *refs):
    near = near_a[...].astype(f32) + near_b[...].astype(f32)
    halo = jnp.where(pl.program_id(0) == 0, far[...].astype(f32), near)
    normed, _ = layer_norm_rows(halo)
    normed = (normed * in_gain[...]).astype(bf16)
    project_kv(normed, w_kv, *refs[4:])


def halo_call(far, near_a, near_b, in_gain, w_kv, window):
    operands = (far, near_a, near_b, in_gain, w_kv)
    return pl.pallas_call(
        halo_kernel,
        grid=(2,),
        in_specs=[whole(operand.shape) for operand in operands] + [pl.BlockSpec(memory_space=pl.ANY)] * 4,
        out_specs=window_specs(lambda i: i),
        out_shape=WINDOW_SHAPES,
        input_output_aliases={5: 0, 6: 1, 7: 2, 8: 3},
        compiler_params=pltpu.CompilerParams(vmem_limit_bytes=40 * MIB),
        cost_estimate=pl.CostEstimate(
            flops=4 * ROWS * WIDTH * 2 * WIDTH, bytes_accessed=12 * MIB, transcendentals=ROWS * 4 * WIDTH
        ),
        name="halo_projection",
    )(*operands, *window)


def main_kernel(
    core, keys, values, keys_t, values_t, keys_slope, values_slope, query_t, query_slope_t,
    normed_t, u_t, u_slope_t, grad_gated_t, tokens, out_gain, w_out, cotangent, ids_row, ids_col,
    layer_out, grad_u_pre, grad_query_pre, grad_keys_pre, grad_values_pre, mine, theirs,
    mask, weights, slopes, mixed_t, grad_attn_t, grad_kv, grad_kv_pre,
):
    step_at = pl.program_id(0)
    head = lax.rem(step_at, HEADS)
    own = pl.ds(HALO, ROWS)

    def put(block, value):
        value = value.astype(bf16)
        high = jnp.where(block >= HALF_BLOCKS, 1, 0)
        at = block - high * HALF_BLOCKS

        @pl.when(core[0] == high)
        def _():
            mine[at] = value

        @pl.when(core[0] != high)
        def _():
            theirs[at] = value

    @pl.when(step_at == 0)
    def _():
        key_at = lax.broadcasted_iota(jnp.int32, (TILE, TILE), 0)
        query_at = lax.broadcasted_iota(jnp.int32, (TILE, TILE), 1)
        for tile in range(TILES):
            query_ids = ids_row[:, pl.ds(tile * TILE, TILE)]
            for step in range(SPREAD):
                allowed = ids_col[pl.ds((tile + step) * TILE, TILE), :] == query_ids
                if step == 0:
                    allowed = allowed & (key_at > query_at)
                if step == SPREAD - 1:
                    allowed = allowed & (key_at <= query_at)
                mask[tile, pl.ds(step * TILE, TILE), :] = jnp.where(allowed, 1.0, 0.0).astype(bf16)

    @pl.when(step_at < HEADS)
    def _():
        for tile in range(TILES):
            queries = pl.ds(tile * TILE, TILE)
            for step in range(SPREAD):
                at = pl.ds(step * TILE, TILE)
                scores = dot(keys[0, pl.ds((tile + step) * TILE, TILE), :], query_t[0, :, queries])
                half = scores * HALF_SCALE
                tanh = jnp.tanh(half)
                silu = half + half * tanh
                slope = (1.0 + tanh) + silu * (1.0 - tanh)
                keep = mask[tile, at, :]
                weights[head, tile, at, :] = silu.astype(bf16) * keep
                slopes[head, tile, at, :] = slope.astype(bf16) * keep
            mixed_t[head, :, queries] = dot(
                values_t[0, :, pl.ds(tile * TILE, SPREAD * TILE)], weights[head, tile]
            )

    @pl.when(step_at == HEADS)
    def _():
        gain = out_gain[...]
        for tile in range(TILES):
            rows = pl.ds(tile * TILE, TILE)
            mixed = mixed_t[:, :, rows].reshape(WIDTH, TILE)
            center = mixed - jnp.mean(mixed, axis=0, keepdims=True)
            inverse = lax.rsqrt(jnp.mean(center * center, axis=0, keepdims=True) + EPSILON)
            normed_out = center * inverse
            scaled_out = normed_out * gain
            u_part = u_t[:, :, rows].reshape(WIDTH, TILE).astype(f32)
            gated_t = (scaled_out * u_part).astype(bf16)
            upstream = grad_gated_t[:, rows]
            u_slope = u_slope_t[:, :, rows].reshape(WIDTH, TILE).astype(f32)
            grad_u_pre[:, rows] = (upstream * scaled_out * u_slope).astype(bf16)
            scaled_grad = upstream * u_part * gain
            first = jnp.mean(scaled_grad, axis=0, keepdims=True)
            second = jnp.mean(scaled_grad * normed_out, axis=0, keepdims=True)
            grad_attn = ((scaled_grad - first - normed_out * second) * inverse).astype(bf16)
            grad_attn_t[:, :, rows] = grad_attn.reshape(HEADS, HEAD_DIM, TILE)
            layer_out[rows, :] = (tokens[rows, :].astype(f32) + dot(gated_t.T, w_out[...])).astype(bf16)
            mixed_t[:, :, rows] = gated_t.astype(f32).reshape(HEADS, HEAD_DIM, TILE)
        gated_t = mixed_t[...].reshape(WIDTH, ROWS).astype(bf16)
        for block in range(HEADS):
            columns = pl.ds(block * HEAD_DIM, HEAD_DIM)
            put(4 * HEADS + block, dot(gated_t, cotangent[:, columns]))
            put(block, dot_nt(normed_t[:, own], grad_u_pre[columns, :]))

    @pl.when(step_at >= HEADS)
    def _():
        grad_kv[...] = jnp.zeros_like(grad_kv)
        for tile in range(TILES):
            queries = pl.ds(tile * TILE, TILE)
            attn_t = grad_attn_t[head, :, queries]
            for step in range(SPREAD):
                at = pl.ds(step * TILE, TILE)
                rows = pl.ds((tile + step) * TILE, TILE)
                grad_weights = dot(values[0, rows, :], attn_t)
                grad_scores = grad_weights.astype(bf16) * slopes[head, tile, at, :]
                slopes[head, tile, at, :] = grad_scores
                grad_kv[0, rows, :] += dot_nt(grad_scores, query_t[0, :, queries])
                grad_kv[1, rows, :] += dot_nt(weights[head, tile, at, :], attn_t)
            grad_query_t = dot(keys_t[0, :, pl.ds(tile * TILE, SPREAD * TILE)], slopes[head, tile])
            grad_query_pre[:, queries] = (
                grad_query_t * query_slope_t[0, :, queries].astype(f32) * HALF_SCALE
            ).astype(bf16)
        put(HEADS + head, dot_nt(normed_t[:, own], grad_query_pre[...]))
        piece = (grad_kv[0] * keys_slope[0].astype(f32) * HALF_SCALE).astype(bf16)
        grad_keys_pre[...] = piece
        grad_kv_pre[:, :HEAD_DIM] = piece
        piece = (grad_kv[1] * values_slope[0].astype(f32)).astype(bf16)
        grad_values_pre[...] = piece
        grad_kv_pre[:, HEAD_DIM:] = piece
        both = dot(normed_t[...], grad_kv_pre[...])
        put(2 * HEADS + head, both[:, :HEAD_DIM])
        put(3 * HEADS + head, both[:, HEAD_DIM:])


def main_call(core, window, uq_t, uq_slope_t, grad_gated_t, tokens, out_gain, w_out, cotangent, ids_row, ids_col):
    normed_t, kv, kv_t, kv_slope = window

    def forward_head(i):
        return lax.rem(i, HEADS)

    def backward_head(i):
        return jnp.maximum(i - HEADS, 0)

    natural, across, along = (1, WINDOW_ROWS, HEAD_DIM), (1, HEAD_DIM, WINDOW_ROWS), (1, HEAD_DIM, ROWS)
    constants = (tokens, out_gain, w_out, cotangent, ids_row, ids_col)
    in_specs = [
        pl.BlockSpec(memory_space=pltpu.SMEM),
        pl.BlockSpec(natural, lambda i: (forward_head(i), 0, 0)),
        pl.BlockSpec(natural, lambda i: (HEADS + forward_head(i), 0, 0)),
        pl.BlockSpec(across, lambda i: (forward_head(i), 0, 0)),
        pl.BlockSpec(across, lambda i: (HEADS + forward_head(i), 0, 0)),
        pl.BlockSpec(natural, lambda i: (backward_head(i), 0, 0)),
        pl.BlockSpec(natural, lambda i: (HEADS + backward_head(i), 0, 0)),
        pl.BlockSpec(along, lambda i: (HEADS + forward_head(i), 0, 0)),
        pl.BlockSpec(along, lambda i: (HEADS + backward_head(i), 0, 0)),
        whole(normed_t.shape),
        whole((HEADS, HEAD_DIM, ROWS)),
        whole((HEADS, HEAD_DIM, ROWS)),
        whole(grad_gated_t.shape),
    ] + [whole(operand.shape) for operand in constants]
    return pl.pallas_call(
        main_kernel,
        grid=(2 * HEADS,),
        in_specs=in_specs,
        out_specs=[
            whole((ROWS, WIDTH)),
            whole((WIDTH, ROWS)),
            pl.BlockSpec((HEAD_DIM, ROWS), lambda i: (backward_head(i), 0)),
            pl.BlockSpec((WINDOW_ROWS, HEAD_DIM), lambda i: (0, backward_head(i))),
            pl.BlockSpec((WINDOW_ROWS, HEAD_DIM), lambda i: (0, backward_head(i))),
            whole((HALF_BLOCKS, WIDTH, HEAD_DIM)),
            whole((HALF_BLOCKS, WIDTH, HEAD_DIM)),
        ],
        out_shape=(
            jax.ShapeDtypeStruct((ROWS, WIDTH), bf16),
            jax.ShapeDtypeStruct((WIDTH, ROWS), bf16),
            jax.ShapeDtypeStruct((WIDTH, ROWS), bf16),
            jax.ShapeDtypeStruct((WINDOW_ROWS, WIDTH), bf16),
            jax.ShapeDtypeStruct((WINDOW_ROWS, WIDTH), bf16),
            jax.ShapeDtypeStruct((HALF_BLOCKS, WIDTH, HEAD_DIM), bf16),
            jax.ShapeDtypeStruct((HALF_BLOCKS, WIDTH, HEAD_DIM), bf16),
        ),
        scratch_shapes=[
            pltpu.VMEM((TILES, SPREAD * TILE, TILE), bf16),
            pltpu.VMEM((HEADS, TILES, SPREAD * TILE, TILE), bf16),
            pltpu.VMEM((HEADS, TILES, SPREAD * TILE, TILE), bf16),
            pltpu.VMEM((HEADS, HEAD_DIM, ROWS), f32),
            pltpu.VMEM((HEADS, HEAD_DIM, ROWS), bf16),
            pltpu.VMEM((2, WINDOW_ROWS, HEAD_DIM), f32),
            pltpu.VMEM((WINDOW_ROWS, 2 * HEAD_DIM), bf16),
        ],
        compiler_params=pltpu.CompilerParams(vmem_limit_bytes=60 * MIB),
        cost_estimate=pl.CostEstimate(flops=20 * 10**9, bytes_accessed=24 * MIB, transcendentals=6 * 10**6),
        name="attention",
    )(
        core, kv, kv, kv_t, kv_t, kv_slope, kv_slope, uq_t, uq_slope_t,
        normed_t, uq_t, uq_slope_t, grad_gated_t, *constants,
    )


def back_kernel(grad_u_pre, grad_query_pre, grad_keys_pre, grad_values_pre, w_in, halo_grad, grad_normed):
    w_u, w_query, w_keys, w_values = (w_in[:, pl.ds(part * WIDTH, WIDTH)] for part in range(4))
    halo = pl.ds(0, HALO)
    own = pl.ds(HALO, ROWS)
    halo_grad[...] = (
        dot_nt(grad_keys_pre[halo, :], w_keys) + dot_nt(grad_values_pre[halo, :], w_values)
    ).astype(bf16)
    across = dot(w_u, grad_u_pre[...]) + dot(w_query, grad_query_pre[...])
    grad_normed[...] = (
        across.T + dot_nt(grad_keys_pre[own, :], w_keys) + dot_nt(grad_values_pre[own, :], w_values)
    )


def back_call(*operands):
    vmem = pl.BlockSpec(memory_space=pltpu.VMEM)
    return pl.pallas_call(
        back_kernel,
        in_specs=[vmem] * len(operands),
        out_specs=[vmem] * 2,
        out_shape=(
            jax.ShapeDtypeStruct((HALO, WIDTH), bf16),
            jax.ShapeDtypeStruct((ROWS, WIDTH), f32),
        ),
        compiler_params=pltpu.CompilerParams(vmem_limit_bytes=32 * MIB),
        cost_estimate=pl.CostEstimate(flops=32 * 10**8, bytes_accessed=14 * MIB, transcendentals=0),
        name="projection_gradient",
    )(*operands)


def unpack_kernel(core, first, second, grad_w_in, grad_w_out):
    def piece(block):
        half, at = divmod(block, HALF_BLOCKS)
        return jnp.where(core[0] == half, first[at].astype(f32), second[at].astype(f32))

    for block in range(4 * HEADS):
        grad_w_in[:, pl.ds(block * HEAD_DIM, HEAD_DIM)] = piece(block)
    for block in range(HEADS):
        grad_w_out[:, pl.ds(block * HEAD_DIM, HEAD_DIM)] = piece(4 * HEADS + block)


def unpack_call(core, first, second):
    vmem = pl.BlockSpec(memory_space=pltpu.VMEM)
    return pl.pallas_call(
        unpack_kernel,
        in_specs=[pl.BlockSpec(memory_space=pltpu.SMEM), vmem, vmem],
        out_specs=[vmem] * 2,
        out_shape=(
            jax.ShapeDtypeStruct((WIDTH, 4 * WIDTH), f32),
            jax.ShapeDtypeStruct((WIDTH, WIDTH), f32),
        ),
        compiler_params=pltpu.CompilerParams(vmem_limit_bytes=24 * MIB),
        name="unpack",
    )(core, first, second)


def step_kernel(tokens, in_gain, cotangent, grad_normed, sent, swapped, core, grad_tokens):
    normed, inverse = layer_norm_rows(tokens[...].astype(f32))
    near = jnp.where(core[0] == 0, swapped[...].astype(f32), 0.0)
    upstream = grad_normed[...] + sent[...].astype(f32) + near
    scaled_grad = upstream * in_gain[...]
    first = jnp.mean(scaled_grad, axis=1, keepdims=True)
    second = jnp.mean(scaled_grad * normed, axis=1, keepdims=True)
    grad_tokens[...] = (
        cotangent[...].astype(f32) + (scaled_grad - first - normed * second) * inverse
    ).astype(bf16)


def step_call(tokens, in_gain, cotangent, grad_normed, sent, swapped, core):
    vmem = pl.BlockSpec(memory_space=pltpu.VMEM)
    return pl.pallas_call(
        step_kernel,
        in_specs=[vmem] * 6 + [pl.BlockSpec(memory_space=pltpu.SMEM)],
        out_specs=vmem,
        out_shape=jax.ShapeDtypeStruct((ROWS, WIDTH), bf16),
        compiler_params=pltpu.CompilerParams(vmem_limit_bytes=24 * MIB),
        name="input_norm_gradient",
    )(tokens, in_gain, cotangent, grad_normed, sent, swapped, core)


def shifted(value, steps):
    count = 128
    first, last = (max(0, -steps), min(count, count - steps))
    return lax.ppermute(value, ALL, [(source, source + steps) for source in range(first, last)])


SWAP = [(0, 1), (1, 0)]


def on_device(tokens, user_ids, in_gain, out_gain, w_in, w_out, cotangent):
    core = lax.axis_index("core").astype(jnp.int32).reshape(1)
    far = shifted(tokens, 2)
    near_a = lax.ppermute(tokens, "core", [(0, 1)])
    far_ids = shifted(user_ids, 2)
    near_ids = shifted(user_ids, 1)
    near_b = lax.ppermute(far, "core", [(1, 0)])

    in_gain_row = in_gain.reshape(1, WIDTH)
    w_kv = w_in[:, 2 * WIDTH :]
    *window, uq_t, uq_slope_t, grad_gated_t = own_call(
        tokens, in_gain_row, w_in[:, : 2 * WIDTH].T, w_kv, w_out, cotangent
    )
    window = halo_call(far, near_a, near_b, in_gain_row, w_kv, window)
    window_ids = jnp.concatenate([far_ids, near_ids, user_ids])
    layer_out, *grad_pre, mine, theirs = main_call(
        core, window, uq_t, uq_slope_t, grad_gated_t, tokens, out_gain.reshape(WIDTH, 1), w_out, cotangent,
        user_ids.reshape(1, ROWS), window_ids.reshape(WINDOW_ROWS, 1),
    )
    halo_grad, grad_normed = back_call(*grad_pre, w_in)

    arrived = lax.ppermute(theirs, "core", SWAP)
    partial = (mine.astype(f32) + arrived.astype(f32)).astype(bf16).reshape(64, 80, HEAD_DIM)
    parts = lax.all_to_all(partial, CHIPS, 0, 0, tiled=True)
    total = jnp.sum(parts.astype(f32), axis=0, keepdims=True).astype(bf16)
    whole = lax.all_to_all(jnp.broadcast_to(total, (64, 80, HEAD_DIM)), CHIPS, 0, 0, tiled=True)
    whole = whole.reshape(HALF_BLOCKS, WIDTH, HEAD_DIM)
    other = lax.ppermute(whole, "core", SWAP)
    grad_w_in, grad_w_out = unpack_call(core, whole, other)

    swapped = lax.ppermute(halo_grad[ROWS:], "core", SWAP)
    outgoing = (
        halo_grad[:ROWS].astype(f32) + jnp.where(core[0] == 1, swapped.astype(f32), 0.0)
    ).astype(bf16)
    sent = shifted(outgoing, -2)
    grad_tokens = step_call(tokens, in_gain_row, cotangent, grad_normed, sent, swapped, core)
    return (layer_out, grad_tokens, grad_w_in, grad_w_out)


def solution(mesh):
    fine = Mesh(mesh.devices.reshape(2, 4, 2, 4, 2), ALL)
    placed = (P(ALL, None), P(ALL), P(), P(), P(), P(), P(ALL, None))
    return jax.shard_map(
        on_device,
        mesh=fine,
        in_specs=placed,
        out_specs=(P(ALL, None), P(ALL, None), P(), P()),
        check_vma=False,
    )
```

time: 426 us -> 214 us (0.50); the launches traced: 419 us -> 212 us
  waiting for transfers between devices: 212 us -> 44.6 us
  matrix products: 101 us -> 0 us
  Pallas kernels: 0 us -> 72 us
  blocking collectives: 0 us -> 27.8 us
  local copies, waits for them, and re-layouts: 49.7 us -> 30.9 us
  other arithmetic: 21.9 us -> 3.41 us
  between operations: 14.9 us -> 0.78 us
  starting transfers between devices: 19.4 us -> 32.4 us
    psum x1 -> x0, waiting for transfers between devices: 162 us -> none  [on_device(): grad_w_in, grad_w_out = lax.psum((local_w_in, local_w_out), ('wide', 'seq'))]
    dot_general x24 -> x0, matrix products: 101 us -> none  [the longest x3 24 us: score_grads(): jnp.einsum('rhd,chd->hrc', split_heads(grad_attn), split_heads(values), p...]
    pallas_call x0 -> x6, Pallas kernels: none -> 72 us  [the longest x1 47.5 us: main_call(): pl.pallas_call(main_kernel, grid=(2 * HEADS,), in_specs=in_specs, out_spe...]
    all_to_all x0 -> x1, blocking collectives: none -> 27.8 us  [on_device(): parts = lax.all_to_all(partial, CHIPS, 0, 0, tiled=True)]
    reshape x11 -> x3, local copies, waits for them, and re-layouts: 25.1 us -> 3.33 us  [the longest x1 1.89 us: on_device(): window_ids.reshape(WINDOW_ROWS, 1)]
    ppermute x6 -> x9, waiting for transfers between devices: 50.4 us -> 41.4 us  [the longest x4 38.5 us: shifted(): lax.ppermute(value, ALL, [(source, source + steps) for source in range(fi...]
    all_to_all x0 -> x1, starting transfers between devices: none -> 8.17 us  [on_device(): lax.all_to_all(jnp.broadcast_to(total, (64, 80, HEAD_DIM)), CHIPS, 0, 0,...]
    unnamed x111 -> x47, local copies, waits for them, and re-layouts: 17.1 us -> 23.7 us
  transfers between devices with their start and end apart: 7 -> 10, of which waited for: 5 -> 4; matrix products, arithmetic and copies ran while one was open for 13% -> 4% of each run, Pallas kernels for 0% -> 6%
where the time goes in v1:
time: 214 us; the launch traced here: 212 us
  Pallas kernels  72 us (34%)
  waiting for transfers between devices  44.6 us (21%)
  starting transfers between devices  32.4 us (15%)
  local copies, waits for them, and re-layouts  30.9 us (14%)
  blocking collectives  27.8 us (13%)
  other arithmetic  3.41 us (2%)
    pallas_call x1, Pallas kernels, main_call(): pl.pallas_call(main_kernel, grid=(2 * HEADS,), in_specs=in_specs, out_spe...  47.5 us
    ppermute x4, waiting for transfers between devices, shifted(): lax.ppermute(value, ALL, [(source, source + steps) for source in range(fi...  38.5 us
    all_to_all x1, blocking collectives, on_device(): parts = lax.all_to_all(partial, CHIPS, 0, 0, tiled=True)  27.8 us
    unnamed x47, local copies, waits for them, and re-layouts  23.7 us
    ppermute x4, starting transfers between devices, shifted(): lax.ppermute(value, ALL, [(source, source + steps) for source in range(fi...  12.5 us
    pallas_call x1, Pallas kernels, halo_call(): pl.pallas_call(halo_kernel, grid=(2,), in_specs=[whole(operand.shape) for...  8.82 us
    all_to_all x1, starting transfers between devices, on_device(): lax.all_to_all(jnp.broadcast_to(total, (64, 80, HEAD_DIM)), CHIPS, 0, 0,...  8.17 us
    pallas_call x1, Pallas kernels, own_call(): pl.pallas_call(own_kernel, grid=(1,), in_specs=[whole(operand.shape) for...  6.93 us
  transfers between devices with their start and end apart: 10, of which 4 were waited for; matrix products, arithmetic and copies ran while one was open for 4% of the time, Pallas kernels for 6%

profile of v1, /device:TPU:39, one launch (start us, length us, event | category | flops | bytes accessed | tf_op | source)
XLA Modules:
  0.0 211.8 jit_solution(14588825535682513166)
XLA Ops:
  0.6 2.7 %collective-permute-start = (bf16[768,512]{1,0:T(8,128)(2,1)}, bf16[768,512]{1,0:T(8,128)(2,1)}, u32[]{:S(2)}, u32[]{:S(2)}) collective-permute-start(bf16[768,512]{1,0:T(8,128)(2,1)} %tokens.5), channel_id=1, source_target_pairs={{0,2},{1,3},{2,4},{3,5},{4,6},{5,7},{6,8},{7,9},{8,10},{9,11},{10,... | collective-permute-start | bytes 2359304 | tf_op jit(solution)/shard_map/ppermute | solution.py:409
  3.3 1.3 collective-permute-start.1
  4.6 16.6 %collective-permute-done.far = bf16[768,512]{1,0:T(8,128)(2,1)} collective-permute-done((bf16[768,512]{1,0:T(8,128)(2,1)}, bf16[768,512]{1,0:T(8,128)(2,1)}, u32[]{:S(2)}, u32[]{:S(2)}) %collective-permute-start) | collective-permute-done | bytes 786464 | tf_op jit(solution)/shard_map/ppermute | solution.py:409
  21.3 4.4 %collective-permute-start.2 = (bf16[768,512]{1,0:T(8,128)(2,1)}, bf16[768,512]{1,0:T(8,128)(2,1)}, u32[]{:S(2)}, u32[]{:S(2)}) collective-permute-start(bf16[768,512]{1,0:T(8,128)(2,1)} %collective-permute-done.far), channel_id=1, source_target_pairs={{1,0},{3,2},{5,4},{7,6},{9,8},{11,10},{13,12},{15,14},{17,16},{19,... | collective-permute-start | bytes 2359304 | tf_op jit(solution)/shard_map/ppermute | solution.py:421
  25.6 5.7 %collective-permute-start.3 = (s32[768]{0:T(1024)}, s32[768]{0:T(1024)S(1)}, u32[]{:S(2)}, u32[]{:S(2)}) collective-permute-start(s32[768]{0:T(1024)} %param.8), channel_id=1, source_target_pairs={{0,2},{1,3},{2,4},{3,5},{4,6},{5,7},{6,8},{7,9},{8,10},{9,11},{10,... | collective-permute-start | bytes 9224 | tf_op jit(solution)/shard_map/ppermute | solution.py:409
  31.3 1.9 collective-permute-start.4
  33.2 1.7 fusion
  35.0 1.3 copy.19
  36.3 1.2 copy-done.7
  37.5 1.1 copy-done.8
  38.7 1.1 copy-done.10
  39.8 1.0 copy-done.13
  40.8 6.9 %own_projection.1 = (bf16[512,2304]{1,0:T(8,128)(2,1)S(1)}, bf16[8,2304,128]{2,1,0:T(8,128)(2,1)}, bf16[8,128,2304]{2,1,0:T(8,128)(2,1)}, bf16[8,2304,128]{2,1,0...) custom-call(bf16[768,512]{1,0:T(8,128)(2,1)S(1)} %copy-done.8, ...), custom_call_target="tpu_custom_call" | custom-call | flops 2013265920 | bytes 12582912 | tf_op jit(solution)/shard_map/own_projection/pallas_call | solution.py:104
  47.8 1.1 copy-done.16
  48.9 1.2 copy-done.17
  50.1 1.2 copy-done.18
  51.3 0.6 reshape.36.ids_row
  51.9 0.9 copy.17.out_gain
  52.7 1.9 reshape.40.ids_col
  54.6 2.3 %copy-done = bf16[8,2304,128]{2,1,0:T(8,128)(2,1)S(1)} copy-done((bf16[8,2304,128]{2,1,0:T(8,128)(2,1)S(1)}, bf16[8,2304,128]{2,1,0:T(8,128)(2,1)}, u32[]{:S(2)}) %copy-start) | copy-done | bytes 4718616
  57.0 8.8 %halo_projection.1 = (bf16[512,2304]{1,0:T(8,128)(2,1)S(1)}, bf16[8,2304,128]{2,1,0:T(8,128)(2,1)S(1)}, bf16[8,128,2304]{2,1,0:T(8,128)(2,1)}, bf16[8,2304,128]{2,1,0:T(8,128)(2,1)}) custom-call(bf16[768,512]{1,0:T(8,128)(2,1)} %collective-permute-done.far, ...), custom_call_target="tpu_custom_call", output_to_operand_aliasing={{0}: (5, {}), {1}: (6, {}), {2}: (7, {}), {3}: (8, {})} | custom-call | flops 1610612736 | bytes 12582912 | tf_op jit(solution)/shard_map/halo_projection/pallas_call | solution.py:133
  65.8 2.2 %copy-done.1 = bf16[8,2304,128]{2,1,0:T(8,128)(2,1)} copy-done((bf16[8,2304,128]{2,1,0:T(8,128)(2,1)}, bf16[8,2304,128]{2,1,0:T(8,128)(2,1)S(1)}, u32[]{:S(2)}) %copy-start.1) | copy-done | bytes 4718616
  68.0 1.4 copy-done.2
  69.4 47.5 %attention.1 = (bf16[768,512]{1,0:T(8,128)(2,1)}, bf16[512,768]{1,0:T(8,128)(2,1)}, bf16[512,768]{1,0:T(8,128)(2,1)}, bf16[2304,512]{1,0:T(8,128)(2,1)}, bf16[23...) custom-call(s32[1]{0:T(128)} %bitcast.core, bf16[8,2304,128]{2,1,0:T(8,128)(2,1)} %copy-done.1, ...), custom_call_target="tpu_custom_call" | custom-call | flops 20000000000 | bytes 25165824 | tf_op jit(solution)/shard_map/attention/pallas_call | solution.py:287
  116.9 0.8 collective-permute-start.7
  117.7 2.9 %collective-permute-done.7 = bf16[10,512,128]{2,1,0:T(8,128)(2,1)S(1)} collective-permute-done((bf16[10,512,128]{2,1,0:T(8,128)(2,1)}, bf16[10,512,128]{2,1,0:T(8,128)(2,1)S(1)}, u32[]{:S(2)}, u32[]{:S(2)}) %collective-permute-start.7) | collective-permute-done | bytes 1310752 | tf_op jit(solution)/shard_map/ppermute | solution.py:436
  120.6 1.7 add_convert_fusion
  122.3 27.8 %all_to_all.10 = bf16[64,80,128]{2,1,0:T(8,128)(2,1)S(1)} all-to-all(bf16[64,80,128]{2,1,0:T(8,128)(2,1)S(1)} %bitcast.12), channel_id=1, replica_groups=mesh['z_hi'=2,'y'=4,'z_lo'=2,'x'=4,'core'=2] {'z_hi','y','z_lo','x'}, dimensions={0} | all-to-all | bytes 2621440 | tf_op jit(solution)/shard_map/all_to_all | solution.py:438
  150.0 0.2 reduce_sum.12
  150.3 1.2 broadcast_in_dim.11
  151.5 8.2 %all-to-all-start.1 = ((bf16[64,80,128]{2,1,0:T(8,128)(2,1)}), bf16[64,80,128]{2,1,0:T(8,128)(2,1)S(1)}, u32[]{:S(2)}, u32[]{:S(2)}) async-start(bf16[64,80,128]{2,1,0:T(8,128)(2,1)} %broadcast_in_dim.11), calls=%async_computation.1 | async-start | bytes 2621440 | tf_op jit(solution)/shard_map/all_to_all | solution.py:440
  159.7 1.7 copy-done.14
  161.3 1.7 copy-done.15
  163.0 1.1 copy-done.19
  164.1 1.1 copy-done.20
  165.3 3.6 %projection_gradient.1 = (bf16[1536,512]{1,0:T(8,128)(2,1)S(1)}, f32[768,512]{1,0:T(8,128)S(1)}) custom-call(bf16[512,768]{1,0:T(8,128)(2,1)S(1)} %copy-done.19, bf16[512,768]{1,0:T(8,128)(2,1)S(1)} %copy-done.20, bf16[2304,512]{1,0:T(8,128)(2,1)S(1)} %copy-done.14, bf16[2304,512]{1,0:T(8,128)(2,1)S(1)} %copy-done.15, bf16[512,2048]{1,0:T(8,128)(2,1)S(1)} %copy-done.3), custom_call_target="tpu_custom_call" | custom-call | flops 3200000000 | bytes 14680064 | tf_op jit(solution)/shard_map/projection_gradient/pallas_call | solution.py:342
  168.9 1.1 copy-done.5
  170.0 1.0 slice.15
  171.0 0.4 copy-done.4
  171.4 1.8 collective-permute-start.5
  173.2 3.3 %all-to-all-done.1 = bf16[64,80,128]{2,1,0:T(8,128)(2,1)S(1)} async-done(((bf16[64,80,128]{2,1,0:T(8,128)(2,1)}), bf16[64,80,128]{2,1,0:T(8,128)(2,1)S(1)}, u32[]{:S(2)}, u32[]{:S(2)}) %all-to-all-start.1) | async-done | bytes 1310752 | tf_op jit(solution)/shard_map/all_to_all | solution.py:440
  176.5 3.4 %collective-permute-start.8 = (bf16[10,512,128]{2,1,0:T(8,128)(2,1)S(1)}, bf16[10,512,128]{2,1,0:T(8,128)(2,1)S(1)}, u32[]{:S(2)}, u32[]{:S(2)}) collective-permute-start(bf16[10,512,128]{2,1,0:T(8,128)(2,1)S(1)} %bitcast.6), channel_id=1, source_target_pairs={{0,1},{1,0},{2,3},{3,2},{4,5},{5,4},{6,7},{7,6},{8,9},{9,8},{10,11... | collective-permute-start | bytes 3932168 | tf_op jit(solution)/shard_map/ppermute | solution.py:442
  179.9 1.5 add_convert_fusion.1
  181.4 2.2 %collective-permute-start.6 = (bf16[768,512]{1,0:T(8,128)(2,1)S(1)}, bf16[768,512]{1,0:T(8,128)(2,1)S(1)}, u32[]{:S(2)}, u32[]{:S(2)}) collective-permute-start(bf16[768,512]{1,0:T(8,128)(2,1)S(1)} %add_convert_fusion.1), channel_id=1, source_target_pairs={{2,0},{3,1},{4,2},{5,3},{6,4},{7,5},{8,6},{9,7},{10,8},{11,9},{12,... | collective-permute-start | bytes 2359304 | tf_op jit(solution)/shard_map/ppermute | solution.py:409
  183.7 21.8 %collective-permute-done.6.sent = bf16[768,512]{1,0:T(8,128)(2,1)S(1)} collective-permute-done((bf16[768,512]{1,0:T(8,128)(2,1)S(1)}, bf16[768,512]{1,0:T(8,128)(2,1)S(1)}, u32[]{:S(2)}, u32[]{:S(2)}) %collective-permute-start.6) | collective-permute-done | bytes 786464 | tf_op jit(solution)/shard_map/ppermute | solution.py:409
  205.5 1.1 copy-done.11
  206.6 2.2 %input_norm_gradient.1 = bf16[768,512]{1,0:T(8,128)(2,1)} custom-call(bf16[768,512]{1,0:T(8,128)(2,1)S(1)} %copy-done.9, f32[1,512]{1,0:T(1,128)S(1)} %bitcast.11, bf16[768,512]{1,0:T(8,128)(2,1)S(1)} %copy-done.11, f32[768,512]{1,0:T(8,128)S(1)} %copy-done.6, bf16[768,512]{1,0:T(8,128)(2,1)S(1)} %collective-permute-done.6.sent, ...), custom_call_target="tpu_custom_call" | custom-call | tf_op jit(solution)/shard_map/input_norm_gradient/pallas_call | solution.py:396
  208.8 3.0 %unpack.1 = (f32[512,2048]{1,0:T(8,128)}, f32[512,512]{1,0:T(8,128)}) custom-call(s32[1]{0:T(128)} %bitcast.core, bf16[10,512,128]{2,1,0:T(8,128)(2,1)S(1)} %bitcast.7, bf16[10,512,128]{2,1,0:T(8,128)(2,1)S(1)} %collective-permute-done.8.second), custom_call_target="tpu_custom_call" | custom-call | tf_op jit(solution)/shard_map/unpack/pallas_call | solution.py:369
  (36 shorter events, 0.1 us)
Async XLA Ops:
  0.6 20.6 %collective-permute-start = (bf16[768,512]{1,0:T(8,128)(2,1)}, bf16[768,512]{1,0:T(8,128)(2,1)}, u32[]{:S(2)}, u32[]{:S(2)}) collective-permute-start(bf16[768,512]{1,0:T(8,128)(2,1)} %tokens.5), channel_id=1, source_target_pairs={{0,2},{1,3},{2,4},{3,5},{4,6},{5,7},{6,8},{7,9},{8,10},{9,11},{10,... | collective-permute-start | bytes 2359304 | tf_op jit(solution)/shard_map/ppermute | solution.py:409
  3.3 51.3 %collective-permute-start.1 = (bf16[768,512]{1,0:T(8,128)(2,1)}, bf16[768,512]{1,0:T(8,128)(2,1)}, u32[]{:S(2)}, u32[]{:S(2)}) collective-permute-start(bf16[768,512]{1,0:T(8,128)(2,1)} %tokens.5), channel_id=1, source_target_pairs={{0,1},{2,3},{4,5},{6,7},{8,9},{10,11},{12,13},{14,15},{16,17},{18,... | collective-permute-start | bytes 2359304 | tf_op jit(solution)/shard_map/ppermute | solution.py:418
  21.3 33.4 %collective-permute-start.2 = (bf16[768,512]{1,0:T(8,128)(2,1)}, bf16[768,512]{1,0:T(8,128)(2,1)}, u32[]{:S(2)}, u32[]{:S(2)}) collective-permute-start(bf16[768,512]{1,0:T(8,128)(2,1)} %collective-permute-done.far), channel_id=1, source_target_pairs={{1,0},{3,2},{5,4},{7,6},{9,8},{11,10},{13,12},{15,14},{17,16},{19,... | collective-permute-start | bytes 2359304 | tf_op jit(solution)/shard_map/ppermute | solution.py:421
  25.6 27.1 %collective-permute-start.3 = (s32[768]{0:T(1024)}, s32[768]{0:T(1024)S(1)}, u32[]{:S(2)}, u32[]{:S(2)}) collective-permute-start(s32[768]{0:T(1024)} %param.8), channel_id=1, source_target_pairs={{0,2},{1,3},{2,4},{3,5},{4,6},{5,7},{6,8},{7,9},{8,10},{9,11},{10,... | collective-permute-start | bytes 9224 | tf_op jit(solution)/shard_map/ppermute | solution.py:409
  31.3 21.4 %collective-permute-start.4 = (s32[768]{0:T(1024)}, s32[768]{0:T(1024)S(1)}, u32[]{:S(2)}, u32[]{:S(2)}) collective-permute-start(s32[768]{0:T(1024)} %param.8), channel_id=1, source_target_pairs={{0,1},{1,2},{2,3},{3,4},{4,5},{5,6},{6,7},{7,8},{8,9},{9,10},{10,1... | collective-permute-start | bytes 9224 | tf_op jit(solution)/shard_map/ppermute | solution.py:409
  35.0 1.3 copy-start.12
  36.3 1.2 copy-start.7
  37.5 1.1 copy-start.8
  38.7 1.1 copy-start.10
  39.8 1.0 copy-start.13
  40.8 10.4 %copy-start.21 = (s32[768]{0:T(1024)S(1)}, s32[768]{0:T(1024)}, u32[]{:S(2)}) copy-start(s32[768]{0:T(1024)} %param.8) | copy-start | bytes 9220
  40.8 11.0 %copy-start.22 = (f32[512]{0:T(512)S(1)}, f32[512]{0:T(512)}, u32[]{:S(2)}) copy-start(f32[512]{0:T(512)} %param.10) | copy-start | bytes 6148
  47.8 1.1 copy-start.16
  48.9 1.2 copy-start.17
  50.1 1.2 copy-start.18
  54.6 2.3 %copy-start = (bf16[8,2304,128]{2,1,0:T(8,128)(2,1)S(1)}, bf16[8,2304,128]{2,1,0:T(8,128)(2,1)}, u32[]{:S(2)}) copy-start(bf16[8,2304,128]{2,1,0:T(8,128)(2,1)} %get-tuple-element.27.refs_1_) | copy-start | bytes 14155780
  65.8 2.2 %copy-start.1 = (bf16[8,2304,128]{2,1,0:T(8,128)(2,1)}, bf16[8,2304,128]{2,1,0:T(8,128)(2,1)S(1)}, u32[]{:S(2)}) copy-start(bf16[8,2304,128]{2,1,0:T(8,128)(2,1)S(1)} %get-tuple-element.30.keys.values) | copy-start | bytes 14155780
  68.0 1.4 copy-start.2
  116.9 3.7 %collective-permute-start.7 = (bf16[10,512,128]{2,1,0:T(8,128)(2,1)}, bf16[10,512,128]{2,1,0:T(8,128)(2,1)S(1)}, u32[]{:S(2)}, u32[]{:S(2)}) collective-permute-start(bf16[10,512,128]{2,1,0:T(8,128)(2,1)} %get-tuple-element.45), channel_id=1, source_target_pairs={{0,1},{1,0},{2,3},{3,2},{4,5},{5,4},{6,7},{7,6},{8,9},{9,8},{10,11... | collective-permute-start | bytes 3932168 | tf_op jit(solution)/shard_map/ppermute | solution.py:436
  151.5 8.2 %copy-start.3 = (bf16[512,2048]{1,0:T(8,128)(2,1)S(1)}, bf16[512,2048]{1,0:T(8,128)(2,1)}, u32[]{:S(2)}) copy-start(bf16[512,2048]{1,0:T(8,128)(2,1)} %w_in.1) | copy-start | bytes 6291460
  151.5 25.0 %all-to-all-start.1 = ((bf16[64,80,128]{2,1,0:T(8,128)(2,1)}), bf16[64,80,128]{2,1,0:T(8,128)(2,1)S(1)}, u32[]{:S(2)}, u32[]{:S(2)}) async-start(bf16[64,80,128]{2,1,0:T(8,128)(2,1)} %broadcast_in_dim.11), calls=%async_computation.1 | async-start | bytes 2621440 | tf_op jit(solution)/shard_map/all_to_all | solution.py:440
  159.7 1.7 copy-start.14
  161.3 1.7 copy-start.15
  163.0 1.1 copy-start.19
  164.1 1.1 copy-start.20
  168.8 1.1 copy-start.5
  170.0 1.4 copy-start.4
  171.4 8.5 %collective-permute-start.5 = (bf16[768,512]{1,0:T(8,128)(2,1)}, bf16[768,512]{1,0:T(8,128)(2,1)S(1)}, u32[]{:S(2)}, u32[]{:S(2)}) collective-permute-start(bf16[768,512]{1,0:T(8,128)(2,1)} %slice.15), channel_id=1, source_target_pairs={{0,1},{1,0},{2,3},{3,2},{4,5},{5,4},{6,7},{7,6},{8,9},{9,8},{10,11... | collective-permute-start | bytes 2359304 | tf_op jit(solution)/shard_map/ppermute | solution.py:445
  176.5 32.3 %collective-permute-start.8 = (bf16[10,512,128]{2,1,0:T(8,128)(2,1)S(1)}, bf16[10,512,128]{2,1,0:T(8,128)(2,1)S(1)}, u32[]{:S(2)}, u32[]{:S(2)}) collective-permute-start(bf16[10,512,128]{2,1,0:T(8,128)(2,1)S(1)} %bitcast.6), channel_id=1, source_target_pairs={{0,1},{1,0},{2,3},{3,2},{4,5},{5,4},{6,7},{7,6},{8,9},{9,8},{10,11... | collective-permute-start | bytes 3932168 | tf_op jit(solution)/shard_map/ppermute | solution.py:442
  179.9 25.6 %copy-start.6 = (f32[768,512]{1,0:T(8,128)S(1)}, f32[768,512]{1,0:T(8,128)}, u32[]{:S(2)}) copy-start(f32[768,512]{1,0:T(8,128)} %copy-done.5) | copy-start | bytes 4718596
  179.9 25.6 %copy-start.9 = (bf16[768,512]{1,0:T(8,128)(2,1)S(1)}, bf16[768,512]{1,0:T(8,128)(2,1)}, u32[]{:S(2)}) copy-start(bf16[768,512]{1,0:T(8,128)(2,1)} %tokens.5) | copy-start | bytes 2359300
  181.4 24.1 %collective-permute-start.6 = (bf16[768,512]{1,0:T(8,128)(2,1)S(1)}, bf16[768,512]{1,0:T(8,128)(2,1)S(1)}, u32[]{:S(2)}, u32[]{:S(2)}) collective-permute-start(bf16[768,512]{1,0:T(8,128)(2,1)S(1)} %add_convert_fusion.1), channel_id=1, source_target_pairs={{2,0},{3,1},{4,2},{5,3},{6,4},{7,5},{8,6},{9,7},{10,8},{11,9},{12,... | collective-permute-start | bytes 2359304 | tf_op jit(solution)/shard_map/ppermute | solution.py:409
  205.5 1.1 copy-start.11

commit v2 on v1

v2 whole, which is shorter than its diff:
```python
import jax
import jax.numpy as jnp
from jax import lax
from jax.experimental import pallas as pl
from jax.experimental.pallas import tpu as pltpu
from jax.sharding import Mesh
from jax.sharding import PartitionSpec as P

HEADS = 4
HEAD_DIM = 128
ROWS = 768
WIDTH = 512
WINDOW_ROWS = 3 * ROWS
HALO = 2 * ROWS
TILE = 256
TILES = ROWS // TILE
SPREAD = 7
PAIR = 2 * HEAD_DIM
KEY_TILES = WINDOW_ROWS // TILE
HALF_SCALE = 0.5 * HEAD_DIM ** (-0.5)
EPSILON = 1e-05
BLOCKS = 5 * HEADS
HALF_BLOCKS = BLOCKS // 2

ALL = ("z_hi", "y", "z_lo", "x", "core")
CHIPS = ("z_hi", "y", "z_lo", "x")
MIB = 1024 * 1024

f32 = jnp.float32
bf16 = jnp.bfloat16


def dot(left, right):
    return lax.dot_general(left, right, (((1,), (0,)), ((), ())), preferred_element_type=f32)


def dot_nt(left, right):
    return lax.dot_general(left, right, (((1,), (1,)), ((), ())), preferred_element_type=f32)


def layer_norm_rows(values):
    center = values - jnp.mean(values, axis=1, keepdims=True)
    inverse = lax.rsqrt(jnp.mean(center * center, axis=1, keepdims=True) + EPSILON)
    return center * inverse, inverse


def silu_and_slope(value):
    half = 0.5 * value
    tanh = jnp.tanh(half)
    silu = half + half * tanh
    slope = 0.5 * ((1.0 + tanh) + silu * (1.0 - tanh))
    return silu, slope


def first_query_tile(key_tile):
    return max(0, key_tile - SPREAD + 1)


def query_tiles(key_tile):
    return range(first_query_tile(key_tile), min(TILES, key_tile + 1))


PLACE = {}
for _key_tile in range(KEY_TILES):
    for _tile in query_tiles(_key_tile):
        PLACE[_key_tile, _tile] = len(PLACE) * TILE
BAND = len(PLACE) * TILE


def project_kv(normed, w_kv, rows, normed_t, kv, kv_t, kv_slope):
    normed_t[:, rows] = normed.T
    for head in range(HEADS):
        silu, slope = silu_and_slope(dot(normed, w_kv[:, pl.ds(head * PAIR, PAIR)]))
        silu = silu.astype(bf16)
        kv_slope[head, rows, :] = slope.astype(bf16)
        for part in range(2):
            one = silu[:, part * HEAD_DIM : (part + 1) * HEAD_DIM]
            kv[part * HEADS + head, rows, :] = one
            kv_t[part * HEADS + head, :, rows] = one.T


def own_kernel(tokens, in_gain, w_uq_t, w_kv, normed_t, kv, kv_t, kv_slope, uq_t, uq_slope_t):
    for tile in range(TILES):
        rows = pl.ds(tile * TILE, TILE)
        normed, _ = layer_norm_rows(tokens[rows, :].astype(f32))
        normed = (normed * in_gain[...]).astype(bf16)
        project_kv(normed, w_kv, rows, normed_t, kv, kv_t, kv_slope)
        for block in range(2 * HEADS):
            silu, slope = silu_and_slope(dot_nt(w_uq_t[pl.ds(block * HEAD_DIM, HEAD_DIM), :], normed))
            uq_t[block, :, rows] = silu.astype(bf16)
            uq_slope_t[block, :, rows] = slope.astype(bf16)


VMEM = pl.BlockSpec(memory_space=pltpu.VMEM)
SMEM = pl.BlockSpec(memory_space=pltpu.SMEM)
ANY = pl.BlockSpec(memory_space=pl.ANY)
HBM = pl.BlockSpec(memory_space=pltpu.HBM)


def window_shapes(rows):
    return (
        (WIDTH, rows),
        (2 * HEADS, rows, HEAD_DIM),
        (2 * HEADS, HEAD_DIM, rows),
        (HEADS, rows, PAIR),
    )


def own_call(*operands):
    along = (2 * HEADS, HEAD_DIM, ROWS)
    return pl.pallas_call(
        own_kernel,
        in_specs=[VMEM] * len(operands),
        out_specs=[VMEM] * 6,
        out_shape=[jax.ShapeDtypeStruct(shape, bf16) for shape in window_shapes(ROWS) + (along, along)],
        compiler_params=pltpu.CompilerParams(vmem_limit_bytes=40 * MIB),
        cost_estimate=pl.CostEstimate(
            flops=2 * ROWS * WIDTH * 4 * WIDTH, bytes_accessed=12 * MIB, transcendentals=ROWS * 4 * WIDTH
        ),
        name="own_projection",
    )(*operands)


def relay_kernel(far, after, passed):
    del far, after, passed


def relay_call(far, after):
    return pl.pallas_call(
        relay_kernel,
        in_specs=[ANY, ANY],
        out_specs=ANY,
        out_shape=jax.ShapeDtypeStruct(far.shape, far.dtype),
        input_output_aliases={0: 0},
        name="relay",
    )(far, after)


def main_kernel(
    core, far, near_a, near_b, own_normed_t, own_kv, own_kv_t, own_kv_slope, own_uq_slope_t,
    uq_t, tokens, in_gain, out_gain, w_kv, w_out, cotangent, ids_row, ids_col,
    layer_out, grad_kv_pre, grad_uq_pre, mine, theirs,
    normed_t, kv, kv_t, kv_slope, uq_slope_t, mask, weights, slopes, mixed_t, grad_attn_t, gated_t, both, sems,
):
    own = pl.ds(HALO, ROWS)

    def staged(slot, tile):
        return weights.at[slot, :, pl.ds(tile * WIDTH, WIDTH)]

    arrivals = []
    for slot, source in enumerate((far, near_a, near_b)):
        for tile in range(TILES):
            arrivals.append(
                pltpu.make_async_copy(source.at[pl.ds(tile * TILE, TILE)], staged(slot, tile), sems.at[len(arrivals)])
            )
    fetches = [
        pltpu.make_async_copy(source, target, sems.at[len(arrivals) + at])
        for at, (source, target) in enumerate(
            (
                (own_normed_t, normed_t.at[:, own]),
                (own_kv, kv.at[:, own, :]),
                (own_kv_t, kv_t.at[:, :, own]),
                (own_kv_slope, kv_slope.at[:, own, :]),
                (own_uq_slope_t, uq_slope_t),
            )
        )
    ]
    for copy in arrivals + fetches:
        copy.start()

    key_at = lax.broadcasted_iota(jnp.int32, (TILE, TILE), 0)
    query_at = lax.broadcasted_iota(jnp.int32, (TILE, TILE), 1)
    for (key_tile, tile), place in PLACE.items():
        allowed = ids_col[pl.ds(key_tile * TILE, TILE), :] == ids_row[:, pl.ds(tile * TILE, TILE)]
        if key_tile == tile:
            allowed = allowed & (key_at > query_at)
        if key_tile == tile + SPREAD - 1:
            allowed = allowed & (key_at <= query_at)
        mask[:, pl.ds(place, TILE)] = jnp.where(allowed, 1.0, 0.0).astype(bf16)

    for copy in arrivals:
        copy.wait()
    for tile in range(2 * TILES):
        at = tile % TILES
        if tile < TILES:
            halo = staged(0, at)[...].astype(f32)
        else:
            halo = staged(1, at)[...].astype(f32) + staged(2, at)[...].astype(f32)
        normed, _ = layer_norm_rows(halo)
        normed = (normed * in_gain[...]).astype(bf16)
        project_kv(normed, w_kv, pl.ds(tile * TILE, TILE), normed_t, kv, kv_t, kv_slope)
    for copy in fetches:
        copy.wait()

    def forward(head, carry):
        for (key_tile, tile), place in PLACE.items():
            band = pl.ds(place, TILE)
            scores = dot(
                kv[head, pl.ds(key_tile * TILE, TILE), :], uq_t[HEADS + head, :, pl.ds(tile * TILE, TILE)]
            )
            half = scores * HALF_SCALE
            tanh = jnp.tanh(half)
            silu = half + half * tanh
            slope = (1.0 + tanh) + silu * (1.0 - tanh)
            keep = mask[:, band]
            weights[head, :, band] = silu.astype(bf16) * keep
            slopes[head, :, band] = slope.astype(bf16) * keep
        for tile in range(TILES):
            total = None
            for key_tile in range(tile, tile + SPREAD):
                term = dot(
                    kv_t[HEADS + head, :, pl.ds(key_tile * TILE, TILE)],
                    weights[head, :, pl.ds(PLACE[key_tile, tile], TILE)],
                )
                total = term if total is None else total + term
            mixed_t[head, :, pl.ds(tile * TILE, TILE)] = total
        return carry

    lax.fori_loop(0, HEADS, forward, 0)

    def put(block, value):
        value = value.astype(bf16)
        for part in range(2):
            at = block[part]
            high = jnp.where(at >= HALF_BLOCKS, 1, 0)
            slot = jnp.where(high == core[0], 0, 1)
            both[slot, at - high * HALF_BLOCKS] = value[:, part * HEAD_DIM : (part + 1) * HEAD_DIM]

    gain = out_gain[...]
    for tile in range(TILES):
        rows = pl.ds(tile * TILE, TILE)
        mixed = mixed_t[:, :, rows].reshape(WIDTH, TILE)
        center = mixed - jnp.mean(mixed, axis=0, keepdims=True)
        inverse = lax.rsqrt(jnp.mean(center * center, axis=0, keepdims=True) + EPSILON)
        normed_out = center * inverse
        scaled_out = normed_out * gain
        u_part = uq_t[pl.ds(0, HEADS), :, rows].reshape(WIDTH, TILE).astype(f32)
        gated = (scaled_out * u_part).astype(bf16)
        gated_t[:, rows] = gated
        upstream = dot_nt(w_out[...], cotangent[rows, :])
        u_slope = uq_slope_t[pl.ds(0, HEADS), :, rows].reshape(WIDTH, TILE).astype(f32)
        grad_u = (upstream * scaled_out * u_slope).astype(bf16)
        uq_slope_t[pl.ds(0, HEADS), :, rows] = grad_u.reshape(HEADS, HEAD_DIM, TILE)
        scaled_grad = upstream * u_part * gain
        first = jnp.mean(scaled_grad, axis=0, keepdims=True)
        second = jnp.mean(scaled_grad * normed_out, axis=0, keepdims=True)
        grad_attn = ((scaled_grad - first - normed_out * second) * inverse).astype(bf16)
        grad_attn_t[:, :, rows] = grad_attn.reshape(HEADS, HEAD_DIM, TILE)
        layer_out[rows, :] = (tokens[rows, :].astype(f32) + dot(gated.T, w_out[...])).astype(bf16)
    for pair in range(HEADS // 2):
        blocks = (2 * pair, 2 * pair + 1)
        columns = pl.ds(pair * PAIR, PAIR)
        put([4 * HEADS + block for block in blocks], dot(gated_t[...], cotangent[:, columns]))
        put(blocks, dot_nt(normed_t[:, own], uq_slope_t[pl.ds(2 * pair, 2)].reshape(PAIR, ROWS)))

    def backward(head, carry):
        for (key_tile, tile), place in PLACE.items():
            band = pl.ds(place, TILE)
            grad_weights = dot(
                kv[HEADS + head, pl.ds(key_tile * TILE, TILE), :], grad_attn_t[head, :, pl.ds(tile * TILE, TILE)]
            )
            slopes[head, :, band] = grad_weights.astype(bf16) * slopes[head, :, band]
        for key_tile in range(KEY_TILES):
            rows = pl.ds(key_tile * TILE, TILE)
            span = query_tiles(key_tile)
            band = pl.ds(PLACE[key_tile, span[0]], len(span) * TILE)
            queries = pl.ds(span[0] * TILE, len(span) * TILE)
            grad_keys = dot_nt(slopes[head, :, band], uq_t[HEADS + head, :, queries])
            grad_values = dot_nt(weights[head, :, band], grad_attn_t[head, :, queries])
            slope = kv_slope[head, rows, :].astype(f32)
            kv_slope[head, rows, :] = jnp.concatenate(
                [
                    (grad_keys * slope[:, :HEAD_DIM] * HALF_SCALE).astype(bf16),
                    (grad_values * slope[:, HEAD_DIM:]).astype(bf16),
                ],
                axis=1,
            )
        for tile in range(TILES):
            total = None
            for key_tile in range(tile, tile + SPREAD):
                term = dot(
                    kv_t[head, :, pl.ds(key_tile * TILE, TILE)],
                    slopes[head, :, pl.ds(PLACE[key_tile, tile], TILE)],
                )
                total = term if total is None else total + term
            queries = pl.ds(tile * TILE, TILE)
            slope = uq_slope_t[HEADS + head, :, queries].astype(f32)
            uq_slope_t[HEADS + head, :, queries] = (total * slope * HALF_SCALE).astype(bf16)
        put((2 * HEADS + head, 3 * HEADS + head), dot(normed_t[...], kv_slope[head]))
        return carry

    lax.fori_loop(0, HEADS, backward, 0)
    for pair in range(HEADS // 2):
        queries = uq_slope_t[pl.ds(HEADS + 2 * pair, 2)].reshape(PAIR, ROWS)
        put((HEADS + 2 * pair, HEADS + 2 * pair + 1), dot_nt(normed_t[:, own], queries))
    results = [
        pltpu.make_async_copy(source, target, sems.at[at])
        for at, (source, target) in enumerate(
            ((both.at[1], theirs), (both.at[0], mine), (kv_slope, grad_kv_pre), (uq_slope_t, grad_uq_pre))
        )
    ]
    for copy in results:
        copy.start()
    for copy in results:
        copy.wait()


def main_call(*operands):
    along = (2 * HEADS, HEAD_DIM, ROWS)
    half = (HALF_BLOCKS, WIDTH, HEAD_DIM)
    scratch = [pltpu.VMEM(shape, bf16) for shape in window_shapes(WINDOW_ROWS)] + [
        pltpu.VMEM(along, bf16),
        pltpu.VMEM((TILE, BAND), bf16),
        pltpu.VMEM((HEADS, TILE, BAND), bf16),
        pltpu.VMEM((HEADS, TILE, BAND), bf16),
        pltpu.VMEM((HEADS, HEAD_DIM, ROWS), f32),
        pltpu.VMEM((HEADS, HEAD_DIM, ROWS), bf16),
        pltpu.VMEM((WIDTH, ROWS), bf16),
        pltpu.VMEM((2,) + half, bf16),
        pltpu.SemaphoreType.DMA((16,)),
    ]
    return pl.pallas_call(
        main_kernel,
        in_specs=[SMEM] + [ANY] * 8 + [VMEM] * (len(operands) - 9),
        out_specs=[VMEM] + [ANY] * 2 + [HBM] * 2,
        out_shape=[
            jax.ShapeDtypeStruct(shape, bf16)
            for shape in ((ROWS, WIDTH), (HEADS, WINDOW_ROWS, PAIR), along, half, half)
        ],
        scratch_shapes=scratch,
        compiler_params=pltpu.CompilerParams(vmem_limit_bytes=62 * MIB),
        cost_estimate=pl.CostEstimate(flops=20 * 10**9, bytes_accessed=24 * MIB, transcendentals=6 * 10**6),
        name="attention",
    )(*operands)


def back_kernel(grad_kv_pre, grad_uq_pre, w_uq, w_kv, halo_grad, grad_normed):
    halo = pl.ds(0, HALO)
    own = pl.ds(HALO, ROWS)

    def along(rows):
        total = None
        for head in range(HEADS):
            term = dot_nt(grad_kv_pre[head, rows, :], w_kv[:, pl.ds(head * PAIR, PAIR)])
            total = term if total is None else total + term
        return total

    halo_grad[...] = along(halo).astype(bf16)
    across = dot(w_uq[...], grad_uq_pre[...].reshape(2 * WIDTH, ROWS))
    grad_normed[...] = across.T + along(own)


def back_call(*operands):
    return pl.pallas_call(
        back_kernel,
        in_specs=[VMEM] * len(operands),
        out_specs=[VMEM] * 2,
        out_shape=(
            jax.ShapeDtypeStruct((HALO, WIDTH), bf16),
            jax.ShapeDtypeStruct((ROWS, WIDTH), f32),
        ),
        compiler_params=pltpu.CompilerParams(vmem_limit_bytes=32 * MIB),
        cost_estimate=pl.CostEstimate(flops=32 * 10**8, bytes_accessed=14 * MIB, transcendentals=0),
        name="projection_gradient",
    )(*operands)


def pair_kernel(mine, arrived, total, staging, sem):
    staging[...] = (mine[...].astype(f32) + arrived[...].astype(f32)).astype(bf16)
    copy = pltpu.make_async_copy(staging, total, sem)
    copy.start()
    copy.wait()


def pair_call(mine, arrived):
    return pl.pallas_call(
        pair_kernel,
        in_specs=[VMEM] * 2,
        out_specs=HBM,
        out_shape=jax.ShapeDtypeStruct(mine.shape, bf16),
        scratch_shapes=[pltpu.VMEM(mine.shape, bf16), pltpu.SemaphoreType.DMA],
        compiler_params=pltpu.CompilerParams(vmem_limit_bytes=24 * MIB),
        name="pair_sum",
    )(mine, arrived)


def chips_kernel(parts, after, totals, staging, sem):
    del after
    total = jnp.sum(parts[...].astype(f32), axis=0, keepdims=True).astype(bf16)
    staging[...] = jnp.broadcast_to(total, staging.shape)
    copy = pltpu.make_async_copy(staging, totals, sem)
    copy.start()
    copy.wait()


def chips_call(parts, after):
    return pl.pallas_call(
        chips_kernel,
        in_specs=[VMEM, ANY],
        out_specs=HBM,
        out_shape=jax.ShapeDtypeStruct(parts.shape, bf16),
        scratch_shapes=[pltpu.VMEM(parts.shape, bf16), pltpu.SemaphoreType.DMA],
        compiler_params=pltpu.CompilerParams(vmem_limit_bytes=24 * MIB),
        name="chip_sum",
    )(parts, after)


def unpack_kernel(core, first, second, grad_w_in, grad_w_out):
    def piece(block):
        half, at = divmod(block, HALF_BLOCKS)
        return jnp.where(core[0] == half, first[at].astype(f32), second[at].astype(f32))

    for block in range(4 * HEADS):
        grad_w_in[:, pl.ds(block * HEAD_DIM, HEAD_DIM)] = piece(block)
    for block in range(HEADS):
        grad_w_out[:, pl.ds(block * HEAD_DIM, HEAD_DIM)] = piece(4 * HEADS + block)


def unpack_call(core, first, second):
    vmem = pl.BlockSpec(memory_space=pltpu.VMEM)
    return pl.pallas_call(
        unpack_kernel,
        in_specs=[pl.BlockSpec(memory_space=pltpu.SMEM), vmem, vmem],
        out_specs=[vmem] * 2,
        out_shape=(
            jax.ShapeDtypeStruct((WIDTH, 4 * WIDTH), f32),
            jax.ShapeDtypeStruct((WIDTH, WIDTH), f32),
        ),
        compiler_params=pltpu.CompilerParams(vmem_limit_bytes=24 * MIB),
        name="unpack",
    )(core, first, second)


def step_kernel(tokens, in_gain, cotangent, grad_normed, sent, swapped, core, grad_tokens):
    normed, inverse = layer_norm_rows(tokens[...].astype(f32))
    near = jnp.where(core[0] == 0, swapped[...].astype(f32), 0.0)
    upstream = grad_normed[...] + sent[...].astype(f32) + near
    scaled_grad = upstream * in_gain[...]
    first = jnp.mean(scaled_grad, axis=1, keepdims=True)
    second = jnp.mean(scaled_grad * normed, axis=1, keepdims=True)
    grad_tokens[...] = (
        cotangent[...].astype(f32) + (scaled_grad - first - normed * second) * inverse
    ).astype(bf16)


def step_call(tokens, in_gain, cotangent, grad_normed, sent, swapped, core):
    vmem = pl.BlockSpec(memory_space=pltpu.VMEM)
    return pl.pallas_call(
        step_kernel,
        in_specs=[vmem] * 6 + [pl.BlockSpec(memory_space=pltpu.SMEM)],
        out_specs=vmem,
        out_shape=jax.ShapeDtypeStruct((ROWS, WIDTH), bf16),
        compiler_params=pltpu.CompilerParams(vmem_limit_bytes=24 * MIB),
        name="input_norm_gradient",
    )(tokens, in_gain, cotangent, grad_normed, sent, swapped, core)


def shifted(value, steps):
    count = 128
    first, last = (max(0, -steps), min(count, count - steps))
    return lax.ppermute(value, ALL, [(source, source + steps) for source in range(first, last)])


SWAP = [(0, 1), (1, 0)]


def on_device(tokens, user_ids, in_gain, out_gain, w_in, w_out, cotangent):
    core = lax.axis_index("core").astype(jnp.int32).reshape(1)
    in_gain_row = in_gain.reshape(1, WIDTH)
    w_uq = w_in[:, : 2 * WIDTH]
    w_kv = w_in[:, 2 * WIDTH :].reshape(WIDTH, 2, HEADS, HEAD_DIM).transpose(0, 2, 1, 3).reshape(WIDTH, 2 * WIDTH)

    far = shifted(tokens, 2)
    near_a = lax.ppermute(tokens, "core", [(0, 1)])
    far_ids = shifted(user_ids, 2)
    near_ids = shifted(user_ids, 1)
    *window, uq_t, uq_slope_t = own_call(tokens, in_gain_row, w_uq.T, w_kv)
    far = relay_call(far, uq_t)
    near_b = lax.ppermute(far, "core", [(1, 0)])
    window_ids = jnp.concatenate([far_ids, near_ids, user_ids])
    layer_out, grad_kv_pre, grad_uq_pre, mine, theirs = main_call(
        core, far, near_a, near_b, *window, uq_slope_t,
        uq_t, tokens, in_gain_row, out_gain.reshape(WIDTH, 1), w_kv, w_out, cotangent,
        user_ids.reshape(1, ROWS), window_ids.reshape(WINDOW_ROWS, 1),
    )

    arrived = lax.ppermute(theirs, "core", SWAP)
    partial = pair_call(mine, arrived).reshape(64, 80, HEAD_DIM)
    parts = lax.all_to_all(partial, CHIPS, 0, 0, tiled=True)
    halo_grad, grad_normed = back_call(grad_kv_pre, grad_uq_pre, w_uq, w_kv)
    swapped = lax.ppermute(halo_grad[ROWS:], "core", SWAP)
    outgoing = (
        halo_grad[:ROWS].astype(f32) + jnp.where(core[0] == 1, swapped.astype(f32), 0.0)
    ).astype(bf16)
    sent = shifted(outgoing, -2)
    totals = lax.all_to_all(chips_call(parts, outgoing), CHIPS, 0, 0, tiled=True)
    totals = totals.reshape(HALF_BLOCKS, WIDTH, HEAD_DIM)
    other = lax.ppermute(totals, "core", SWAP)
    grad_tokens = step_call(tokens, in_gain_row, cotangent, grad_normed, sent, swapped, core)
    grad_w_in, grad_w_out = unpack_call(core, totals, other)
    return (layer_out, grad_tokens, grad_w_in, grad_w_out)


def solution(mesh):
    fine = Mesh(mesh.devices.reshape(2, 4, 2, 4, 2), ALL)
    placed = (P(ALL, None), P(ALL), P(), P(), P(), P(), P(ALL, None))
    return jax.shard_map(
        on_device,
        mesh=fine,
        in_specs=placed,
        out_specs=(P(ALL, None), P(ALL, None), P(), P()),
        check_vma=False,
    )
```

time: 214 us -> 179 us (0.84)
  Pallas kernels: 72 us -> 55.4 us
  waiting for transfers between devices: 44.6 us -> 30.2 us
  blocking collectives: 27.8 us -> 25.1 us
    ppermute x4, waiting for transfers between devices: 38.5 us -> 21.8 us  [shifted(): lax.ppermute(value, ALL, [(source, source + steps) for source in range(fi...]
    pallas_call x4 -> x6, Pallas kernels: 66.8 us -> 50.2 us  [the longest x1 40.9 us: main_call(): pl.pallas_call(main_kernel, in_specs=[SMEM] + [ANY] * 8 + [VMEM] * (len(o...]
    unnamed x47 -> x46, local copies, waits for them, and re-layouts: 23.7 us -> 16.8 us
    reshape x0 -> x3, local copies, waits for them, and re-layouts: none -> 6.59 us  [on_device(): w_in[:, 2 * WIDTH:].reshape(WIDTH, 2, HEADS, HEAD_DIM).transpose(0, 2, 1, 3)]
    all_to_all x1, starting transfers between devices: 8.17 us -> 11.2 us  [on_device(): parts = lax.all_to_all(partial, CHIPS, 0, 0, tiled=True)]
    transpose x0 -> x1, local copies, waits for them, and re-layouts: none -> 2.67 us  [on_device(): *window, uq_t, uq_slope_t = own_call(tokens, in_gain_row, w_uq.T, w_kv)]
    all_to_all x1, blocking collectives: 27.8 us -> 25.1 us  [on_device(): lax.all_to_all(chips_call(parts, outgoing), CHIPS, 0, 0, tiled=True)]
  transfers between devices with their start and end apart: 10 -> 10, of which waited for: 4 -> 4; matrix products, arithmetic and copies ran while one was open for 4% -> 10% of each run, Pallas kernels for 6% -> 6%
where the time goes in v2:
time: 179 us; the launch traced here: 177 us
  Pallas kernels  55.4 us (31%)
  local copies, waits for them, and re-layouts  32.4 us (18%)
  starting transfers between devices  31.7 us (18%)
  waiting for transfers between devices  30.2 us (17%)
  blocking collectives  25.1 us (14%)
    pallas_call x1, Pallas kernels, main_call(): pl.pallas_call(main_kernel, in_specs=[SMEM] + [ANY] * 8 + [VMEM] * (len(o...  40.9 us
    all_to_all x1, blocking collectives, on_device(): lax.all_to_all(chips_call(parts, outgoing), CHIPS, 0, 0, tiled=True)  25.1 us
    ppermute x4, waiting for transfers between devices, shifted(): lax.ppermute(value, ALL, [(source, source + steps) for source in range(fi...  21.8 us
    unnamed x46, local copies, waits for them, and re-layouts  16.8 us
    all_to_all x1, starting transfers between devices, on_device(): parts = lax.all_to_all(partial, CHIPS, 0, 0, tiled=True)  11.2 us
    ppermute x4, starting transfers between devices, shifted(): lax.ppermute(value, ALL, [(source, source + steps) for source in range(fi...  10.8 us
    reshape x3, local copies, waits for them, and re-layouts, on_device(): w_in[:, 2 * WIDTH:].reshape(WIDTH, 2, HEADS, HEAD_DIM).transpose(0, 2, 1, 3)  6.59 us
    ppermute x1, starting transfers between devices, on_device(): near_b = lax.ppermute(far, 'core', [(1, 0)])  4.16 us
  transfers between devices with their start and end apart: 10, of which 4 were waited for; matrix products, arithmetic and copies ran while one was open for 10% of the time, Pallas kernels for 6%

profile of v2, /device:TPU:39, one launch (start us, length us, event | category | flops | bytes accessed | tf_op | source)
XLA Modules:
  0.0 177.1 jit_solution(5783310227265727749)
XLA Ops:
  0.6 2.7 %collective-permute-start = (bf16[768,512]{1,0:T(8,128)(2,1)}, bf16[768,512]{1,0:T(8,128)(2,1)}, u32[]{:S(2)}, u32[]{:S(2)}) collective-permute-start(bf16[768,512]{1,0:T(8,128)(2,1)} %tokens.5), channel_id=1, source_target_pairs={{0,2},{1,3},{2,4},{3,5},{4,6},{5,7},{6,8},{7,9},{8,10},{9,11},{10,... | collective-permute-start | bytes 2359304 | tf_op jit(solution)/shard_map/ppermute | solution.py:461
  3.3 1.3 collective-permute-start.1
  4.6 3.0 %fusion = (bf16[512,1024]{1,0:T(8,128)(2,1)S(1)}, bf16[1024,512]{0,1:T(8,128)(2,1)}, bf16[512,1024]{1,0:T(8,128)(2,1)S(1)}) fusion(bf16[512,2048]{1,0:T(8,128)(2,1)} %param.11), kind=kLoop, calls=%fused_computation.4 | loop fusion | bytes 5242880 | tf_op jit(solution)/shard_map/slice | solution.py:470
  7.6 1.5 reshape.37
  9.1 3.3 %copy.19 = bf16[512,2,4,128]{3,1,2,0:T(2,128)(2,1)} copy(bf16[512,2,4,128]{3,2,1,0:T(4,128)(2,1)} %reshape.37) | data formatting | bytes 2097152 | tf_op jit(solution)/shard_map/reshape | solution.py:471
  12.4 1.8 %reshape.38.w_kv = bf16[512,1024]{1,0:T(8,128)(2,1)S(1)} reshape(bf16[512,4,2,128]{3,2,1,0:T(2,128)(2,1)} %bitcast.15) | data formatting | bytes 2097152 | tf_op jit(solution)/shard_map/reshape | solution.py:471
  14.2 0.0 copy-start.11
  14.2 2.7 %copy.15.w_uq_t = bf16[1024,512]{1,0:T(8,128)(2,1)} copy(bf16[1024,512]{0,1:T(8,128)(2,1)} %get-tuple-element.35) | data formatting | bytes 2097152 | tf_op jit(solution)/shard_map/transpose | solution.py:477
  16.9 1.2 copy-done.7
  18.1 4.0 %own_projection.1 = (bf16[512,768]{1,0:T(8,128)(2,1)S(1)}, bf16[8,768,128]{2,1,0:T(8,128)(2,1)S(1)}, bf16[8,128,768]{2,1,0:T(8,128)(2,1)S(1)}, bf16[4,768,256]{2...) custom-call(bf16[768,512]{1,0:T(8,128)(2,1)S(1)} %copy-done.8, ...), custom_call_target="tpu_custom_call" | custom-call | flops 1610612736 | bytes 12582912 | tf_op jit(solution)/shard_map/own_projection/pallas_call | solution.py:111
  22.2 0.0 copy-start
  22.2 1.1 copy-done
  23.3 1.2 copy-done.14
  24.5 1.2 copy-done.15
  25.7 1.2 copy-done.16
  26.9 1.1 copy-done.17
  28.1 0.9 copy-done.19
  28.9 4.2 %collective-permute-start.2 = (bf16[768,512]{1,0:T(8,128)(2,1)}, bf16[768,512]{1,0:T(8,128)(2,1)S(1)}, u32[]{:S(2)}, u32[]{:S(2)}) collective-permute-start(bf16[768,512]{1,0:T(8,128)(2,1)} %relay.1.far), channel_id=1, source_target_pairs={{1,0},{3,2},{5,4},{7,6},{9,8},{11,10},{13,12},{15,14},{17,16},{19,... | collective-permute-start | bytes 2359304 | tf_op jit(solution)/shard_map/ppermute | solution.py:479
  33.1 3.1 %collective-permute-start.3 = (s32[768]{0:T(1024)S(1)}, s32[768]{0:T(1024)S(1)}, u32[]{:S(2)}, u32[]{:S(2)}) collective-permute-start(s32[768]{0:T(1024)S(1)} %copy-done.20), channel_id=1, source_target_pairs={{0,2},{1,3},{2,4},{3,5},{4,6},{5,7},{6,8},{7,9},{8,10},{9,11},{10,... | collective-permute-start | bytes 9224 | tf_op jit(solution)/shard_map/ppermute | solution.py:461
  36.2 2.8 %collective-permute-start.4 = (s32[768]{0:T(1024)S(1)}, s32[768]{0:T(1024)S(1)}, u32[]{:S(2)}, u32[]{:S(2)}) collective-permute-start(s32[768]{0:T(1024)S(1)} %copy-done.20), channel_id=1, source_target_pairs={{0,1},{1,2},{2,3},{3,4},{4,5},{5,6},{6,7},{7,8},{8,9},{9,10},{10,1... | collective-permute-start | bytes 9224 | tf_op jit(solution)/shard_map/ppermute | solution.py:461
  39.1 0.6 reshape.40.ids_row
  39.7 0.9 copy.16.out_gain
  40.5 1.9 %reshape.44.ids_col = s32[2304,1]{1,0:T(8,128)} reshape(s32[2304]{0:T(1024)S(1)} %pad_add_fusion) | data formatting | bytes 18432 | tf_op jit(solution)/shard_map/reshape | solution.py:484
  42.4 0.9 copy-done.22
  43.3 40.9 %attention.1 = (bf16[768,512]{1,0:T(8,128)(2,1)}, bf16[4,2304,256]{2,1,0:T(8,128)(2,1)}, bf16[8,128,768]{2,1,0:T(8,128)(2,1)}, bf16[10,512,128]{2,1,0:T(8,128)(2,1)}, bf16[10,512,128]{2,1,0:T(8,128)(2,1)}) custom-call(s32[1]{0:T(128)} %bitcast.core, bf16[768,512]{1,0:T(8,128)(2,1)} %relay.1.far, bf16[768,512]{1,0:T(8,128)(2,1)} %collective-permute-done.1.near_a, ...), custom_call_target="tpu_custom_call" | custom-call | flops 20000000000 | bytes 25165824 | tf_op jit(solution)/shard_map/attention/pallas_call | solution.py:322
  84.2 0.3 collective-permute-start.7
  84.5 3.0 %collective-permute-done.7.arrived = bf16[10,512,128]{2,1,0:T(8,128)(2,1)S(1)} collective-permute-done((bf16[10,512,128]{2,1,0:T(8,128)(2,1)}, bf16[10,512,128]{2,1,0:T(8,128)(2,1)S(1)}, u32[]{:S(2)}, u32[]{:S(2)}) %collective-permute-start.7) | collective-permute-done | bytes 1310752 | tf_op jit(solution)/shard_map/ppermute | solution.py:487
  87.5 1.3 copy-done.4
  88.8 1.4 pair_sum.1
  90.3 11.2 %all-to-all-start = ((bf16[64,80,128]{2,1,0:T(8,128)(2,1)}), bf16[64,80,128]{2,1,0:T(8,128)(2,1)S(1)}, u32[]{:S(2)}, u32[]{:S(2)}) async-start(bf16[64,80,128]{2,1,0:T(8,128)(2,1)} %bitcast.5), calls=%async_computation | async-start | bytes 2621440 | tf_op jit(solution)/shard_map/all_to_all | solution.py:489
  101.4 1.2 copy-done.6
  102.6 2.3 %copy-done.13 = bf16[4,2304,256]{2,1,0:T(8,128)(2,1)S(1)} copy-done((bf16[4,2304,256]{2,1,0:T(8,128)(2,1)S(1)}, bf16[4,2304,256]{2,1,0:T(8,128)(2,1)}, u32[]{:S(2)}) %copy-start.13) | copy-done | bytes 4718616
  105.0 1.4 copy-done.18
  106.4 3.5 %projection_gradient.1 = (bf16[1536,512]{1,0:T(8,128)(2,1)S(1)}, f32[768,512]{1,0:T(8,128)S(1)}) custom-call(bf16[4,2304,256]{2,1,0:T(8,128)(2,1)S(1)} %copy-done.13, bf16[8,128,768]{2,1,0:T(8,128)(2,1)S(1)} %copy-done.18, bf16[512,1024]{1,0:T(8,128)(2,1)S(1)} %get-tuple-element.34.w_uq, bf16[512,1024]{1,0:T(8,128)(2,1)S(1)} %copy-done.6), custom_call_target="tpu_custom_call" | custom-call | flops 3200000000 | bytes 14680064 | tf_op jit(solution)/shard_map/projection_gradient/pallas_call | solution.py:354
  110.0 1.2 copy-done.1
  111.1 0.1 slice.15
  111.2 0.4 copy-done.2
  111.6 0.9 collective-permute-start.5
  112.5 1.9 %collective-permute-done.5.swapped = bf16[768,512]{1,0:T(8,128)(2,1)S(1)} collective-permute-done((bf16[768,512]{1,0:T(8,128)(2,1)S(1)}, bf16[768,512]{1,0:T(8,128)(2,1)S(1)}, u32[]{:S(2)}, u32[]{:S(2)}) %collective-permute-start.5) | collective-permute-done | bytes 786464 | tf_op jit(solution)/shard_map/ppermute | solution.py:491
  114.4 1.4 add_convert_fusion.after
  115.8 3.4 %all-to-all-done.parts = bf16[64,80,128]{2,1,0:T(8,128)(2,1)S(1)} async-done(((bf16[64,80,128]{2,1,0:T(8,128)(2,1)}), bf16[64,80,128]{2,1,0:T(8,128)(2,1)S(1)}, u32[]{:S(2)}, u32[]{:S(2)}) %all-to-all-start) | async-done | bytes 1310752 | tf_op jit(solution)/shard_map/all_to_all | solution.py:489
  119.2 0.3 chip_sum.1
  119.6 25.1 %all_to_all.10 = bf16[64,80,128]{2,1,0:T(8,128)(2,1)S(1)} all-to-all(bf16[64,80,128]{2,1,0:T(8,128)(2,1)S(1)} %chip_sum.1), channel_id=1, replica_groups=mesh['z_hi'=2,'y'=4,'z_lo'=2,'x'=4,'core'=2] {'z_hi','y','z_lo','x'}, dimensions={0} | all-to-all | bytes 2621440 | tf_op jit(solution)/shard_map/all_to_all | solution.py:496
  144.7 3.1 %collective-permute-start.8 = (bf16[10,512,128]{2,1,0:T(8,128)(2,1)S(1)}, bf16[10,512,128]{2,1,0:T(8,128)(2,1)S(1)}, u32[]{:S(2)}, u32[]{:S(2)}) collective-permute-start(bf16[10,512,128]{2,1,0:T(8,128)(2,1)S(1)} %bitcast.10), channel_id=1, source_target_pairs={{0,1},{1,0},{2,3},{3,2},{4,5},{5,4},{6,7},{7,6},{8,9},{9,8},{10,11... | collective-permute-start | bytes 3932168 | tf_op jit(solution)/shard_map/ppermute | solution.py:498
  147.8 2.2 %collective-permute-start.6 = (bf16[768,512]{1,0:T(8,128)(2,1)S(1)}, bf16[768,512]{1,0:T(8,128)(2,1)S(1)}, u32[]{:S(2)}, u32[]{:S(2)}) collective-permute-start(bf16[768,512]{1,0:T(8,128)(2,1)S(1)} %add_convert_fusion.after), channel_id=1, source_target_pairs={{2,0},{3,1},{4,2},{5,3},{6,4},{7,5},{8,6},{9,7},{10,8},{11,9},{12,... | collective-permute-start | bytes 2359304 | tf_op jit(solution)/shard_map/ppermute | solution.py:461
  150.0 21.8 %collective-permute-done.6.sent = bf16[768,512]{1,0:T(8,128)(2,1)S(1)} collective-permute-done((bf16[768,512]{1,0:T(8,128)(2,1)S(1)}, bf16[768,512]{1,0:T(8,128)(2,1)S(1)}, u32[]{:S(2)}, u32[]{:S(2)}) %collective-permute-start.6) | collective-permute-done | bytes 786464 | tf_op jit(solution)/shard_map/ppermute | solution.py:461
  171.9 2.2 %input_norm_gradient.1 = bf16[768,512]{1,0:T(8,128)(2,1)} custom-call(bf16[768,512]{1,0:T(8,128)(2,1)S(1)} %copy-done.9, f32[1,512]{1,0:T(1,128)S(1)} %bitcast.14, bf16[768,512]{1,0:T(8,128)(2,1)S(1)} %copy-done.10, f32[768,512]{1,0:T(8,128)S(1)} %copy-done.3, bf16[768,512]{1,0:T(8,128)(2,1)S(1)} %collective-permute-done.6.sent, ...), custom_call_target="tpu_custom_call" | custom-call | tf_op jit(solution)/shard_map/input_norm_gradient/pallas_call | solution.py:448
  174.1 3.0 %unpack.1 = (f32[512,2048]{1,0:T(8,128)}, f32[512,512]{1,0:T(8,128)}) custom-call(s32[1]{0:T(128)} %bitcast.core, bf16[10,512,128]{2,1,0:T(8,128)(2,1)S(1)} %bitcast.11, bf16[10,512,128]{2,1,0:T(8,128)(2,1)S(1)} %collective-permute-done.8.second), custom_call_target="tpu_custom_call" | custom-call | tf_op jit(solution)/shard_map/unpack/pallas_call | solution.py:421
  (38 shorter events, 0.1 us)
Async XLA Ops:
  0.6 28.3 %collective-permute-start = (bf16[768,512]{1,0:T(8,128)(2,1)}, bf16[768,512]{1,0:T(8,128)(2,1)}, u32[]{:S(2)}, u32[]{:S(2)}) collective-permute-start(bf16[768,512]{1,0:T(8,128)(2,1)} %tokens.5), channel_id=1, source_target_pairs={{0,2},{1,3},{2,4},{3,5},{4,6},{5,7},{6,8},{7,9},{8,10},{9,11},{10,... | collective-permute-start | bytes 2359304 | tf_op jit(solution)/shard_map/ppermute | solution.py:461
  3.3 39.1 %collective-permute-start.1 = (bf16[768,512]{1,0:T(8,128)(2,1)}, bf16[768,512]{1,0:T(8,128)(2,1)}, u32[]{:S(2)}, u32[]{:S(2)}) collective-permute-start(bf16[768,512]{1,0:T(8,128)(2,1)} %tokens.5), channel_id=1, source_target_pairs={{0,1},{2,3},{4,5},{6,7},{8,9},{10,11},{12,13},{14,15},{16,17},{18,... | collective-permute-start | bytes 2359304 | tf_op jit(solution)/shard_map/ppermute | solution.py:474
  14.2 8.0 %copy-start.5 = (bf16[512,1024]{1,0:T(8,128)(2,1)}, bf16[512,1024]{1,0:T(8,128)(2,1)S(1)}, u32[]{:S(2)}) copy-start(bf16[512,1024]{1,0:T(8,128)(2,1)S(1)} %reshape.38.w_kv) | copy-start | bytes 3145732
  14.2 2.7 %copy-start.8 = (bf16[768,512]{1,0:T(8,128)(2,1)S(1)}, bf16[768,512]{1,0:T(8,128)(2,1)}, u32[]{:S(2)}) copy-start(bf16[768,512]{1,0:T(8,128)(2,1)} %tokens.5) | copy-start | bytes 2359300
  14.2 2.7 %copy-start.11 = (f32[512]{0:T(512)S(1)}, f32[512]{0:T(512)}, u32[]{:S(2)}) copy-start(f32[512]{0:T(512)} %param.9) | copy-start | bytes 6148
  16.9 1.2 copy-start.7
  22.2 1.1 copy-start
  23.3 1.2 copy-start.14
  24.5 1.2 copy-start.15
  25.7 1.2 copy-start.16
  26.9 1.1 copy-start.17
  28.1 0.9 copy-start.19
  28.9 4.2 %copy-start.20 = (s32[768]{0:T(1024)S(1)}, s32[768]{0:T(1024)}, u32[]{:S(2)}) copy-start(s32[768]{0:T(1024)} %param.8) | copy-start | bytes 9220
  28.9 10.7 %copy-start.21 = (f32[512]{0:T(512)S(1)}, f32[512]{0:T(512)}, u32[]{:S(2)}) copy-start(f32[512]{0:T(512)} %param.10) | copy-start | bytes 6148
  28.9 13.5 %collective-permute-start.2 = (bf16[768,512]{1,0:T(8,128)(2,1)}, bf16[768,512]{1,0:T(8,128)(2,1)S(1)}, u32[]{:S(2)}, u32[]{:S(2)}) collective-permute-start(bf16[768,512]{1,0:T(8,128)(2,1)} %relay.1.far), channel_id=1, source_target_pairs={{1,0},{3,2},{5,4},{7,6},{9,8},{11,10},{13,12},{15,14},{17,16},{19,... | collective-permute-start | bytes 2359304 | tf_op jit(solution)/shard_map/ppermute | solution.py:479
  33.1 7.4 %collective-permute-start.3 = (s32[768]{0:T(1024)S(1)}, s32[768]{0:T(1024)S(1)}, u32[]{:S(2)}, u32[]{:S(2)}) collective-permute-start(s32[768]{0:T(1024)S(1)} %copy-done.20), channel_id=1, source_target_pairs={{0,2},{1,3},{2,4},{3,5},{4,6},{5,7},{6,8},{7,9},{8,10},{9,11},{10,... | collective-permute-start | bytes 9224 | tf_op jit(solution)/shard_map/ppermute | solution.py:461
  36.2 4.3 %collective-permute-start.4 = (s32[768]{0:T(1024)S(1)}, s32[768]{0:T(1024)S(1)}, u32[]{:S(2)}, u32[]{:S(2)}) collective-permute-start(s32[768]{0:T(1024)S(1)} %copy-done.20), channel_id=1, source_target_pairs={{0,1},{1,2},{2,3},{3,4},{4,5},{5,6},{6,7},{7,8},{8,9},{9,10},{10,1... | collective-permute-start | bytes 9224 | tf_op jit(solution)/shard_map/ppermute | solution.py:461
  42.4 0.9 copy-start.22
  84.2 3.3 %collective-permute-start.7 = (bf16[10,512,128]{2,1,0:T(8,128)(2,1)}, bf16[10,512,128]{2,1,0:T(8,128)(2,1)S(1)}, u32[]{:S(2)}, u32[]{:S(2)}) collective-permute-start(bf16[10,512,128]{2,1,0:T(8,128)(2,1)} %get-tuple-element.31), channel_id=1, source_target_pairs={{0,1},{1,0},{2,3},{3,2},{4,5},{5,4},{6,7},{7,6},{8,9},{9,8},{10,11... | collective-permute-start | bytes 3932168 | tf_op jit(solution)/shard_map/ppermute | solution.py:487
  87.5 1.3 copy-start.4
  90.3 29.0 %all-to-all-start = ((bf16[64,80,128]{2,1,0:T(8,128)(2,1)}), bf16[64,80,128]{2,1,0:T(8,128)(2,1)S(1)}, u32[]{:S(2)}, u32[]{:S(2)}) async-start(bf16[64,80,128]{2,1,0:T(8,128)(2,1)} %bitcast.5), calls=%async_computation | async-start | bytes 2621440 | tf_op jit(solution)/shard_map/all_to_all | solution.py:489
  101.4 1.2 copy-start.6
  102.6 2.3 %copy-start.13 = (bf16[4,2304,256]{2,1,0:T(8,128)(2,1)S(1)}, bf16[4,2304,256]{2,1,0:T(8,128)(2,1)}, u32[]{:S(2)}) copy-start(bf16[4,2304,256]{2,1,0:T(8,128)(2,1)} %get-tuple-element.26.grad_kv_pre) | copy-start | bytes 14155780
  105.0 1.4 copy-start.18
  109.9 1.2 copy-start.1
  109.9 1.7 copy-start.2
  111.6 2.8 %collective-permute-start.5 = (bf16[768,512]{1,0:T(8,128)(2,1)S(1)}, bf16[768,512]{1,0:T(8,128)(2,1)S(1)}, u32[]{:S(2)}, u32[]{:S(2)}) collective-permute-start(bf16[768,512]{1,0:T(8,128)(2,1)S(1)} %slice.15), channel_id=1, source_target_pairs={{0,1},{1,0},{2,3},{3,2},{4,5},{5,4},{6,7},{7,6},{8,9},{9,8},{10,11... | collective-permute-start | bytes 2359304 | tf_op jit(solution)/shard_map/ppermute | solution.py:491
  119.2 52.6 %copy-start.10 = (bf16[768,512]{1,0:T(8,128)(2,1)S(1)}, bf16[768,512]{1,0:T(8,128)(2,1)}, u32[]{:S(2)}) copy-start(bf16[768,512]{1,0:T(8,128)(2,1)} %cotangent.3) | copy-start | bytes 2359300
  119.6 52.3 %copy-start.3 = (f32[768,512]{1,0:T(8,128)S(1)}, f32[768,512]{1,0:T(8,128)}, u32[]{:S(2)}) copy-start(f32[768,512]{1,0:T(8,128)} %copy-done.2) | copy-start | bytes 4718596
  119.6 52.3 %copy-start.9 = (bf16[768,512]{1,0:T(8,128)(2,1)S(1)}, bf16[768,512]{1,0:T(8,128)(2,1)}, u32[]{:S(2)}) copy-start(bf16[768,512]{1,0:T(8,128)(2,1)} %tokens.5) | copy-start | bytes 2359300
  119.6 52.3 %copy-start.12 = (f32[512]{0:T(512)S(1)}, f32[512]{0:T(512)}, u32[]{:S(2)}) copy-start(f32[512]{0:T(512)} %param.9) | copy-start | bytes 6148
  144.7 29.3 %collective-permute-start.8 = (bf16[10,512,128]{2,1,0:T(8,128)(2,1)S(1)}, bf16[10,512,128]{2,1,0:T(8,128)(2,1)S(1)}, u32[]{:S(2)}, u32[]{:S(2)}) collective-permute-start(bf16[10,512,128]{2,1,0:T(8,128)(2,1)S(1)} %bitcast.10), channel_id=1, source_target_pairs={{0,1},{1,0},{2,3},{3,2},{4,5},{5,4},{6,7},{7,6},{8,9},{9,8},{10,11... | collective-permute-start | bytes 3932168 | tf_op jit(solution)/shard_map/ppermute | solution.py:498
  147.8 24.1 %collective-permute-start.6 = (bf16[768,512]{1,0:T(8,128)(2,1)S(1)}, bf16[768,512]{1,0:T(8,128)(2,1)S(1)}, u32[]{:S(2)}, u32[]{:S(2)}) collective-permute-start(bf16[768,512]{1,0:T(8,128)(2,1)S(1)} %add_convert_fusion.after), channel_id=1, source_target_pairs={{2,0},{3,1},{4,2},{5,3},{6,4},{7,5},{8,6},{9,7},{10,8},{11,9},{12,... | collective-permute-start | bytes 2359304 | tf_op jit(solution)/shard_map/ppermute | solution.py:461

commit v3 on v2

--- a/solution.py
+++ b/solution.py
@@ -67,28 +67,35 @@
 BAND = len(PLACE) * TILE
 
 
-def project_kv(normed, w_kv, rows, normed_t, kv, kv_t, kv_slope):
+def project_kv(normed, w_in, rows, normed_t, kv, kv_t, kv_slope):
     normed_t[:, rows] = normed.T
-    for head in range(HEADS):
-        silu, slope = silu_and_slope(dot(normed, w_kv[:, pl.ds(head * PAIR, PAIR)]))
-        silu = silu.astype(bf16)
-        kv_slope[head, rows, :] = slope.astype(bf16)
-        for part in range(2):
-            one = silu[:, part * HEAD_DIM : (part + 1) * HEAD_DIM]
-            kv[part * HEADS + head, rows, :] = one
-            kv_t[part * HEADS + head, :, rows] = one.T
-
-
-def own_kernel(tokens, in_gain, w_uq_t, w_kv, normed_t, kv, kv_t, kv_slope, uq_t, uq_slope_t):
+    for part in range(2):
+        for pair in range(HEADS // 2):
+            columns = pl.ds((2 + part) * WIDTH + pair * PAIR, PAIR)
+            silu, slope = silu_and_slope(dot(normed, w_in[:, columns]))
+            silu = silu.astype(bf16)
+            slope = slope.astype(bf16)
+            for which in range(2):
+                head = 2 * pair + which
+                lanes = slice(which * HEAD_DIM, (which + 1) * HEAD_DIM)
+                kv_slope[head, rows, pl.ds(part * HEAD_DIM, HEAD_DIM)] = slope[:, lanes]
+                kv[part * HEADS + head, rows, :] = silu[:, lanes]
+                kv_t[part * HEADS + head, :, rows] = silu[:, lanes].T
+
+
+def own_kernel(tokens, in_gain, w_in, normed_t, kv, kv_t, kv_slope, uq_t, uq_slope_t):
     for tile in range(TILES):
         rows = pl.ds(tile * TILE, TILE)
         normed, _ = layer_norm_rows(tokens[rows, :].astype(f32))
         normed = (normed * in_gain[...]).astype(bf16)
-        project_kv(normed, w_kv, rows, normed_t, kv, kv_t, kv_slope)
-        for block in range(2 * HEADS):
-            silu, slope = silu_and_slope(dot_nt(w_uq_t[pl.ds(block * HEAD_DIM, HEAD_DIM), :], normed))
-            uq_t[block, :, rows] = silu.astype(bf16)
-            uq_slope_t[block, :, rows] = slope.astype(bf16)
+        project_kv(normed, w_in, rows, normed_t, kv, kv_t, kv_slope)
+    for pair in range(HEADS):
+        w_t = w_in[:, pl.ds(pair * PAIR, PAIR)].T
+        for tile in range(TILES):
+            rows = pl.ds(tile * TILE, TILE)
+            silu, slope = silu_and_slope(dot(w_t, normed_t[:, rows]))
+            uq_t[pl.ds(2 * pair, 2), :, rows] = silu.astype(bf16).reshape(2, HEAD_DIM, TILE)
+            uq_slope_t[pl.ds(2 * pair, 2), :, rows] = slope.astype(bf16).reshape(2, HEAD_DIM, TILE)
 
 
 VMEM = pl.BlockSpec(memory_space=pltpu.VMEM)
@@ -113,7 +120,7 @@
         in_specs=[VMEM] * len(operands),
         out_specs=[VMEM] * 6,
         out_shape=[jax.ShapeDtypeStruct(shape, bf16) for shape in window_shapes(ROWS) + (along, along)],
-        compiler_params=pltpu.CompilerParams(vmem_limit_bytes=40 * MIB),
+        compiler_params=pltpu.CompilerParams(vmem_limit_bytes=62 * MIB),
         cost_estimate=pl.CostEstimate(
             flops=2 * ROWS * WIDTH * 4 * WIDTH, bytes_accessed=12 * MIB, transcendentals=ROWS * 4 * WIDTH
         ),
@@ -138,7 +145,7 @@
 
 def main_kernel(
     core, far, near_a, near_b, own_normed_t, own_kv, own_kv_t, own_kv_slope, own_uq_slope_t,
-    uq_t, tokens, in_gain, out_gain, w_kv, w_out, cotangent, ids_row, ids_col,
+    uq_t, tokens, in_gain, out_gain, w_in, w_out, cotangent, far_ids, near_ids, own_ids,
     layer_out, grad_kv_pre, grad_uq_pre, mine, theirs,
     normed_t, kv, kv_t, kv_slope, uq_slope_t, mask, weights, slopes, mixed_t, grad_attn_t, gated_t, both, sems,
 ):
@@ -170,13 +177,17 @@
 
     key_at = lax.broadcasted_iota(jnp.int32, (TILE, TILE), 0)
     query_at = lax.broadcasted_iota(jnp.int32, (TILE, TILE), 1)
-    for (key_tile, tile), place in PLACE.items():
-        allowed = ids_col[pl.ds(key_tile * TILE, TILE), :] == ids_row[:, pl.ds(tile * TILE, TILE)]
-        if key_tile == tile:
-            allowed = allowed & (key_at > query_at)
-        if key_tile == tile + SPREAD - 1:
-            allowed = allowed & (key_at <= query_at)
-        mask[:, pl.ds(place, TILE)] = jnp.where(allowed, 1.0, 0.0).astype(bf16)
+    for key_tile in range(KEY_TILES):
+        source = (far_ids, near_ids, own_ids)[key_tile // TILES]
+        key_ids = source[:, pl.ds(key_tile % TILES * TILE, TILE)].astype(f32)
+        key_ids = jnp.broadcast_to(key_ids, (TILE, TILE)).T
+        for tile in query_tiles(key_tile):
+            allowed = key_ids == own_ids[:, pl.ds(tile * TILE, TILE)].astype(f32)
+            if key_tile == tile:
+                allowed = allowed & (key_at > query_at)
+            if key_tile == tile + SPREAD - 1:
+                allowed = allowed & (key_at <= query_at)
+            mask[:, pl.ds(PLACE[key_tile, tile], TILE)] = jnp.where(allowed, 1.0, 0.0).astype(bf16)
 
     for copy in arrivals:
         copy.wait()
@@ -188,7 +199,7 @@
             halo = staged(1, at)[...].astype(f32) + staged(2, at)[...].astype(f32)
         normed, _ = layer_norm_rows(halo)
         normed = (normed * in_gain[...]).astype(bf16)
-        project_kv(normed, w_kv, pl.ds(tile * TILE, TILE), normed_t, kv, kv_t, kv_slope)
+        project_kv(normed, w_in, pl.ds(tile * TILE, TILE), normed_t, kv, kv_t, kv_slope)
     for copy in fetches:
         copy.wait()
 
@@ -226,7 +237,8 @@
             slot = jnp.where(high == core[0], 0, 1)
             both[slot, at - high * HALF_BLOCKS] = value[:, part * HEAD_DIM : (part + 1) * HEAD_DIM]
 
-    gain = out_gain[...]
+    gain = jnp.broadcast_to(out_gain[...], (HEAD_DIM, WIDTH)).T
+    gain = jnp.concatenate([gain] * (TILE // HEAD_DIM), axis=1)
     for tile in range(TILES):
         rows = pl.ds(tile * TILE, TILE)
         mixed = mixed_t[:, :, rows].reshape(WIDTH, TILE)
@@ -334,19 +346,20 @@
     )(*operands)
 
 
-def back_kernel(grad_kv_pre, grad_uq_pre, w_uq, w_kv, halo_grad, grad_normed):
+def back_kernel(grad_kv_pre, grad_uq_pre, w_in, halo_grad, grad_normed):
     halo = pl.ds(0, HALO)
     own = pl.ds(HALO, ROWS)
 
     def along(rows):
         total = None
         for head in range(HEADS):
-            term = dot_nt(grad_kv_pre[head, rows, :], w_kv[:, pl.ds(head * PAIR, PAIR)])
+            w_pair = [w_in[:, pl.ds((2 + part) * WIDTH + head * HEAD_DIM, HEAD_DIM)] for part in range(2)]
+            term = dot_nt(grad_kv_pre[head, rows, :], jnp.concatenate(w_pair, axis=1))
             total = term if total is None else total + term
         return total
 
     halo_grad[...] = along(halo).astype(bf16)
-    across = dot(w_uq[...], grad_uq_pre[...].reshape(2 * WIDTH, ROWS))
+    across = dot(w_in[:, pl.ds(0, 2 * WIDTH)], grad_uq_pre[...].reshape(2 * WIDTH, ROWS))
     grad_normed[...] = across.T + along(own)
 
 
@@ -359,7 +372,7 @@
             jax.ShapeDtypeStruct((HALO, WIDTH), bf16),
             jax.ShapeDtypeStruct((ROWS, WIDTH), f32),
         ),
-        compiler_params=pltpu.CompilerParams(vmem_limit_bytes=32 * MIB),
+        compiler_params=pltpu.CompilerParams(vmem_limit_bytes=62 * MIB),
         cost_estimate=pl.CostEstimate(flops=32 * 10**8, bytes_accessed=14 * MIB, transcendentals=0),
         name="projection_gradient",
     )(*operands)
@@ -379,7 +392,7 @@
         out_specs=HBM,
         out_shape=jax.ShapeDtypeStruct(mine.shape, bf16),
         scratch_shapes=[pltpu.VMEM(mine.shape, bf16), pltpu.SemaphoreType.DMA],
-        compiler_params=pltpu.CompilerParams(vmem_limit_bytes=24 * MIB),
+        compiler_params=pltpu.CompilerParams(vmem_limit_bytes=62 * MIB),
         name="pair_sum",
     )(mine, arrived)
 
@@ -400,7 +413,7 @@
         out_specs=HBM,
         out_shape=jax.ShapeDtypeStruct(parts.shape, bf16),
         scratch_shapes=[pltpu.VMEM(parts.shape, bf16), pltpu.SemaphoreType.DMA],
-        compiler_params=pltpu.CompilerParams(vmem_limit_bytes=24 * MIB),
+        compiler_params=pltpu.CompilerParams(vmem_limit_bytes=62 * MIB),
         name="chip_sum",
     )(parts, after)
 
@@ -426,7 +439,7 @@
             jax.ShapeDtypeStruct((WIDTH, 4 * WIDTH), f32),
             jax.ShapeDtypeStruct((WIDTH, WIDTH), f32),
         ),
-        compiler_params=pltpu.CompilerParams(vmem_limit_bytes=24 * MIB),
+        compiler_params=pltpu.CompilerParams(vmem_limit_bytes=62 * MIB),
         name="unpack",
     )(core, first, second)
 
@@ -450,7 +463,7 @@
         in_specs=[vmem] * 6 + [pl.BlockSpec(memory_space=pltpu.SMEM)],
         out_specs=vmem,
         out_shape=jax.ShapeDtypeStruct((ROWS, WIDTH), bf16),
-        compiler_params=pltpu.CompilerParams(vmem_limit_bytes=24 * MIB),
+        compiler_params=pltpu.CompilerParams(vmem_limit_bytes=62 * MIB),
         name="input_norm_gradient",
     )(tokens, in_gain, cotangent, grad_normed, sent, swapped, core)
 
@@ -467,27 +480,25 @@
 def on_device(tokens, user_ids, in_gain, out_gain, w_in, w_out, cotangent):
     core = lax.axis_index("core").astype(jnp.int32).reshape(1)
     in_gain_row = in_gain.reshape(1, WIDTH)
-    w_uq = w_in[:, : 2 * WIDTH]
-    w_kv = w_in[:, 2 * WIDTH :].reshape(WIDTH, 2, HEADS, HEAD_DIM).transpose(0, 2, 1, 3).reshape(WIDTH, 2 * WIDTH)
+    own_ids = user_ids.reshape(1, ROWS)
 
     far = shifted(tokens, 2)
     near_a = lax.ppermute(tokens, "core", [(0, 1)])
-    far_ids = shifted(user_ids, 2)
-    near_ids = shifted(user_ids, 1)
-    *window, uq_t, uq_slope_t = own_call(tokens, in_gain_row, w_uq.T, w_kv)
+    far_ids = shifted(own_ids, 2)
+    near_ids = shifted(own_ids, 1)
+    *window, uq_t, uq_slope_t = own_call(tokens, in_gain_row, w_in)
     far = relay_call(far, uq_t)
     near_b = lax.ppermute(far, "core", [(1, 0)])
-    window_ids = jnp.concatenate([far_ids, near_ids, user_ids])
     layer_out, grad_kv_pre, grad_uq_pre, mine, theirs = main_call(
         core, far, near_a, near_b, *window, uq_slope_t,
-        uq_t, tokens, in_gain_row, out_gain.reshape(WIDTH, 1), w_kv, w_out, cotangent,
-        user_ids.reshape(1, ROWS), window_ids.reshape(WINDOW_ROWS, 1),
+        uq_t, tokens, in_gain_row, out_gain.reshape(1, WIDTH), w_in, w_out, cotangent,
+        far_ids, near_ids, own_ids,
     )
 
     arrived = lax.ppermute(theirs, "core", SWAP)
     partial = pair_call(mine, arrived).reshape(64, 80, HEAD_DIM)
     parts = lax.all_to_all(partial, CHIPS, 0, 0, tiled=True)
-    halo_grad, grad_normed = back_call(grad_kv_pre, grad_uq_pre, w_uq, w_kv)
+    halo_grad, grad_normed = back_call(grad_kv_pre, grad_uq_pre, w_in)
     swapped = lax.ppermute(halo_grad[ROWS:], "core", SWAP)
     outgoing = (
         halo_grad[:ROWS].astype(f32) + jnp.where(core[0] == 1, swapped.astype(f32), 0.0)

time: 179 us -> 183 us (1.022)
  local copies, waits for them, and re-layouts: 32.4 us -> 7.72 us
  Pallas kernels: 55.4 us -> 72.2 us
  waiting for transfers between devices: 30.2 us -> 37.7 us
  starting transfers between devices: 31.7 us -> 34.4 us
    unnamed x46 -> x24, local copies, waits for them, and re-layouts: 16.8 us -> 5.65 us
    reshape x6 -> x1, local copies, waits for them, and re-layouts: 9.93 us -> 0.01 us  [on_device(): own_ids = user_ids.reshape(1, ROWS)]
    ppermute x4, waiting for transfers between devices: 21.8 us -> 31.3 us  [shifted(): lax.ppermute(value, ALL, [(source, source + steps) for source in range(fi...]
    pallas_call x1, Pallas kernels: 3.54 us -> 8.13 us  [back_call(): pl.pallas_call(back_kernel, in_specs=[VMEM] * len(operands), out_specs=[V...]
    pallas_call x1, Pallas kernels: 4.04 us -> 8.19 us  [own_call(): pl.pallas_call(own_kernel, in_specs=[VMEM] * len(operands), out_specs=[VM...]
    slice x1 -> x0, local copies, waits for them, and re-layouts: 2.97 us -> none  [on_device(): w_uq = w_in[:, :2 * WIDTH]]
    transpose x1 -> x0, local copies, waits for them, and re-layouts: 2.67 us -> none  [on_device(): *window, uq_t, uq_slope_t = own_call(tokens, in_gain_row, w_uq.T, w_kv)]
    pallas_call x1, Pallas kernels: 0.35 us -> 2.64 us  [chips_call(): pl.pallas_call(chips_kernel, in_specs=[VMEM, ANY], out_specs=HBM, out_sha...]
  transfers between devices with their start and end apart: 10 -> 10, of which waited for: 4 -> 6; matrix products, arithmetic and copies ran while one was open for 10% -> 2% of each run, Pallas kernels for 6% -> 12%
where the time goes in v3:
time: 183 us; the launch traced here: 181 us
  Pallas kernels  72.2 us (39%)
  waiting for transfers between devices  37.7 us (21%)
  starting transfers between devices  34.4 us (19%)
  blocking collectives  25.7 us (14%)
  local copies, waits for them, and re-layouts  7.72 us (4%)
  other arithmetic  2.25 us (1%)
    pallas_call x1, Pallas kernels, main_call(): pl.pallas_call(main_kernel, in_specs=[SMEM] + [ANY] * 8 + [VMEM] * (len(o...  40.9 us
    ppermute x4, waiting for transfers between devices, shifted(): lax.ppermute(value, ALL, [(source, source + steps) for source in range(fi...  31.3 us
    all_to_all x1, blocking collectives, on_device(): lax.all_to_all(chips_call(parts, outgoing), CHIPS, 0, 0, tiled=True)  25.7 us
    ppermute x4, starting transfers between devices, shifted(): lax.ppermute(value, ALL, [(source, source + steps) for source in range(fi...  12.5 us
    all_to_all x1, starting transfers between devices, on_device(): parts = lax.all_to_all(partial, CHIPS, 0, 0, tiled=True)  11.4 us
    pallas_call x1, Pallas kernels, own_call(): pl.pallas_call(own_kernel, in_specs=[VMEM] * len(operands), out_specs=[VM...  8.19 us
    pallas_call x1, Pallas kernels, back_call(): pl.pallas_call(back_kernel, in_specs=[VMEM] * len(operands), out_specs=[V...  8.13 us
    unnamed x24, local copies, waits for them, and re-layouts  5.65 us
  transfers between devices with their start and end apart: 10, of which 6 were waited for; matrix products, arithmetic and copies ran while one was open for 2% of the time, Pallas kernels for 12%

profile of v3, /device:TPU:39, one launch (start us, length us, event | category | flops | bytes accessed | tf_op | source)
XLA Modules:
  0.0 180.7 jit_solution(130350538905645108)
XLA Ops:
  0.6 2.7 %collective-permute-start = (bf16[768,512]{1,0:T(8,128)(2,1)}, bf16[768,512]{1,0:T(8,128)(2,1)S(1)}, u32[]{:S(2)}, u32[]{:S(2)}) collective-permute-start(bf16[768,512]{1,0:T(8,128)(2,1)} %tokens.5), channel_id=1, source_target_pairs={{0,2},{1,3},{2,4},{3,5},{4,6},{5,7},{6,8},{7,9},{8,10},{9,11},{10,... | collective-permute-start | bytes 2359304 | tf_op jit(solution)/shard_map/ppermute | solution.py:474
  3.3 1.3 collective-permute-start.1
  4.6 8.2 %own_projection.1 = (bf16[512,768]{1,0:T(8,128)(2,1)}, bf16[8,768,128]{2,1,0:T(8,128)(2,1)}, bf16[8,128,768]{2,1,0:T(8,128)(2,1)}, bf16[4,768,256]{2,1,0:T(8,128...) custom-call(bf16[768,512]{1,0:T(8,128)(2,1)} %tokens.5, f32[1,512]{1,0:T(1,128)} %bitcast.8, ...), custom_call_target="tpu_custom_call" | custom-call | flops 1610612736 | bytes 12582912 | tf_op jit(solution)/shard_map/own_projection/pallas_call | solution.py:118
  12.8 8.3 %collective-permute-done.far = bf16[768,512]{1,0:T(8,128)(2,1)S(1)} collective-permute-done((bf16[768,512]{1,0:T(8,128)(2,1)}, bf16[768,512]{1,0:T(8,128)(2,1)S(1)}, u32[]{:S(2)}, u32[]{:S(2)}) %collective-permute-start) | collective-permute-done | bytes 786464 | tf_op jit(solution)/shard_map/ppermute | solution.py:474
  21.1 0.0 copy-start.5
  21.1 0.9 copy-done.5
  22.0 0.0 copy-start.7
  22.0 4.5 %collective-permute-start.2 = (bf16[768,512]{1,0:T(8,128)(2,1)}, bf16[768,512]{1,0:T(8,128)(2,1)}, u32[]{:S(2)}, u32[]{:S(2)}) collective-permute-start(bf16[768,512]{1,0:T(8,128)(2,1)} %relay.1.far), channel_id=1, source_target_pairs={{1,0},{3,2},{5,4},{7,6},{9,8},{11,10},{13,12},{15,14},{17,16},{19,... | collective-permute-start | bytes 2359304 | tf_op jit(solution)/shard_map/ppermute | solution.py:491
  26.5 0.0 copy-done.7
  26.5 0.0 copy-start.8
  26.5 5.7 %collective-permute-start.3 = (s32[1,768]{1,0:T(1,128)S(1)}, s32[1,768]{1,0:T(1,128)S(1)}, u32[]{:S(2)}, u32[]{:S(2)}) collective-permute-start(s32[1,768]{1,0:T(1,128)S(1)} %reshape.29.own_ids), channel_id=1, source_target_pairs={{0,2},{1,3},{2,4},{3,5},{4,6},{5,7},{6,8},{7,9},{8,10},{9,11},{10,... | collective-permute-start | bytes 9224 | tf_op jit(solution)/shard_map/ppermute | solution.py:474
  32.2 1.9 %collective-permute-start.4 = (s32[1,768]{1,0:T(1,128)S(1)}, s32[1,768]{1,0:T(1,128)S(1)}, u32[]{:S(2)}, u32[]{:S(2)}) collective-permute-start(s32[1,768]{1,0:T(1,128)S(1)} %reshape.29.own_ids), channel_id=1, source_target_pairs={{0,1},{1,2},{2,3},{3,4},{4,5},{5,6},{6,7},{7,8},{8,9},{9,10},{10,1... | collective-permute-start | bytes 9224 | tf_op jit(solution)/shard_map/ppermute | solution.py:474
  34.1 0.0 collective-permute-done.3.far_ids
  34.1 0.0 copy-start.10
  34.2 1.1 collective-permute-done.4.near_ids
  35.3 0.0 copy-start.11
  35.3 0.0 collective-permute-done.1.near_a
  35.3 0.0 collective-permute-done.2.near_b
  35.3 0.0 copy-done.8
  35.3 0.0 copy-done.10
  35.3 0.6 copy-done.11
  35.9 0.3 copy-done.9
  36.2 40.9 %attention.1 = (bf16[768,512]{1,0:T(8,128)(2,1)}, bf16[4,2304,256]{2,1,0:T(8,128)(2,1)}, bf16[8,128,768]{2,1,0:T(8,128)(2,1)}, bf16[10,512,128]{2,1,0:T(8,128)(2,1)}, bf16[10,512,128]{2,1,0:T(8,128)(2,1)}) custom-call(s32[1]{0:T(128)} %bitcast.core, bf16[768,512]{1,0:T(8,128)(2,1)} %relay.1.far, bf16[768,512]{1,0:T(8,128)(2,1)} %copy-done.9, ...), custom_call_target="tpu_custom_call" | custom-call | flops 20000000000 | bytes 25165824 | tf_op jit(solution)/shard_map/attention/pallas_call | solution.py:334
  77.0 0.7 collective-permute-start.7
  77.7 2.9 %collective-permute-done.7.arrived = bf16[10,512,128]{2,1,0:T(8,128)(2,1)S(1)} collective-permute-done((bf16[10,512,128]{2,1,0:T(8,128)(2,1)}, bf16[10,512,128]{2,1,0:T(8,128)(2,1)S(1)}, u32[]{:S(2)}, u32[]{:S(2)}) %collective-permute-start.7) | collective-permute-done | bytes 1310752 | tf_op jit(solution)/shard_map/ppermute | solution.py:498
  80.6 1.1 copy-done.4
  81.7 3.2 %pair_sum.1 = bf16[10,512,128]{2,1,0:T(8,128)(2,1)} custom-call(bf16[10,512,128]{2,1,0:T(8,128)(2,1)} %get-tuple-element.30.mine, bf16[10,512,128]{2,1,0:T(8,128)(2,1)} %copy-done.4), custom_call_target="tpu_custom_call" | custom-call | tf_op jit(solution)/shard_map/pair_sum/pallas_call | solution.py:389
  84.9 11.4 %all-to-all-start = ((bf16[64,80,128]{2,1,0:T(8,128)(2,1)}), bf16[64,80,128]{2,1,0:T(8,128)(2,1)S(1)}, u32[]{:S(2)}, u32[]{:S(2)}) async-start(bf16[64,80,128]{2,1,0:T(8,128)(2,1)} %bitcast.7), calls=%async_computation | async-start | bytes 2621440 | tf_op jit(solution)/shard_map/all_to_all | solution.py:500
  96.3 8.1 %projection_gradient.1 = (bf16[1536,512]{1,0:T(8,128)(2,1)}, f32[768,512]{1,0:T(8,128)}) custom-call(bf16[4,2304,256]{2,1,0:T(8,128)(2,1)} %get-tuple-element.26.grad_kv_pre, bf16[8,128,768]{2,1,0:T(8,128)(2,1)} %get-tuple-element.27.grad_uq_pre, bf16[512,2048]{1,0:T(8,128)(2,1)} %w_in.5), custom_call_target="tpu_custom_call" | custom-call | flops 3200000000 | bytes 14680064 | tf_op jit(solution)/shard_map/projection_gradient/pallas_call | solution.py:367
  104.4 2.1 %slice.7 = bf16[768,512]{1,0:T(8,128)(2,1)} slice(bf16[1536,512]{1,0:T(8,128)(2,1)} %get-tuple-element.29), slice={[768:1536], [0:512]} | slice | bytes 1572864 | tf_op jit(solution)/shard_map/slice | solution.py:502
  106.5 0.9 collective-permute-start.5
  107.4 2.1 %collective-permute-done.5.swapped = bf16[768,512]{1,0:T(8,128)(2,1)S(1)} collective-permute-done((bf16[768,512]{1,0:T(8,128)(2,1)}, bf16[768,512]{1,0:T(8,128)(2,1)S(1)}, u32[]{:S(2)}, u32[]{:S(2)}) %collective-permute-start.5) | collective-permute-done | bytes 786464 | tf_op jit(solution)/shard_map/ppermute | solution.py:502
  109.6 0.9 copy-done.2
  110.4 2.2 %add_convert_fusion.after = bf16[768,512]{1,0:T(8,128)(2,1)} fusion(bf16[768,512]{1,0:T(8,128)(2,1)S(1)} %collective-permute-done.5.swapped, bf16[1536,512]{1,0:T(8,128)(2,1)} %get-tuple-element.29, pred[]{:T(512)S(6)} %eq.3), kind=kLoop, calls=%fused_computation | loop fusion | flops 1966080 | bytes 2359297 | tf_op jit(solution)/shard_map/convert_element_type | solution.py:505
  112.7 1.4 all-to-all-done.parts
  114.1 1.1 copy-done
  115.2 2.6 %chip_sum.1 = bf16[64,80,128]{2,1,0:T(8,128)(2,1)} custom-call(bf16[64,80,128]{2,1,0:T(8,128)(2,1)} %copy-done, bf16[768,512]{1,0:T(8,128)(2,1)} %add_convert_fusion.after), custom_call_target="tpu_custom_call" | custom-call | tf_op jit(solution)/shard_map/chip_sum/pallas_call | solution.py:410
  117.8 0.0 copy-start.3
  117.8 25.7 %all_to_all.10 = bf16[64,80,128]{2,1,0:T(8,128)(2,1)S(1)} all-to-all(bf16[64,80,128]{2,1,0:T(8,128)(2,1)} %chip_sum.1), channel_id=1, replica_groups=mesh['z_hi'=2,'y'=4,'z_lo'=2,'x'=4,'core'=2] {'z_hi','y','z_lo','x'}, dimensions={0} | all-to-all | bytes 2621440 | tf_op jit(solution)/shard_map/all_to_all | solution.py:507
  143.5 3.1 %collective-permute-start.8 = (bf16[10,512,128]{2,1,0:T(8,128)(2,1)S(1)}, bf16[10,512,128]{2,1,0:T(8,128)(2,1)}, u32[]{:S(2)}, u32[]{:S(2)}) collective-permute-start(bf16[10,512,128]{2,1,0:T(8,128)(2,1)S(1)} %bitcast.5), channel_id=1, source_target_pairs={{0,1},{1,0},{2,3},{3,2},{4,5},{5,4},{6,7},{7,6},{8,9},{9,8},{10,11... | collective-permute-start | bytes 3932168 | tf_op jit(solution)/shard_map/ppermute | solution.py:509
  146.6 0.0 copy-done.3
  146.6 2.2 %collective-permute-start.6 = (bf16[768,512]{1,0:T(8,128)(2,1)S(1)}, bf16[768,512]{1,0:T(8,128)(2,1)S(1)}, u32[]{:S(2)}, u32[]{:S(2)}) collective-permute-start(bf16[768,512]{1,0:T(8,128)(2,1)S(1)} %copy-done.3), channel_id=1, source_target_pairs={{2,0},{3,1},{4,2},{5,3},{6,4},{7,5},{8,6},{9,7},{10,8},{11,9},{12,... | collective-permute-start | bytes 2359304 | tf_op jit(solution)/shard_map/ppermute | solution.py:474
  148.8 21.8 %collective-permute-done.6.sent = bf16[768,512]{1,0:T(8,128)(2,1)S(1)} collective-permute-done((bf16[768,512]{1,0:T(8,128)(2,1)S(1)}, bf16[768,512]{1,0:T(8,128)(2,1)S(1)}, u32[]{:S(2)}, u32[]{:S(2)}) %collective-permute-start.6) | collective-permute-done | bytes 786464 | tf_op jit(solution)/shard_map/ppermute | solution.py:474
  170.7 0.9 copy-done.6
  171.5 4.5 %input_norm_gradient.1 = bf16[768,512]{1,0:T(8,128)(2,1)} custom-call(bf16[768,512]{1,0:T(8,128)(2,1)} %tokens.5, f32[1,512]{1,0:T(1,128)} %bitcast.10, bf16[768,512]{1,0:T(8,128)(2,1)} %cotangent.3, f32[768,512]{1,0:T(8,128)} %get-tuple-element.28.grad_normed, bf16[768,512]{1,0:T(8,128)(2,1)} %copy-done.6, bf16[768,512]{1,0:T(8,128)(2,1)} %copy-done.2, ...), custom_call_target="tpu_custom_call" | custom-call | tf_op jit(solution)/shard_map/input_norm_gradient/pallas_call | solution.py:461
  176.0 0.0 copy-done.1
  176.0 0.0 collective-permute-done.8.second
  176.0 4.7 %unpack.1 = (f32[512,2048]{1,0:T(8,128)}, f32[512,512]{1,0:T(8,128)}) custom-call(s32[1]{0:T(128)} %bitcast.core, bf16[10,512,128]{2,1,0:T(8,128)(2,1)} %bitcast.6, bf16[10,512,128]{2,1,0:T(8,128)(2,1)} %collective-permute-done.8.second), custom_call_target="tpu_custom_call" | custom-call | tf_op jit(solution)/shard_map/unpack/pallas_call | solution.py:434
  (8 shorter events, 0.0 us)
Async XLA Ops:
  0.6 20.5 %collective-permute-start = (bf16[768,512]{1,0:T(8,128)(2,1)}, bf16[768,512]{1,0:T(8,128)(2,1)S(1)}, u32[]{:S(2)}, u32[]{:S(2)}) collective-permute-start(bf16[768,512]{1,0:T(8,128)(2,1)} %tokens.5), channel_id=1, source_target_pairs={{0,2},{1,3},{2,4},{3,5},{4,6},{5,7},{6,8},{7,9},{8,10},{9,11},{10,... | collective-permute-start | bytes 2359304 | tf_op jit(solution)/shard_map/ppermute | solution.py:474
  3.3 32.0 %collective-permute-start.1 = (bf16[768,512]{1,0:T(8,128)(2,1)}, bf16[768,512]{1,0:T(8,128)(2,1)S(1)}, u32[]{:S(2)}, u32[]{:S(2)}) collective-permute-start(bf16[768,512]{1,0:T(8,128)(2,1)} %tokens.5), channel_id=1, source_target_pairs={{0,1},{2,3},{4,5},{6,7},{8,9},{10,11},{12,13},{14,15},{16,17},{18,... | collective-permute-start | bytes 2359304 | tf_op jit(solution)/shard_map/ppermute | solution.py:486
  21.1 0.9 copy-start.5
  22.0 4.5 %copy-start.7 = (s32[768]{0:T(1024)S(1)}, s32[768]{0:T(1024)}, u32[]{:S(2)}) copy-start(s32[768]{0:T(1024)} %param.8) | copy-start | bytes 9220
  22.0 13.2 %collective-permute-start.2 = (bf16[768,512]{1,0:T(8,128)(2,1)}, bf16[768,512]{1,0:T(8,128)(2,1)}, u32[]{:S(2)}, u32[]{:S(2)}) collective-permute-start(bf16[768,512]{1,0:T(8,128)(2,1)} %relay.1.far), channel_id=1, source_target_pairs={{1,0},{3,2},{5,4},{7,6},{9,8},{11,10},{13,12},{15,14},{17,16},{19,... | collective-permute-start | bytes 2359304 | tf_op jit(solution)/shard_map/ppermute | solution.py:491
  26.5 8.8 %copy-start.8 = (s32[1,768]{1,0:T(1,128)}, s32[1,768]{1,0:T(1,128)S(1)}, u32[]{:S(2)}) copy-start(s32[1,768]{1,0:T(1,128)S(1)} %reshape.29.own_ids) | copy-start | bytes 9220
  26.5 7.6 %collective-permute-start.3 = (s32[1,768]{1,0:T(1,128)S(1)}, s32[1,768]{1,0:T(1,128)S(1)}, u32[]{:S(2)}, u32[]{:S(2)}) collective-permute-start(s32[1,768]{1,0:T(1,128)S(1)} %reshape.29.own_ids), channel_id=1, source_target_pairs={{0,2},{1,3},{2,4},{3,5},{4,6},{5,7},{6,8},{7,9},{8,10},{9,11},{10,... | collective-permute-start | bytes 9224 | tf_op jit(solution)/shard_map/ppermute | solution.py:474
  32.2 3.1 %collective-permute-start.4 = (s32[1,768]{1,0:T(1,128)S(1)}, s32[1,768]{1,0:T(1,128)S(1)}, u32[]{:S(2)}, u32[]{:S(2)}) collective-permute-start(s32[1,768]{1,0:T(1,128)S(1)} %reshape.29.own_ids), channel_id=1, source_target_pairs={{0,1},{1,2},{2,3},{3,4},{4,5},{5,6},{6,7},{7,8},{8,9},{9,10},{10,1... | collective-permute-start | bytes 9224 | tf_op jit(solution)/shard_map/ppermute | solution.py:474
  34.1 1.1 copy-start.10
  35.3 0.6 copy-start.11
  35.3 0.9 copy-start.9
  77.0 3.6 %collective-permute-start.7 = (bf16[10,512,128]{2,1,0:T(8,128)(2,1)}, bf16[10,512,128]{2,1,0:T(8,128)(2,1)S(1)}, u32[]{:S(2)}, u32[]{:S(2)}) collective-permute-start(bf16[10,512,128]{2,1,0:T(8,128)(2,1)} %get-tuple-element.31), channel_id=1, source_target_pairs={{0,1},{1,0},{2,3},{3,2},{4,5},{5,4},{6,7},{7,6},{8,9},{9,8},{10,11... | collective-permute-start | bytes 3932168 | tf_op jit(solution)/shard_map/ppermute | solution.py:498
  80.6 1.1 copy-start.4
  84.9 29.2 %all-to-all-start = ((bf16[64,80,128]{2,1,0:T(8,128)(2,1)}), bf16[64,80,128]{2,1,0:T(8,128)(2,1)S(1)}, u32[]{:S(2)}, u32[]{:S(2)}) async-start(bf16[64,80,128]{2,1,0:T(8,128)(2,1)} %bitcast.7), calls=%async_computation | async-start | bytes 2621440 | tf_op jit(solution)/shard_map/all_to_all | solution.py:500
  106.5 3.1 %collective-permute-start.5 = (bf16[768,512]{1,0:T(8,128)(2,1)}, bf16[768,512]{1,0:T(8,128)(2,1)S(1)}, u32[]{:S(2)}, u32[]{:S(2)}) collective-permute-start(bf16[768,512]{1,0:T(8,128)(2,1)} %slice.7), channel_id=1, source_target_pairs={{0,1},{1,0},{2,3},{3,2},{4,5},{5,4},{6,7},{7,6},{8,9},{9,8},{10,11... | collective-permute-start | bytes 2359304 | tf_op jit(solution)/shard_map/ppermute | solution.py:502
  109.6 0.9 copy-start.2
  114.1 1.1 copy-start
  117.8 28.8 %copy-start.3 = (bf16[768,512]{1,0:T(8,128)(2,1)S(1)}, bf16[768,512]{1,0:T(8,128)(2,1)}, u32[]{:S(2)}) copy-start(bf16[768,512]{1,0:T(8,128)(2,1)} %add_convert_fusion.after) | copy-start | bytes 2359300
  143.5 32.5 %copy-start.1 = (bf16[64,80,128]{2,1,0:T(8,128)(2,1)}, bf16[64,80,128]{2,1,0:T(8,128)(2,1)S(1)}, u32[]{:S(2)}) copy-start(bf16[64,80,128]{2,1,0:T(8,128)(2,1)S(1)} %all_to_all.10) | copy-start | bytes 3932164
  143.5 32.5 %collective-permute-start.8 = (bf16[10,512,128]{2,1,0:T(8,128)(2,1)S(1)}, bf16[10,512,128]{2,1,0:T(8,128)(2,1)}, u32[]{:S(2)}, u32[]{:S(2)}) collective-permute-start(bf16[10,512,128]{2,1,0:T(8,128)(2,1)S(1)} %bitcast.5), channel_id=1, source_target_pairs={{0,1},{1,0},{2,3},{3,2},{4,5},{5,4},{6,7},{7,6},{8,9},{9,8},{10,11... | collective-permute-start | bytes 3932168 | tf_op jit(solution)/shard_map/ppermute | solution.py:509
  146.6 24.1 %collective-permute-start.6 = (bf16[768,512]{1,0:T(8,128)(2,1)S(1)}, bf16[768,512]{1,0:T(8,128)(2,1)S(1)}, u32[]{:S(2)}, u32[]{:S(2)}) collective-permute-start(bf16[768,512]{1,0:T(8,128)(2,1)S(1)} %copy-done.3), channel_id=1, source_target_pairs={{2,0},{3,1},{4,2},{5,3},{6,4},{7,5},{8,6},{9,7},{10,8},{11,9},{12,... | collective-permute-start | bytes 2359304 | tf_op jit(solution)/shard_map/ppermute | solution.py:474
  170.7 0.9 copy-start.6

commit v4 on v3

--- a/solution.py
+++ b/solution.py
@@ -74,11 +74,10 @@
             columns = pl.ds((2 + part) * WIDTH + pair * PAIR, PAIR)
             silu, slope = silu_and_slope(dot(normed, w_in[:, columns]))
             silu = silu.astype(bf16)
-            slope = slope.astype(bf16)
+            kv_slope[part, rows, pl.ds(pair * PAIR, PAIR)] = slope.astype(bf16)
             for which in range(2):
                 head = 2 * pair + which
                 lanes = slice(which * HEAD_DIM, (which + 1) * HEAD_DIM)
-                kv_slope[head, rows, pl.ds(part * HEAD_DIM, HEAD_DIM)] = slope[:, lanes]
                 kv[part * HEADS + head, rows, :] = silu[:, lanes]
                 kv_t[part * HEADS + head, :, rows] = silu[:, lanes].T
 
@@ -109,7 +108,7 @@
         (WIDTH, rows),
         (2 * HEADS, rows, HEAD_DIM),
         (2 * HEADS, HEAD_DIM, rows),
-        (HEADS, rows, PAIR),
+        (2, rows, WIDTH),
     )
 
 
@@ -128,25 +127,37 @@
     )(*operands)
 
 
-def relay_kernel(far, after, passed):
-    del far, after, passed
-
-
-def relay_call(far, after):
+def relay_kernel(*refs):
+    del refs
+
+
+def slow_relay_call(far, *after):
     return pl.pallas_call(
         relay_kernel,
-        in_specs=[ANY, ANY],
+        in_specs=[ANY] * (1 + len(after)),
+        out_specs=ANY,
+        out_shape=jax.ShapeDtypeStruct(far.shape, far.dtype),
+        input_output_aliases={0: 0},
+        cost_estimate=pl.CostEstimate(flops=10*10**9, bytes_accessed=0, transcendentals=0),
+        name='relay_home',
+    )(far, *after)
+
+
+def relay_call(far, *after):
+    return pl.pallas_call(
+        relay_kernel,
+        in_specs=[ANY] * (1 + len(after)),
         out_specs=ANY,
         out_shape=jax.ShapeDtypeStruct(far.shape, far.dtype),
         input_output_aliases={0: 0},
         name="relay",
-    )(far, after)
+    )(far, *after)
 
 
 def main_kernel(
     core, far, near_a, near_b, own_normed_t, own_kv, own_kv_t, own_kv_slope, own_uq_slope_t,
     uq_t, tokens, in_gain, out_gain, w_in, w_out, cotangent, far_ids, near_ids, own_ids,
-    layer_out, grad_kv_pre, grad_uq_pre, mine, theirs,
+    layer_out, grad_kv_pre, grad_uq_pre, far_grad, near_grad, mine, theirs,
     normed_t, kv, kv_t, kv_slope, uq_slope_t, mask, weights, slopes, mixed_t, grad_attn_t, gated_t, both, sems,
 ):
     own = pl.ds(HALO, ROWS)
@@ -266,6 +277,7 @@
         put(blocks, dot_nt(normed_t[:, own], uq_slope_t[pl.ds(2 * pair, 2)].reshape(PAIR, ROWS)))
 
     def backward(head, carry):
+        columns = pl.ds(pl.multiple_of(head * HEAD_DIM, HEAD_DIM), HEAD_DIM)
         for (key_tile, tile), place in PLACE.items():
             band = pl.ds(place, TILE)
             grad_weights = dot(
@@ -279,14 +291,10 @@
             queries = pl.ds(span[0] * TILE, len(span) * TILE)
             grad_keys = dot_nt(slopes[head, :, band], uq_t[HEADS + head, :, queries])
             grad_values = dot_nt(weights[head, :, band], grad_attn_t[head, :, queries])
-            slope = kv_slope[head, rows, :].astype(f32)
-            kv_slope[head, rows, :] = jnp.concatenate(
-                [
-                    (grad_keys * slope[:, :HEAD_DIM] * HALF_SCALE).astype(bf16),
-                    (grad_values * slope[:, HEAD_DIM:]).astype(bf16),
-                ],
-                axis=1,
-            )
+            slope = kv_slope[0, rows, columns].astype(f32)
+            kv_slope[0, rows, columns] = (grad_keys * slope * HALF_SCALE).astype(bf16)
+            slope = kv_slope[1, rows, columns].astype(f32)
+            kv_slope[1, rows, columns] = (grad_values * slope).astype(bf16)
         for tile in range(TILES):
             total = None
             for key_tile in range(tile, tile + SPREAD):
@@ -298,22 +306,44 @@
             queries = pl.ds(tile * TILE, TILE)
             slope = uq_slope_t[HEADS + head, :, queries].astype(f32)
             uq_slope_t[HEADS + head, :, queries] = (total * slope * HALF_SCALE).astype(bf16)
-        put((2 * HEADS + head, 3 * HEADS + head), dot(normed_t[...], kv_slope[head]))
         return carry
 
     lax.fori_loop(0, HEADS, backward, 0)
-    for pair in range(HEADS // 2):
-        queries = uq_slope_t[pl.ds(HEADS + 2 * pair, 2)].reshape(PAIR, ROWS)
-        put((HEADS + 2 * pair, HEADS + 2 * pair + 1), dot_nt(normed_t[:, own], queries))
+
+    departures = []
+    for tile in range(2 * TILES):
+        rows = pl.ds(tile * TILE, TILE)
+        total = sum(
+            dot_nt(kv_slope[part, rows, :], w_in[:, pl.ds((2 + part) * WIDTH, WIDTH)]) for part in range(2)
+        )
+        slot, at = divmod(tile, TILES)
+        staged(slot, at)[...] = total.astype(bf16)
+        target = (far_grad, near_grad)[slot].at[pl.ds(at * TILE, TILE)]
+        departures.append(pltpu.make_async_copy(staged(slot, at), target, sems.at[tile]))
+        departures[-1].start()
     results = [
-        pltpu.make_async_copy(source, target, sems.at[at])
+        pltpu.make_async_copy(source, target, sems.at[len(departures) + at])
         for at, (source, target) in enumerate(
-            ((both.at[1], theirs), (both.at[0], mine), (kv_slope, grad_kv_pre), (uq_slope_t, grad_uq_pre))
+            (
+                (kv_slope.at[:, own, :], grad_kv_pre),
+                (uq_slope_t, grad_uq_pre),
+                (both.at[1], theirs),
+                (both.at[0], mine),
+            )
         )
     ]
-    for copy in results:
-        copy.start()
-    for copy in results:
+    results[0].start()
+    results[1].start()
+    for pair in range(HEADS // 2):
+        blocks = (2 * pair, 2 * pair + 1)
+        queries = uq_slope_t[pl.ds(HEADS + 2 * pair, 2)].reshape(PAIR, ROWS)
+        put([HEADS + block for block in blocks], dot_nt(normed_t[:, own], queries))
+        for part in range(2):
+            columns = pl.ds(pair * PAIR, PAIR)
+            put([(2 + part) * HEADS + block for block in blocks], dot(normed_t[...], kv_slope[part, :, columns]))
+    results[2].start()
+    results[3].start()
+    for copy in departures + results:
         copy.wait()
 
 
@@ -334,10 +364,10 @@
     return pl.pallas_call(
         main_kernel,
         in_specs=[SMEM] + [ANY] * 8 + [VMEM] * (len(operands) - 9),
-        out_specs=[VMEM] + [ANY] * 2 + [HBM] * 2,
+        out_specs=[VMEM] + [ANY] * 6,
         out_shape=[
             jax.ShapeDtypeStruct(shape, bf16)
-            for shape in ((ROWS, WIDTH), (HEADS, WINDOW_ROWS, PAIR), along, half, half)
+            for shape in ((ROWS, WIDTH), (2, ROWS, WIDTH), along, (ROWS, WIDTH), (ROWS, WIDTH), half, half)
         ],
         scratch_shapes=scratch,
         compiler_params=pltpu.CompilerParams(vmem_limit_bytes=62 * MIB),
@@ -346,55 +376,40 @@
     )(*operands)
 
 
-def back_kernel(grad_kv_pre, grad_uq_pre, w_in, halo_grad, grad_normed):
-    halo = pl.ds(0, HALO)
-    own = pl.ds(HALO, ROWS)
-
-    def along(rows):
-        total = None
-        for head in range(HEADS):
-            w_pair = [w_in[:, pl.ds((2 + part) * WIDTH + head * HEAD_DIM, HEAD_DIM)] for part in range(2)]
-            term = dot_nt(grad_kv_pre[head, rows, :], jnp.concatenate(w_pair, axis=1))
-            total = term if total is None else total + term
-        return total
-
-    halo_grad[...] = along(halo).astype(bf16)
+def back_kernel(grad_kv_pre, grad_uq_pre, w_in, after, grad_normed):
+    del after
     across = dot(w_in[:, pl.ds(0, 2 * WIDTH)], grad_uq_pre[...].reshape(2 * WIDTH, ROWS))
-    grad_normed[...] = across.T + along(own)
+    along = sum(dot_nt(grad_kv_pre[part], w_in[:, pl.ds((2 + part) * WIDTH, WIDTH)]) for part in range(2))
+    grad_normed[...] = across.T + along
 
 
 def back_call(*operands):
     return pl.pallas_call(
         back_kernel,
-        in_specs=[VMEM] * len(operands),
-        out_specs=[VMEM] * 2,
-        out_shape=(
-            jax.ShapeDtypeStruct((HALO, WIDTH), bf16),
-            jax.ShapeDtypeStruct((ROWS, WIDTH), f32),
-        ),
-        compiler_params=pltpu.CompilerParams(vmem_limit_bytes=62 * MIB),
-        cost_estimate=pl.CostEstimate(flops=32 * 10**8, bytes_accessed=14 * MIB, transcendentals=0),
+        in_specs=[VMEM] * 3 + [ANY],
+        out_specs=VMEM,
+        out_shape=jax.ShapeDtypeStruct((ROWS, WIDTH), f32),
+        compiler_params=pltpu.CompilerParams(vmem_limit_bytes=24 * MIB),
+        cost_estimate=pl.CostEstimate(flops=16 * 10**8, bytes_accessed=8 * MIB, transcendentals=0),
         name="projection_gradient",
     )(*operands)
 
 
-def pair_kernel(mine, arrived, total, staging, sem):
-    staging[...] = (mine[...].astype(f32) + arrived[...].astype(f32)).astype(bf16)
-    copy = pltpu.make_async_copy(staging, total, sem)
-    copy.start()
-    copy.wait()
-
-
-def pair_call(mine, arrived):
+def pair_kernel(core, mine, arrived, far_grad, swapped, total, outgoing):
+    total[...] = (mine[...].astype(f32) + arrived[...].astype(f32)).astype(bf16)
+    near = jnp.where(core[0] == 1, swapped[...].astype(f32), 0.0)
+    outgoing[...] = (far_grad[...].astype(f32) + near).astype(bf16)
+
+
+def pair_call(core, mine, arrived, far_grad, swapped):
     return pl.pallas_call(
         pair_kernel,
-        in_specs=[VMEM] * 2,
-        out_specs=HBM,
-        out_shape=jax.ShapeDtypeStruct(mine.shape, bf16),
-        scratch_shapes=[pltpu.VMEM(mine.shape, bf16), pltpu.SemaphoreType.DMA],
-        compiler_params=pltpu.CompilerParams(vmem_limit_bytes=62 * MIB),
+        in_specs=[SMEM] + [VMEM] * 4,
+        out_specs=[VMEM] * 2,
+        out_shape=[jax.ShapeDtypeStruct(like.shape, bf16) for like in (mine, far_grad)],
+        compiler_params=pltpu.CompilerParams(vmem_limit_bytes=24 * MIB),
         name="pair_sum",
-    )(mine, arrived)
+    )(core, mine, arrived, far_grad, swapped)
 
 
 def chips_kernel(parts, after, totals, staging, sem):
@@ -439,7 +454,7 @@
             jax.ShapeDtypeStruct((WIDTH, 4 * WIDTH), f32),
             jax.ShapeDtypeStruct((WIDTH, WIDTH), f32),
         ),
-        compiler_params=pltpu.CompilerParams(vmem_limit_bytes=62 * MIB),
+        compiler_params=pltpu.CompilerParams(vmem_limit_bytes=24 * MIB),
         name="unpack",
     )(core, first, second)
 
@@ -456,16 +471,15 @@
     ).astype(bf16)
 
 
-def step_call(tokens, in_gain, cotangent, grad_normed, sent, swapped, core):
-    vmem = pl.BlockSpec(memory_space=pltpu.VMEM)
+def step_call(*operands):
     return pl.pallas_call(
         step_kernel,
-        in_specs=[vmem] * 6 + [pl.BlockSpec(memory_space=pltpu.SMEM)],
-        out_specs=vmem,
+        in_specs=[VMEM] * 6 + [SMEM],
+        out_specs=VMEM,
         out_shape=jax.ShapeDtypeStruct((ROWS, WIDTH), bf16),
-        compiler_params=pltpu.CompilerParams(vmem_limit_bytes=62 * MIB),
+        compiler_params=pltpu.CompilerParams(vmem_limit_bytes=24 * MIB),
         name="input_norm_gradient",
-    )(tokens, in_gain, cotangent, grad_normed, sent, swapped, core)
+    )(*operands)
 
 
 def shifted(value, steps):
@@ -487,27 +501,25 @@
     far_ids = shifted(own_ids, 2)
     near_ids = shifted(own_ids, 1)
     *window, uq_t, uq_slope_t = own_call(tokens, in_gain_row, w_in)
-    far = relay_call(far, uq_t)
+    far = relay_call(far, uq_t, far_ids, near_ids)
     near_b = lax.ppermute(far, "core", [(1, 0)])
-    layer_out, grad_kv_pre, grad_uq_pre, mine, theirs = main_call(
+    layer_out, grad_kv_pre, grad_uq_pre, far_grad, near_grad, mine, theirs = main_call(
         core, far, near_a, near_b, *window, uq_slope_t,
         uq_t, tokens, in_gain_row, out_gain.reshape(1, WIDTH), w_in, w_out, cotangent,
         far_ids, near_ids, own_ids,
     )
 
     arrived = lax.ppermute(theirs, "core", SWAP)
-    partial = pair_call(mine, arrived).reshape(64, 80, HEAD_DIM)
-    parts = lax.all_to_all(partial, CHIPS, 0, 0, tiled=True)
-    halo_grad, grad_normed = back_call(grad_kv_pre, grad_uq_pre, w_in)
-    swapped = lax.ppermute(halo_grad[ROWS:], "core", SWAP)
-    outgoing = (
-        halo_grad[:ROWS].astype(f32) + jnp.where(core[0] == 1, swapped.astype(f32), 0.0)
-    ).astype(bf16)
-    sent = shifted(outgoing, -2)
-    totals = lax.all_to_all(chips_call(parts, outgoing), CHIPS, 0, 0, tiled=True)
-    totals = totals.reshape(HALF_BLOCKS, WIDTH, HEAD_DIM)
+    swapped = lax.ppermute(near_grad, "core", SWAP)
+    partial, outgoing = pair_call(core, mine, arrived, far_grad, swapped)
+    sent = slow_relay_call(shifted(outgoing, -2))
+    grad_normed = back_call(grad_kv_pre, grad_uq_pre, w_in, outgoing)
+    parts = lax.all_to_all(partial.reshape(64, 80, HEAD_DIM), CHIPS, 0, 0, tiled=True)
+    total = chips_call(parts, grad_normed)
+    totals = lax.all_to_all(total, CHIPS, 0, 0, tiled=True)
+    grad_tokens = step_call(tokens, in_gain_row, cotangent, grad_normed, sent, swapped, core)
+    totals = relay_call(totals.reshape(HALF_BLOCKS, WIDTH, HEAD_DIM), grad_tokens)
     other = lax.ppermute(totals, "core", SWAP)
-    grad_tokens = step_call(tokens, in_gain_row, cotangent, grad_normed, sent, swapped, core)
     grad_w_in, grad_w_out = unpack_call(core, totals, other)
     return (layer_out, grad_tokens, grad_w_in, grad_w_out)
 

time: 183 us -> 162 us (0.89)
  the two profiles are of different devices: /device:TPU:39 before, /device:TPU:1 now
where the time goes in v4:
time: 162 us; the launch traced here: 161 us
  Pallas kernels  60.9 us (38%)
  starting transfers between devices  52.6 us (32%)
  waiting for transfers between devices  30.7 us (19%)
  local copies, waits for them, and re-layouts  16 us (10%)
    pallas_call x1, Pallas kernels, main_call(): pl.pallas_call(main_kernel, in_specs=[SMEM] + [ANY] * 8 + [VMEM] * (len(o...  40.4 us
    ppermute x1, starting transfers between devices, on_device(): other = lax.ppermute(totals, 'core', SWAP)  17.5 us
    unnamed x42, local copies, waits for them, and re-layouts  15.3 us
    all_to_all x1, waiting for transfers between devices, on_device(): lax.all_to_all(partial.reshape(64, 80, HEAD_DIM), CHIPS, 0, 0, tiled=True)  13.7 us
    all_to_all x1, starting transfers between devices, on_device(): lax.all_to_all(partial.reshape(64, 80, HEAD_DIM), CHIPS, 0, 0, tiled=True)  12.5 us
    ppermute x4, starting transfers between devices, shifted(): lax.ppermute(value, ALL, [(source, source + steps) for source in range(fi...  12 us
    pallas_call x1, Pallas kernels, own_call(): pl.pallas_call(own_kernel, in_specs=[VMEM] * len(operands), out_specs=[VM...  8.18 us
    all_to_all x1, waiting for transfers between devices, on_device(): totals = lax.all_to_all(total, CHIPS, 0, 0, tiled=True)  6.39 us
  transfers between devices with their start and end apart: 11, of which 6 were waited for; matrix products, arithmetic and copies ran while one was open for 0% of the time, Pallas kernels for 10%

profile of v4, /device:TPU:1, one launch (start us, length us, event | category | flops | bytes accessed | tf_op | source)
XLA Modules:
  0.0 161.1 jit_solution(11055766123534257749)
XLA Ops:
  0.6 4.0 %collective-permute-start = (bf16[768,512]{1,0:T(8,128)(2,1)}, bf16[768,512]{1,0:T(8,128)(2,1)S(1)}, u32[]{:S(2)}, u32[]{:S(2)}) collective-permute-start(bf16[768,512]{1,0:T(8,128)(2,1)} %tokens.5), channel_id=1, source_target_pairs={{0,2},{1,3},{2,4},{3,5},{4,6},{5,7},{6,8},{7,9},{8,10},{9,11},{10,... | collective-permute-start | bytes 2359304 | tf_op jit(solution)/shard_map/ppermute | solution.py:488
  4.6 0.7 reshape.28.own_ids
  5.3 3.9 %collective-permute-start.2 = (s32[1,768]{1,0:T(1,128)S(1)}, s32[1,768]{1,0:T(1,128)S(1)}, u32[]{:S(2)}, u32[]{:S(2)}) collective-permute-start(s32[1,768]{1,0:T(1,128)S(1)} %reshape.28.own_ids), channel_id=1, source_target_pairs={{0,1},{1,2},{2,3},{3,4},{4,5},{5,6},{6,7},{7,8},{8,9},{9,10},{10,1... | collective-permute-start | bytes 9224 | tf_op jit(solution)/shard_map/ppermute | solution.py:488
  9.2 2.8 %collective-permute-start.1 = (s32[1,768]{1,0:T(1,128)S(1)}, s32[1,768]{1,0:T(1,128)S(1)}, u32[]{:S(2)}, u32[]{:S(2)}) collective-permute-start(s32[1,768]{1,0:T(1,128)S(1)} %reshape.28.own_ids), channel_id=1, source_target_pairs={{0,2},{1,3},{2,4},{3,5},{4,6},{5,7},{6,8},{7,9},{8,10},{9,11},{10,... | collective-permute-start | bytes 9224 | tf_op jit(solution)/shard_map/ppermute | solution.py:488
  12.1 1.3 collective-permute-start.3
  13.4 8.2 %own_projection.1 = (bf16[512,768]{1,0:T(8,128)(2,1)}, bf16[8,768,128]{2,1,0:T(8,128)(2,1)}, bf16[8,128,768]{2,1,0:T(8,128)(2,1)}, bf16[2,768,512]{2,1,0:T(8,128...) custom-call(bf16[768,512]{1,0:T(8,128)(2,1)} %tokens.5, f32[1,512]{1,0:T(1,128)} %bitcast.6, ...), custom_call_target="tpu_custom_call" | custom-call | flops 1610612736 | bytes 12582912 | tf_op jit(solution)/shard_map/own_projection/pallas_call | solution.py:117
  21.5 0.0 collective-permute-done.2.refs_3_.near_ids
  21.6 0.0 collective-permute-done.1.refs_2_.far_ids
  21.6 0.0 copy-start.15
  21.6 0.5 copy-done.17
  22.1 0.0 copy-done.18
  22.2 0.3 copy-done.15
  22.5 3.1 %collective-permute-start.4 = (bf16[768,512]{1,0:T(8,128)(2,1)}, bf16[768,512]{1,0:T(8,128)(2,1)S(1)}, u32[]{:S(2)}, u32[]{:S(2)}) collective-permute-start(bf16[768,512]{1,0:T(8,128)(2,1)} %relay.2.far), channel_id=1, source_target_pairs={{1,0},{3,2},{5,4},{7,6},{9,8},{11,10},{13,12},{15,14},{17,16},{19,... | collective-permute-start | bytes 2359304 | tf_op jit(solution)/shard_map/ppermute | solution.py:505
  25.6 0.0 collective-permute-done.3.near_a
  25.6 2.0 %collective-permute-done.4.near_b = bf16[768,512]{1,0:T(8,128)(2,1)S(1)} collective-permute-done((bf16[768,512]{1,0:T(8,128)(2,1)}, bf16[768,512]{1,0:T(8,128)(2,1)S(1)}, u32[]{:S(2)}, u32[]{:S(2)}) %collective-permute-start.4) | collective-permute-done | bytes 786464 | tf_op jit(solution)/shard_map/ppermute | solution.py:505
  27.7 0.9 copy-done.20
  28.5 40.4 %attention.1 = (bf16[768,512]{1,0:T(8,128)(2,1)}, bf16[2,768,512]{2,1,0:T(8,128)(2,1)}, bf16[8,128,768]{2,1,0:T(8,128)(2,1)}, bf16[768,512]{1,0:T(8,128)(2,1)}, ...) custom-call(s32[1]{0:T(128)} %bitcast.core, bf16[768,512]{1,0:T(8,128)(2,1)} %relay.2.far, ...), custom_call_target="tpu_custom_call" | custom-call | flops 20000000000 | bytes 25165824 | tf_op jit(solution)/shard_map/attention/pallas_call | solution.py:364
  68.9 0.5 collective-permute-start.5
  69.4 0.3 collective-permute-start.6
  69.7 3.7 %collective-permute-done.6.swapped = bf16[768,512]{1,0:T(8,128)(2,1)S(1)} collective-permute-done((bf16[768,512]{1,0:T(8,128)(2,1)}, bf16[768,512]{1,0:T(8,128)(2,1)S(1)}, u32[]{:S(2)}, u32[]{:S(2)}) %collective-permute-start.6) | collective-permute-done | bytes 786464 | tf_op jit(solution)/shard_map/ppermute | solution.py:513
  73.4 0.0 collective-permute-done.5.arrived
  73.4 1.6 copy-done.9
  75.0 1.1 copy-done.10
  76.1 1.6 pair_sum.1
  77.8 12.5 %all-to-all-start = ((bf16[64,80,128]{2,1,0:T(8,128)(2,1)}), bf16[64,80,128]{2,1,0:T(8,128)(2,1)S(1)}, u32[]{:S(2)}, u32[]{:S(2)}) async-start(bf16[64,80,128]{2,1,0:T(8,128)(2,1)} %bitcast.3), calls=%async_computation | async-start | bytes 2621440 | tf_op jit(solution)/shard_map/all_to_all | solution.py:517
  90.3 1.3 collective-permute-start.7
  91.6 1.4 copy-done.7
  93.0 1.4 copy-done.8
  94.4 1.8 %projection_gradient.1.grad_normed.after = f32[768,512]{1,0:T(8,128)S(1)} custom-call(bf16[2,768,512]{2,1,0:T(8,128)(2,1)S(1)} %copy-done.7, bf16[8,128,768]{2,1,0:T(8,128)(2,1)S(1)} %copy-done.8, bf16[512,2048]{1,0:T(8,128)(2,1)S(1)} %copy-done.6, bf16[768,512]{1,0:T(8,128)(2,1)} %get-tuple-element.34.after), custom_call_target="tpu_custom_call" | custom-call | flops 1600000000 | bytes 8388608 | tf_op jit(solution)/shard_map/projection_gradient/pallas_call | solution.py:387
  96.2 0.0 copy-start
  96.2 1.1 copy-done
  97.4 13.7 %all-to-all-done.parts = bf16[64,80,128]{2,1,0:T(8,128)(2,1)S(1)} async-done(((bf16[64,80,128]{2,1,0:T(8,128)(2,1)}), bf16[64,80,128]{2,1,0:T(8,128)(2,1)S(1)}, u32[]{:S(2)}, u32[]{:S(2)}) %all-to-all-start) | async-done | bytes 1310752 | tf_op jit(solution)/shard_map/all_to_all | solution.py:517
  111.0 1.1 copy-done.14
  112.1 2.6 %chip_sum.1 = bf16[64,80,128]{2,1,0:T(8,128)(2,1)} custom-call(bf16[64,80,128]{2,1,0:T(8,128)(2,1)} %copy-done.14, f32[768,512]{1,0:T(8,128)} %copy-done), custom_call_target="tpu_custom_call" | custom-call | tf_op jit(solution)/shard_map/chip_sum/pallas_call | solution.py:425
  114.7 5.4 %all-to-all-start.1 = ((bf16[64,80,128]{2,1,0:T(8,128)(2,1)}), bf16[64,80,128]{2,1,0:T(8,128)(2,1)S(1)}, u32[]{:S(2)}, u32[]{:S(2)}) async-start(bf16[64,80,128]{2,1,0:T(8,128)(2,1)} %chip_sum.1), calls=%async_computation.1 | async-start | bytes 2621440 | tf_op jit(solution)/shard_map/all_to_all | solution.py:519
  120.2 0.0 copy-start.1
  120.2 0.0 copy-start.13
  120.2 2.1 %collective-permute-done.7.refs_0_ = bf16[768,512]{1,0:T(8,128)(2,1)} collective-permute-done((bf16[768,512]{1,0:T(8,128)(2,1)}, bf16[768,512]{1,0:T(8,128)(2,1)}, u32[]{:S(2)}, u32[]{:S(2)}) %collective-permute-start.7) | collective-permute-done | bytes 786464 | tf_op jit(solution)/shard_map/ppermute | solution.py:488
  122.3 1.1 copy-done.5
  123.4 1.1 copy-done.11
  124.5 1.1 copy-done.12
  125.7 3.3 %input_norm_gradient.1.refs_1_ = bf16[768,512]{1,0:T(8,128)(2,1)} custom-call(bf16[768,512]{1,0:T(8,128)(2,1)S(1)} %copy-done.11, f32[1,512]{1,0:T(1,128)S(1)} %bitcast.8, bf16[768,512]{1,0:T(8,128)(2,1)S(1)} %copy-done.12, f32[768,512]{1,0:T(8,128)S(1)} %copy-done.1, bf16[768,512]{1,0:T(8,128)(2,1)} %relay_home.1.sent, bf16[768,512]{1,0:T(8,128)(2,1)S(1)} %copy-done.5, ...), custom_call_target="tpu_custom_call" | custom-call | tf_op jit(solution)/shard_map/input_norm_gradient/pallas_call | solution.py:475
  129.0 6.4 %all-to-all-done.1 = bf16[64,80,128]{2,1,0:T(8,128)(2,1)S(1)} async-done(((bf16[64,80,128]{2,1,0:T(8,128)(2,1)}), bf16[64,80,128]{2,1,0:T(8,128)(2,1)S(1)}, u32[]{:S(2)}, u32[]{:S(2)}) %all-to-all-start.1) | async-done | bytes 1310752 | tf_op jit(solution)/shard_map/all_to_all | solution.py:519
  135.3 1.1 copy-done.2
  136.4 17.5 %collective-permute-start.8 = (bf16[10,512,128]{2,1,0:T(8,128)(2,1)}, bf16[10,512,128]{2,1,0:T(8,128)(2,1)S(1)}, u32[]{:S(2)}, u32[]{:S(2)}) collective-permute-start(bf16[10,512,128]{2,1,0:T(8,128)(2,1)} %relay.3.first), channel_id=1, source_target_pairs={{0,1},{1,0},{2,3},{3,2},{4,5},{5,4},{6,7},{7,6},{8,9},{9,8},{10,11... | collective-permute-start | bytes 3932168 | tf_op jit(solution)/shard_map/ppermute | solution.py:522
  153.9 2.9 %collective-permute-done.8.second = bf16[10,512,128]{2,1,0:T(8,128)(2,1)S(1)} collective-permute-done((bf16[10,512,128]{2,1,0:T(8,128)(2,1)}, bf16[10,512,128]{2,1,0:T(8,128)(2,1)S(1)}, u32[]{:S(2)}, u32[]{:S(2)}) %collective-permute-start.8) | collective-permute-done | bytes 1310752 | tf_op jit(solution)/shard_map/ppermute | solution.py:522
  156.8 1.3 copy-done.3
  158.1 3.0 %unpack.1 = (f32[512,2048]{1,0:T(8,128)}, f32[512,512]{1,0:T(8,128)}) custom-call(s32[1]{0:T(128)} %bitcast.core, bf16[10,512,128]{2,1,0:T(8,128)(2,1)S(1)} %copy-done.3, bf16[10,512,128]{2,1,0:T(8,128)(2,1)S(1)} %collective-permute-done.8.second), custom_call_target="tpu_custom_call" | custom-call | tf_op jit(solution)/shard_map/unpack/pallas_call | solution.py:449
  (27 shorter events, 0.0 us)
Async XLA Ops:
  0.6 21.0 %collective-permute-start = (bf16[768,512]{1,0:T(8,128)(2,1)}, bf16[768,512]{1,0:T(8,128)(2,1)S(1)}, u32[]{:S(2)}, u32[]{:S(2)}) collective-permute-start(bf16[768,512]{1,0:T(8,128)(2,1)} %tokens.5), channel_id=1, source_target_pairs={{0,2},{1,3},{2,4},{3,5},{4,6},{5,7},{6,8},{7,9},{8,10},{9,11},{10,... | collective-permute-start | bytes 2359304 | tf_op jit(solution)/shard_map/ppermute | solution.py:488
  5.3 16.2 %copy-start.16 = (s32[1,768]{1,0:T(1,128)}, s32[1,768]{1,0:T(1,128)S(1)}, u32[]{:S(2)}) copy-start(s32[1,768]{1,0:T(1,128)S(1)} %reshape.28.own_ids) | copy-start | bytes 9220
  5.3 16.2 %collective-permute-start.2 = (s32[1,768]{1,0:T(1,128)S(1)}, s32[1,768]{1,0:T(1,128)S(1)}, u32[]{:S(2)}, u32[]{:S(2)}) collective-permute-start(s32[1,768]{1,0:T(1,128)S(1)} %reshape.28.own_ids), channel_id=1, source_target_pairs={{0,1},{1,2},{2,3},{3,4},{4,5},{5,6},{6,7},{7,8},{8,9},{9,10},{10,1... | collective-permute-start | bytes 9224 | tf_op jit(solution)/shard_map/ppermute | solution.py:488
  9.2 12.3 %collective-permute-start.1 = (s32[1,768]{1,0:T(1,128)S(1)}, s32[1,768]{1,0:T(1,128)S(1)}, u32[]{:S(2)}, u32[]{:S(2)}) collective-permute-start(s32[1,768]{1,0:T(1,128)S(1)} %reshape.28.own_ids), channel_id=1, source_target_pairs={{0,2},{1,3},{2,4},{3,5},{4,6},{5,7},{6,8},{7,9},{8,10},{9,11},{10,... | collective-permute-start | bytes 9224 | tf_op jit(solution)/shard_map/ppermute | solution.py:488
  12.1 13.5 %collective-permute-start.3 = (bf16[768,512]{1,0:T(8,128)(2,1)}, bf16[768,512]{1,0:T(8,128)(2,1)S(1)}, u32[]{:S(2)}, u32[]{:S(2)}) collective-permute-start(bf16[768,512]{1,0:T(8,128)(2,1)} %tokens.5), channel_id=1, source_target_pairs={{0,1},{2,3},{4,5},{6,7},{8,9},{10,11},{12,13},{14,15},{16,17},{18,... | collective-permute-start | bytes 2359304 | tf_op jit(solution)/shard_map/ppermute | solution.py:500
  21.6 0.6 copy-start.17
  21.6 0.6 copy-start.18
  21.6 0.9 copy-start.15
  22.5 5.2 %collective-permute-start.4 = (bf16[768,512]{1,0:T(8,128)(2,1)}, bf16[768,512]{1,0:T(8,128)(2,1)S(1)}, u32[]{:S(2)}, u32[]{:S(2)}) collective-permute-start(bf16[768,512]{1,0:T(8,128)(2,1)} %relay.2.far), channel_id=1, source_target_pairs={{1,0},{3,2},{5,4},{7,6},{9,8},{11,10},{13,12},{15,14},{17,16},{19,... | collective-permute-start | bytes 2359304 | tf_op jit(solution)/shard_map/ppermute | solution.py:505
  25.6 2.0 %copy-start.19 = (bf16[768,512]{1,0:T(8,128)(2,1)}, bf16[768,512]{1,0:T(8,128)(2,1)S(1)}, u32[]{:S(2)}) copy-start(bf16[768,512]{1,0:T(8,128)(2,1)S(1)} %collective-permute-done.3.near_a) | copy-start | bytes 2359300
  27.7 0.9 copy-start.20
  68.9 4.5 %collective-permute-start.5 = (bf16[10,512,128]{2,1,0:T(8,128)(2,1)}, bf16[10,512,128]{2,1,0:T(8,128)(2,1)S(1)}, u32[]{:S(2)}, u32[]{:S(2)}) collective-permute-start(bf16[10,512,128]{2,1,0:T(8,128)(2,1)} %get-tuple-element.31), channel_id=1, source_target_pairs={{0,1},{1,0},{2,3},{3,2},{4,5},{5,4},{6,7},{7,6},{8,9},{9,8},{10,11... | collective-permute-start | bytes 3932168 | tf_op jit(solution)/shard_map/ppermute | solution.py:512
  69.4 4.0 %collective-permute-start.6 = (bf16[768,512]{1,0:T(8,128)(2,1)}, bf16[768,512]{1,0:T(8,128)(2,1)S(1)}, u32[]{:S(2)}, u32[]{:S(2)}) collective-permute-start(bf16[768,512]{1,0:T(8,128)(2,1)} %get-tuple-element.33), channel_id=1, source_target_pairs={{0,1},{1,0},{2,3},{3,2},{4,5},{5,4},{6,7},{7,6},{8,9},{9,8},{10,11... | collective-permute-start | bytes 2359304 | tf_op jit(solution)/shard_map/ppermute | solution.py:513
  73.4 4.4 %copy-start.4 = (bf16[768,512]{1,0:T(8,128)(2,1)}, bf16[768,512]{1,0:T(8,128)(2,1)S(1)}, u32[]{:S(2)}) copy-start(bf16[768,512]{1,0:T(8,128)(2,1)S(1)} %collective-permute-done.6.swapped) | copy-start | bytes 2359300
  73.4 1.6 copy-start.9
  75.0 1.1 copy-start.10
  77.8 13.8 %copy-start.6 = (bf16[512,2048]{1,0:T(8,128)(2,1)S(1)}, bf16[512,2048]{1,0:T(8,128)(2,1)}, u32[]{:S(2)}) copy-start(bf16[512,2048]{1,0:T(8,128)(2,1)} %w_in.5) | copy-start | bytes 6291460
  77.8 33.3 %all-to-all-start = ((bf16[64,80,128]{2,1,0:T(8,128)(2,1)}), bf16[64,80,128]{2,1,0:T(8,128)(2,1)S(1)}, u32[]{:S(2)}, u32[]{:S(2)}) async-start(bf16[64,80,128]{2,1,0:T(8,128)(2,1)} %bitcast.3), calls=%async_computation | async-start | bytes 2621440 | tf_op jit(solution)/shard_map/all_to_all | solution.py:517
  90.3 32.0 %collective-permute-start.7 = (bf16[768,512]{1,0:T(8,128)(2,1)}, bf16[768,512]{1,0:T(8,128)(2,1)}, u32[]{:S(2)}, u32[]{:S(2)}) collective-permute-start(bf16[768,512]{1,0:T(8,128)(2,1)} %get-tuple-element.34.after), channel_id=1, source_target_pairs={{2,0},{3,1},{4,2},{5,3},{6,4},{7,5},{8,6},{9,7},{10,8},{11,9},{12,... | collective-permute-start | bytes 2359304 | tf_op jit(solution)/shard_map/ppermute | solution.py:488
  91.6 1.4 copy-start.7
  93.0 1.4 copy-start.8
  96.2 1.1 copy-start
  111.0 1.1 copy-start.14
  114.7 20.6 %all-to-all-start.1 = ((bf16[64,80,128]{2,1,0:T(8,128)(2,1)}), bf16[64,80,128]{2,1,0:T(8,128)(2,1)S(1)}, u32[]{:S(2)}, u32[]{:S(2)}) async-start(bf16[64,80,128]{2,1,0:T(8,128)(2,1)} %chip_sum.1), calls=%async_computation.1 | async-start | bytes 2621440 | tf_op jit(solution)/shard_map/all_to_all | solution.py:519
  120.2 2.1 %copy-start.1 = (f32[768,512]{1,0:T(8,128)S(1)}, f32[768,512]{1,0:T(8,128)}, u32[]{:S(2)}) copy-start(f32[768,512]{1,0:T(8,128)} %copy-done) | copy-start | bytes 4718596
  120.2 2.1 %copy-start.13 = (f32[512]{0:T(512)S(1)}, f32[512]{0:T(512)}, u32[]{:S(2)}) copy-start(f32[512]{0:T(512)} %param.9) | copy-start | bytes 6148
  122.3 1.1 copy-start.5
  123.4 1.1 copy-start.11
  124.5 1.1 copy-start.12
  135.3 1.1 copy-start.2
  136.4 20.4 %collective-permute-start.8 = (bf16[10,512,128]{2,1,0:T(8,128)(2,1)}, bf16[10,512,128]{2,1,0:T(8,128)(2,1)S(1)}, u32[]{:S(2)}, u32[]{:S(2)}) collective-permute-start(bf16[10,512,128]{2,1,0:T(8,128)(2,1)} %relay.3.first), channel_id=1, source_target_pairs={{0,1},{1,0},{2,3},{3,2},{4,5},{5,4},{6,7},{7,6},{8,9},{9,8},{10,11... | collective-permute-start | bytes 3932168 | tf_op jit(solution)/shard_map/ppermute | solution.py:522
  156.8 1.3 copy-start.3

commit v5 on v4

--- a/solution.py
+++ b/solution.py
@@ -1,3 +1,5 @@
+import functools
+
 import jax
 import jax.numpy as jnp
 from jax import lax
@@ -47,7 +49,8 @@
 def silu_and_slope(value):
     half = 0.5 * value
     tanh = jnp.tanh(half)
-    silu = half + half * tanh
+    silu = (half + half * tanh).astype(bf16)
+    tanh = tanh.astype(bf16)
     slope = 0.5 * ((1.0 + tanh) + silu * (1.0 - tanh))
     return silu, slope
 
@@ -67,14 +70,13 @@
 BAND = len(PLACE) * TILE
 
 
-def project_kv(normed, w_in, rows, normed_t, kv, kv_t, kv_slope):
+def project_kv(normed, w_kv, rows, normed_t, kv, kv_t, kv_slope):
     normed_t[:, rows] = normed.T
     for part in range(2):
         for pair in range(HEADS // 2):
-            columns = pl.ds((2 + part) * WIDTH + pair * PAIR, PAIR)
-            silu, slope = silu_and_slope(dot(normed, w_in[:, columns]))
-            silu = silu.astype(bf16)
-            kv_slope[part, rows, pl.ds(pair * PAIR, PAIR)] = slope.astype(bf16)
+            columns = pl.ds(part * WIDTH + pair * PAIR, PAIR)
+            silu, slope = silu_and_slope(dot(normed, w_kv[:, columns]))
+            kv_slope[part, rows, pl.ds(pair * PAIR, PAIR)] = slope
             for which in range(2):
                 head = 2 * pair + which
                 lanes = slice(which * HEAD_DIM, (which + 1) * HEAD_DIM)
@@ -82,19 +84,44 @@
                 kv_t[part * HEADS + head, :, rows] = silu[:, lanes].T
 
 
-def own_kernel(tokens, in_gain, w_in, normed_t, kv, kv_t, kv_slope, uq_t, uq_slope_t):
+def own_kernel(
+    tokens, in_gain, w_in, out_normed_t, out_kv, out_kv_t, out_kv_slope, out_uq_t, out_uq_slope_t,
+    normed_t, kv, kv_t, kv_slope, uq_t, uq_slope_t, w_uq, w_kv, sems,
+):
+    fetches = [
+        pltpu.make_async_copy(w_in.at[:, pl.ds(part * 2 * WIDTH, 2 * WIDTH)], target, sems.at[part])
+        for part, target in enumerate((w_uq, w_kv))
+    ]
+    fetches[1].start()
+    fetches[0].start()
+    fetches[1].wait()
     for tile in range(TILES):
         rows = pl.ds(tile * TILE, TILE)
         normed, _ = layer_norm_rows(tokens[rows, :].astype(f32))
         normed = (normed * in_gain[...]).astype(bf16)
-        project_kv(normed, w_in, rows, normed_t, kv, kv_t, kv_slope)
+        project_kv(normed, w_kv, rows, normed_t, kv, kv_t, kv_slope)
+    results = [
+        pltpu.make_async_copy(source, target, sems.at[2 + at])
+        for at, (source, target) in enumerate(
+            ((kv, out_kv), (kv_t, out_kv_t), (kv_slope, out_kv_slope), (normed_t, out_normed_t))
+        )
+    ]
+    for copy in results:
+        copy.start()
+    fetches[0].wait()
     for pair in range(HEADS):
-        w_t = w_in[:, pl.ds(pair * PAIR, PAIR)].T
+        w_t = w_uq[:, pl.ds(pair * PAIR, PAIR)].T
+        both = pl.ds(2 * pair, 2)
         for tile in range(TILES):
             rows = pl.ds(tile * TILE, TILE)
             silu, slope = silu_and_slope(dot(w_t, normed_t[:, rows]))
-            uq_t[pl.ds(2 * pair, 2), :, rows] = silu.astype(bf16).reshape(2, HEAD_DIM, TILE)
-            uq_slope_t[pl.ds(2 * pair, 2), :, rows] = slope.astype(bf16).reshape(2, HEAD_DIM, TILE)
+            uq_t[both, :, rows] = silu.reshape(2, HEAD_DIM, TILE)
+            uq_slope_t[both, :, rows] = slope.reshape(2, HEAD_DIM, TILE)
+        for source, target in ((uq_t, out_uq_t), (uq_slope_t, out_uq_slope_t)):
+            results.append(pltpu.make_async_copy(source.at[both], target.at[both], sems.at[2 + len(results)]))
+            results[-1].start()
+    for copy in results:
+        copy.wait()
 
 
 VMEM = pl.BlockSpec(memory_space=pltpu.VMEM)
@@ -114,11 +141,14 @@
 
 def own_call(*operands):
     along = (2 * HEADS, HEAD_DIM, ROWS)
+    shapes = window_shapes(ROWS) + (along, along)
     return pl.pallas_call(
         own_kernel,
-        in_specs=[VMEM] * len(operands),
-        out_specs=[VMEM] * 6,
-        out_shape=[jax.ShapeDtypeStruct(shape, bf16) for shape in window_shapes(ROWS) + (along, along)],
+        in_specs=[VMEM, VMEM, ANY],
+        out_specs=[ANY] * 6,
+        out_shape=[jax.ShapeDtypeStruct(shape, bf16) for shape in shapes],
+        scratch_shapes=[pltpu.VMEM(shape, bf16) for shape in shapes + ((WIDTH, 2 * WIDTH),) * 2]
+        + [pltpu.SemaphoreType.DMA((14,))],
         compiler_params=pltpu.CompilerParams(vmem_limit_bytes=62 * MIB),
         cost_estimate=pl.CostEstimate(
             flops=2 * ROWS * WIDTH * 4 * WIDTH, bytes_accessed=12 * MIB, transcendentals=ROWS * 4 * WIDTH
@@ -155,36 +185,41 @@
 
 
 def main_kernel(
-    core, far, near_a, near_b, own_normed_t, own_kv, own_kv_t, own_kv_slope, own_uq_slope_t,
-    uq_t, tokens, in_gain, out_gain, w_in, w_out, cotangent, far_ids, near_ids, own_ids,
-    layer_out, grad_kv_pre, grad_uq_pre, far_grad, near_grad, mine, theirs,
-    normed_t, kv, kv_t, kv_slope, uq_slope_t, mask, weights, slopes, mixed_t, grad_attn_t, gated_t, both, sems,
+    core, in_gain, out_gain, far_ids, near_ids, own_ids,
+    far, near_a, near_b, w_in, own_kv, own_uq_t, own_kv_t, own_uq_slope_t, own_w_out, own_cotangent, own_tokens,
+    own_normed_t, own_kv_slope,
+    out_rows, grad_kv_pre, grad_uq_pre, far_grad, near_grad, mine, theirs,
+    normed_t, kv, kv_t, kv_slope, uq_t, uq_slope_t, mask, weights, slopes, mixed_t, grad_attn_t, gated_t, both,
+    w_kv, w_out, cotangent, tokens, layer_out, sems,
 ):
     own = pl.ds(HALO, ROWS)
 
     def staged(slot, tile):
         return weights.at[slot, :, pl.ds(tile * WIDTH, WIDTH)]
 
-    arrivals = []
+    def starter(source, target):
+        copy = pltpu.make_async_copy(source, target, sems.at[len(copies)])
+        copies.append(copy)
+        copy.start()
+        return copy
+
+    copies = []
+    starter(w_in.at[:, pl.ds(2 * WIDTH, 2 * WIDTH)], w_kv)
     for slot, source in enumerate((far, near_a, near_b)):
         for tile in range(TILES):
-            arrivals.append(
-                pltpu.make_async_copy(source.at[pl.ds(tile * TILE, TILE)], staged(slot, tile), sems.at[len(arrivals)])
-            )
-    fetches = [
-        pltpu.make_async_copy(source, target, sems.at[len(arrivals) + at])
-        for at, (source, target) in enumerate(
-            (
-                (own_normed_t, normed_t.at[:, own]),
-                (own_kv, kv.at[:, own, :]),
-                (own_kv_t, kv_t.at[:, :, own]),
-                (own_kv_slope, kv_slope.at[:, own, :]),
-                (own_uq_slope_t, uq_slope_t),
-            )
-        )
-    ]
-    for copy in arrivals + fetches:
-        copy.start()
+            starter(source.at[pl.ds(tile * TILE, TILE)], staged(slot, tile))
+    arrivals = list(copies)
+    starter(own_kv, kv.at[:, own, :])
+    starter(own_uq_t, uq_t)
+    starter(own_kv_t, kv_t.at[:, :, own])
+    for_forward = copies[len(arrivals) :]
+    starter(own_uq_slope_t, uq_slope_t)
+    starter(own_w_out, w_out)
+    starter(own_cotangent, cotangent)
+    starter(own_tokens, tokens)
+    starter(own_normed_t, normed_t.at[:, own])
+    starter(own_kv_slope, kv_slope.at[:, own, :])
+    for_backward = copies[len(arrivals) + len(for_forward) :]
 
     key_at = lax.broadcasted_iota(jnp.int32, (TILE, TILE), 0)
     query_at = lax.broadcasted_iota(jnp.int32, (TILE, TILE), 1)
@@ -210,8 +245,8 @@
             halo = staged(1, at)[...].astype(f32) + staged(2, at)[...].astype(f32)
         normed, _ = layer_norm_rows(halo)
         normed = (normed * in_gain[...]).astype(bf16)
-        project_kv(normed, w_in, pl.ds(tile * TILE, TILE), normed_t, kv, kv_t, kv_slope)
-    for copy in fetches:
+        project_kv(normed, w_kv, pl.ds(tile * TILE, TILE), normed_t, kv, kv_t, kv_slope)
+    for copy in for_forward:
         copy.wait()
 
     def forward(head, carry):
@@ -220,13 +255,13 @@
             scores = dot(
                 kv[head, pl.ds(key_tile * TILE, TILE), :], uq_t[HEADS + head, :, pl.ds(tile * TILE, TILE)]
             )
-            half = scores * HALF_SCALE
+            half = (scores * HALF_SCALE).astype(bf16)
             tanh = jnp.tanh(half)
             silu = half + half * tanh
             slope = (1.0 + tanh) + silu * (1.0 - tanh)
             keep = mask[:, band]
-            weights[head, :, band] = silu.astype(bf16) * keep
-            slopes[head, :, band] = slope.astype(bf16) * keep
+            weights[head, :, band] = silu * keep
+            slopes[head, :, band] = slope * keep
         for tile in range(TILES):
             total = None
             for key_tile in range(tile, tile + SPREAD):
@@ -248,6 +283,8 @@
             slot = jnp.where(high == core[0], 0, 1)
             both[slot, at - high * HALF_BLOCKS] = value[:, part * HEAD_DIM : (part + 1) * HEAD_DIM]
 
+    for copy in for_backward:
+        copy.wait()
     gain = jnp.broadcast_to(out_gain[...], (HEAD_DIM, WIDTH)).T
     gain = jnp.concatenate([gain] * (TILE // HEAD_DIM), axis=1)
     for tile in range(TILES):
@@ -275,6 +312,9 @@
         columns = pl.ds(pair * PAIR, PAIR)
         put([4 * HEADS + block for block in blocks], dot(gated_t[...], cotangent[:, columns]))
         put(blocks, dot_nt(normed_t[:, own], uq_slope_t[pl.ds(2 * pair, 2)].reshape(PAIR, ROWS)))
+
+    departures = [pltpu.make_async_copy(layer_out, out_rows, sems.at[0])]
+    departures[0].start()
 
     def backward(head, carry):
         columns = pl.ds(pl.multiple_of(head * HEAD_DIM, HEAD_DIM), HEAD_DIM)
@@ -310,40 +350,46 @@
 
     lax.fori_loop(0, HEADS, backward, 0)
 
-    departures = []
+    def depart(source, target):
+        departures.append(pltpu.make_async_copy(source, target, sems.at[len(departures)]))
+        departures[-1].start()
+
+    def half_done(half):
+        at = len(departures)
+        departures.append(pltpu.make_async_copy(both.at[0], mine, sems.at[at]))
+
+        @pl.when(core[0] == half)
+        def _():
+            pltpu.make_async_copy(both.at[0], mine, sems.at[at]).start()
+
+        @pl.when(core[0] != half)
+        def _():
+            pltpu.make_async_copy(both.at[1], theirs, sems.at[at]).start()
+
+    def put_pair(part, pair):
+        blocks = [part * HEADS + 2 * pair + which for which in range(2)]
+        columns = pl.ds(pair * PAIR, PAIR)
+        if part == 1:
+            queries = uq_slope_t[pl.ds(HEADS + 2 * pair, 2)].reshape(PAIR, ROWS)
+            put(blocks, dot_nt(normed_t[:, own], queries))
+        else:
+            put(blocks, dot(normed_t[...], kv_slope[part - 2, :, columns]))
+
     for tile in range(2 * TILES):
         rows = pl.ds(tile * TILE, TILE)
-        total = sum(
-            dot_nt(kv_slope[part, rows, :], w_in[:, pl.ds((2 + part) * WIDTH, WIDTH)]) for part in range(2)
-        )
+        total = sum(dot_nt(kv_slope[part, rows, :], w_kv[:, pl.ds(part * WIDTH, WIDTH)]) for part in range(2))
         slot, at = divmod(tile, TILES)
         staged(slot, at)[...] = total.astype(bf16)
-        target = (far_grad, near_grad)[slot].at[pl.ds(at * TILE, TILE)]
-        departures.append(pltpu.make_async_copy(staged(slot, at), target, sems.at[tile]))
-        departures[-1].start()
-    results = [
-        pltpu.make_async_copy(source, target, sems.at[len(departures) + at])
-        for at, (source, target) in enumerate(
-            (
-                (kv_slope.at[:, own, :], grad_kv_pre),
-                (uq_slope_t, grad_uq_pre),
-                (both.at[1], theirs),
-                (both.at[0], mine),
-            )
-        )
-    ]
-    results[0].start()
-    results[1].start()
-    for pair in range(HEADS // 2):
-        blocks = (2 * pair, 2 * pair + 1)
-        queries = uq_slope_t[pl.ds(HEADS + 2 * pair, 2)].reshape(PAIR, ROWS)
-        put([HEADS + block for block in blocks], dot_nt(normed_t[:, own], queries))
-        for part in range(2):
-            columns = pl.ds(pair * PAIR, PAIR)
-            put([(2 + part) * HEADS + block for block in blocks], dot(normed_t[...], kv_slope[part, :, columns]))
-    results[2].start()
-    results[3].start()
-    for copy in departures + results:
+        depart(staged(slot, at), (far_grad, near_grad)[slot].at[pl.ds(at * TILE, TILE)])
+    depart(kv_slope.at[:, own, :], grad_kv_pre)
+    depart(uq_slope_t, grad_uq_pre)
+    for part, pair in ((1, 0), (1, 1), (2, 0)):
+        put_pair(part, pair)
+    half_done(0)
+    for part, pair in ((2, 1), (3, 0), (3, 1)):
+        put_pair(part, pair)
+    half_done(1)
+    for copy in departures:
         copy.wait()
 
 
@@ -351,6 +397,7 @@
     along = (2 * HEADS, HEAD_DIM, ROWS)
     half = (HALF_BLOCKS, WIDTH, HEAD_DIM)
     scratch = [pltpu.VMEM(shape, bf16) for shape in window_shapes(WINDOW_ROWS)] + [
+        pltpu.VMEM(along, bf16),
         pltpu.VMEM(along, bf16),
         pltpu.VMEM((TILE, BAND), bf16),
         pltpu.VMEM((HEADS, TILE, BAND), bf16),
@@ -359,12 +406,17 @@
         pltpu.VMEM((HEADS, HEAD_DIM, ROWS), bf16),
         pltpu.VMEM((WIDTH, ROWS), bf16),
         pltpu.VMEM((2,) + half, bf16),
-        pltpu.SemaphoreType.DMA((16,)),
+        pltpu.VMEM((WIDTH, 2 * WIDTH), bf16),
+        pltpu.VMEM((WIDTH, WIDTH), bf16),
+        pltpu.VMEM((ROWS, WIDTH), bf16),
+        pltpu.VMEM((ROWS, WIDTH), bf16),
+        pltpu.VMEM((ROWS, WIDTH), bf16),
+        pltpu.SemaphoreType.DMA((20,)),
     ]
     return pl.pallas_call(
         main_kernel,
-        in_specs=[SMEM] + [ANY] * 8 + [VMEM] * (len(operands) - 9),
-        out_specs=[VMEM] + [ANY] * 6,
+        in_specs=[SMEM] + [VMEM] * 5 + [ANY] * (len(operands) - 6),
+        out_specs=[ANY] * 7,
         out_shape=[
             jax.ShapeDtypeStruct(shape, bf16)
             for shape in ((ROWS, WIDTH), (2, ROWS, WIDTH), along, (ROWS, WIDTH), (ROWS, WIDTH), half, half)
@@ -395,89 +447,168 @@
     )(*operands)
 
 
-def pair_kernel(core, mine, arrived, far_grad, swapped, total, outgoing):
-    total[...] = (mine[...].astype(f32) + arrived[...].astype(f32)).astype(bf16)
-    near = jnp.where(core[0] == 1, swapped[...].astype(f32), 0.0)
-    outgoing[...] = (far_grad[...].astype(f32) + near).astype(bf16)
-
-
-def pair_call(core, mine, arrived, far_grad, swapped):
+PIECES = 4
+
+
+def pair_kernel(core, mine, arrived, far_grad, swapped, total, out_a, out_b, held, others, homes, nears, sems, out_sems):
+    rows = HALF_BLOCKS * WIDTH // PIECES
+    home_rows = ROWS // 2
+    copies = []
+
+    def start(source, target):
+        copies.append(pltpu.make_async_copy(source, target, sems.at[len(copies)]))
+        copies[-1].start()
+
+    for half in range(2):
+        at = pl.ds(half * home_rows, home_rows)
+        start(far_grad.at[at], homes.at[at])
+        start(swapped.at[at], nears.at[at])
+    for piece in range(PIECES):
+        at = pl.ds(piece * rows, rows)
+        start(mine.at[at], held.at[at])
+        start(arrived.at[at], others.at[at])
+    results = []
+
+    def finish(source, target):
+        results.append(pltpu.make_async_copy(source, target, out_sems.at[len(results)]))
+        results[-1].start()
+
+    for half, target in enumerate((out_a, out_b)):
+        at = pl.ds(half * home_rows, home_rows)
+        copies[2 * half].wait()
+        copies[2 * half + 1].wait()
+        near = jnp.where(core[0] == 1, nears[at, :].astype(f32), 0.0)
+        homes[at, :] = (homes[at, :].astype(f32) + near).astype(bf16)
+        finish(homes.at[at], target)
+    for piece in range(PIECES):
+        at = pl.ds(piece * rows, rows)
+        copies[4 + 2 * piece].wait()
+        copies[5 + 2 * piece].wait()
+        held[at, :] = (held[at, :].astype(f32) + others[at, :].astype(f32)).astype(bf16)
+        finish(held.at[at], total.at[at])
+    for copy in results:
+        copy.wait()
+
+
+def pair_call(core, *operands):
+    half = (HALF_BLOCKS * WIDTH, HEAD_DIM)
+    home = (ROWS, WIDTH)
     return pl.pallas_call(
         pair_kernel,
-        in_specs=[SMEM] + [VMEM] * 4,
-        out_specs=[VMEM] * 2,
-        out_shape=[jax.ShapeDtypeStruct(like.shape, bf16) for like in (mine, far_grad)],
+        in_specs=[SMEM] + [ANY] * 4,
+        out_specs=[ANY] * 3,
+        out_shape=[jax.ShapeDtypeStruct(shape, bf16) for shape in (half, (ROWS // 2, WIDTH), (ROWS // 2, WIDTH))],
+        scratch_shapes=[pltpu.VMEM(shape, bf16) for shape in (half, half, home, home)]
+        + [pltpu.SemaphoreType.DMA((4 + 2 * PIECES,)), pltpu.SemaphoreType.DMA((2 + PIECES,))],
+        compiler_params=pltpu.CompilerParams(vmem_limit_bytes=62 * MIB),
+        name="pair_sum",
+    )(core, *operands)
+
+
+def chips_kernel(parts, *refs):
+    totals = refs[-1]
+    total = jnp.sum(parts[...].astype(f32), axis=0, keepdims=True).astype(bf16)
+    totals[...] = jnp.broadcast_to(total, totals.shape)
+
+
+def chips_call(parts, *after):
+    return pl.pallas_call(
+        chips_kernel,
+        in_specs=[VMEM] + [ANY] * len(after),
+        out_specs=VMEM,
+        out_shape=jax.ShapeDtypeStruct(parts.shape, bf16),
         compiler_params=pltpu.CompilerParams(vmem_limit_bytes=24 * MIB),
-        name="pair_sum",
-    )(core, mine, arrived, far_grad, swapped)
-
-
-def chips_kernel(parts, after, totals, staging, sem):
-    del after
-    total = jnp.sum(parts[...].astype(f32), axis=0, keepdims=True).astype(bf16)
-    staging[...] = jnp.broadcast_to(total, staging.shape)
-    copy = pltpu.make_async_copy(staging, totals, sem)
-    copy.start()
-    copy.wait()
-
-
-def chips_call(parts, after):
-    return pl.pallas_call(
-        chips_kernel,
-        in_specs=[VMEM, ANY],
-        out_specs=HBM,
-        out_shape=jax.ShapeDtypeStruct(parts.shape, bf16),
-        scratch_shapes=[pltpu.VMEM(parts.shape, bf16), pltpu.SemaphoreType.DMA],
-        compiler_params=pltpu.CompilerParams(vmem_limit_bytes=62 * MIB),
         name="chip_sum",
-    )(parts, after)
-
-
-def unpack_kernel(core, first, second, grad_w_in, grad_w_out):
-    def piece(block):
-        half, at = divmod(block, HALF_BLOCKS)
-        return jnp.where(core[0] == half, first[at].astype(f32), second[at].astype(f32))
-
-    for block in range(4 * HEADS):
-        grad_w_in[:, pl.ds(block * HEAD_DIM, HEAD_DIM)] = piece(block)
-    for block in range(HEADS):
-        grad_w_out[:, pl.ds(block * HEAD_DIM, HEAD_DIM)] = piece(4 * HEADS + block)
-
-
-def unpack_call(core, first, second):
-    vmem = pl.BlockSpec(memory_space=pltpu.VMEM)
-    return pl.pallas_call(
-        unpack_kernel,
-        in_specs=[pl.BlockSpec(memory_space=pltpu.SMEM), vmem, vmem],
-        out_specs=[vmem] * 2,
+    )(parts, *after)
+
+
+def unpack_kernel(flip, core, blocks, *refs):
+    grad_w_in, grad_w_out, staging, sems = refs[-4:]
+    for half in range(2):
+
+        @pl.when(core[0] == half ^ flip)
+        def _(half=half):
+            copies = []
+            for at in range(HALF_BLOCKS):
+                staging[at] = blocks[at].astype(f32)
+                block = half * HALF_BLOCKS + at
+                if block < 4 * HEADS:
+                    target = grad_w_in.at[:, pl.ds(block * HEAD_DIM, HEAD_DIM)]
+                else:
+                    target = grad_w_out.at[:, pl.ds((block - 4 * HEADS) * HEAD_DIM, HEAD_DIM)]
+                copies.append(pltpu.make_async_copy(staging.at[at], target, sems.at[at]))
+                copies[-1].start()
+            for copy in copies:
+                copy.wait()
+
+
+def unpack_call(core, blocks, flip, into=()):
+    return pl.pallas_call(
+        functools.partial(unpack_kernel, flip),
+        in_specs=[SMEM, VMEM] + [ANY] * len(into),
+        out_specs=[ANY] * 2,
         out_shape=(
             jax.ShapeDtypeStruct((WIDTH, 4 * WIDTH), f32),
             jax.ShapeDtypeStruct((WIDTH, WIDTH), f32),
         ),
+        scratch_shapes=[
+            pltpu.VMEM((HALF_BLOCKS, WIDTH, HEAD_DIM), f32),
+            pltpu.SemaphoreType.DMA((HALF_BLOCKS,)),
+        ],
+        input_output_aliases={2: 0, 3: 1} if into else {},
         compiler_params=pltpu.CompilerParams(vmem_limit_bytes=24 * MIB),
         name="unpack",
-    )(core, first, second)
-
-
-def step_kernel(tokens, in_gain, cotangent, grad_normed, sent, swapped, core, grad_tokens):
-    normed, inverse = layer_norm_rows(tokens[...].astype(f32))
-    near = jnp.where(core[0] == 0, swapped[...].astype(f32), 0.0)
-    upstream = grad_normed[...] + sent[...].astype(f32) + near
-    scaled_grad = upstream * in_gain[...]
-    first = jnp.mean(scaled_grad, axis=1, keepdims=True)
-    second = jnp.mean(scaled_grad * normed, axis=1, keepdims=True)
-    grad_tokens[...] = (
-        cotangent[...].astype(f32) + (scaled_grad - first - normed * second) * inverse
-    ).astype(bf16)
+    )(core, blocks, *into)
+
+
+def step_kernel(
+    core, in_gain, tokens, cotangent, grad_normed, sent_a, sent_b, swapped, after, grad_tokens,
+    rows_in, cot, grad, sent, near, result, sems, out_sems,
+):
+    del after
+    half = ROWS // 2
+    copies = []
+    for part, sent_half in enumerate((sent_a, sent_b)):
+        at = pl.ds(part * half, half)
+        for source, target in (
+            (tokens.at[at], rows_in.at[at]),
+            (grad_normed.at[at], grad.at[at]),
+            (swapped.at[at], near.at[at]),
+            (sent_half, sent.at[at]),
+            (cotangent.at[at], cot.at[at]),
+        ):
+            copies.append(pltpu.make_async_copy(source, target, sems.at[len(copies)]))
+            copies[-1].start()
+    results = []
+    for part in range(2):
+        at = pl.ds(part * half, half)
+        copies[5 * part].wait()
+        normed, inverse = layer_norm_rows(rows_in[at, :].astype(f32))
+        for copy in copies[5 * part + 1 : 5 * part + 5]:
+            copy.wait()
+        home = jnp.where(core[0] == 0, near[at, :].astype(f32), 0.0)
+        scaled_grad = (grad[at, :] + sent[at, :].astype(f32) + home) * in_gain[...]
+        first = jnp.mean(scaled_grad, axis=1, keepdims=True)
+        second = jnp.mean(scaled_grad * normed, axis=1, keepdims=True)
+        result[at, :] = (
+            cot[at, :].astype(f32) + (scaled_grad - first - normed * second) * inverse
+        ).astype(bf16)
+        results.append(pltpu.make_async_copy(result.at[at], grad_tokens.at[at], out_sems.at[part]))
+        results[-1].start()
+    for copy in results:
+        copy.wait()
 
 
 def step_call(*operands):
+    shape = (ROWS, WIDTH)
     return pl.pallas_call(
         step_kernel,
-        in_specs=[VMEM] * 6 + [SMEM],
-        out_specs=VMEM,
-        out_shape=jax.ShapeDtypeStruct((ROWS, WIDTH), bf16),
-        compiler_params=pltpu.CompilerParams(vmem_limit_bytes=24 * MIB),
+        in_specs=[SMEM, VMEM] + [ANY] * 7,
+        out_specs=ANY,
+        out_shape=jax.ShapeDtypeStruct(shape, bf16),
+        scratch_shapes=[pltpu.VMEM(shape, kind) for kind in (bf16, bf16, f32, bf16, bf16, bf16)]
+        + [pltpu.SemaphoreType.DMA((10,)), pltpu.SemaphoreType.DMA((2,))],
+        compiler_params=pltpu.CompilerParams(vmem_limit_bytes=62 * MIB),
         name="input_norm_gradient",
     )(*operands)
 
@@ -503,24 +634,28 @@
     *window, uq_t, uq_slope_t = own_call(tokens, in_gain_row, w_in)
     far = relay_call(far, uq_t, far_ids, near_ids)
     near_b = lax.ppermute(far, "core", [(1, 0)])
+    normed_t, kv, kv_t, kv_slope = window
     layer_out, grad_kv_pre, grad_uq_pre, far_grad, near_grad, mine, theirs = main_call(
-        core, far, near_a, near_b, *window, uq_slope_t,
-        uq_t, tokens, in_gain_row, out_gain.reshape(1, WIDTH), w_in, w_out, cotangent,
-        far_ids, near_ids, own_ids,
+        core, in_gain_row, out_gain.reshape(1, WIDTH), far_ids, near_ids, own_ids,
+        far, near_a, near_b, w_in, kv, uq_t, kv_t, uq_slope_t, w_out, cotangent, tokens, normed_t, kv_slope,
     )
 
     arrived = lax.ppermute(theirs, "core", SWAP)
     swapped = lax.ppermute(near_grad, "core", SWAP)
-    partial, outgoing = pair_call(core, mine, arrived, far_grad, swapped)
-    sent = slow_relay_call(shifted(outgoing, -2))
-    grad_normed = back_call(grad_kv_pre, grad_uq_pre, w_in, outgoing)
+    flat = (HALF_BLOCKS * WIDTH, HEAD_DIM)
+    partial, out_a, out_b = pair_call(core, mine.reshape(flat), arrived.reshape(flat), far_grad, swapped)
+    sent_a = slow_relay_call(shifted(out_a, -2))
+    sent_b = slow_relay_call(shifted(out_b, -2))
+    grad_normed = back_call(grad_kv_pre, grad_uq_pre, w_in, out_b)
     parts = lax.all_to_all(partial.reshape(64, 80, HEAD_DIM), CHIPS, 0, 0, tiled=True)
-    total = chips_call(parts, grad_normed)
-    totals = lax.all_to_all(total, CHIPS, 0, 0, tiled=True)
-    grad_tokens = step_call(tokens, in_gain_row, cotangent, grad_normed, sent, swapped, core)
-    totals = relay_call(totals.reshape(HALF_BLOCKS, WIDTH, HEAD_DIM), grad_tokens)
+    totals = lax.all_to_all(chips_call(parts, grad_normed, sent_a), CHIPS, 0, 0, tiled=True)
+    totals = totals.reshape(HALF_BLOCKS, WIDTH, HEAD_DIM)
     other = lax.ppermute(totals, "core", SWAP)
-    grad_w_in, grad_w_out = unpack_call(core, totals, other)
+    halves = unpack_call(core, totals, 0)
+    grad_w_in, grad_w_out = unpack_call(core, other, 1, halves)
+    grad_tokens = step_call(
+        core, in_gain_row, tokens, cotangent, grad_normed, sent_a, sent_b, swapped, grad_w_out,
+    )
     return (layer_out, grad_tokens, grad_w_in, grad_w_out)
 
 

time: 162 us -> 151 us (0.932)
  the two profiles are of different devices: /device:TPU:1 before, /device:TPU:39 now
where the time goes in v5:
time: 151 us; the launch traced here: 150 us
  Pallas kernels  53.8 us (36%)
  starting transfers between devices  50.8 us (34%)
  waiting for transfers between devices  31.9 us (21%)
  local copies, waits for them, and re-layouts  12.3 us (8%)
    pallas_call x1, Pallas kernels, main_call(): pl.pallas_call(main_kernel, in_specs=[SMEM] + [VMEM] * 5 + [ANY] * (len(o...  33.4 us
    all_to_all x1, waiting for transfers between devices, on_device(): lax.all_to_all(chips_call(parts, grad_normed, sent_a), CHIPS, 0, 0, tiled...  15.2 us
    ppermute x5, starting transfers between devices, shifted(): lax.ppermute(value, ALL, [(source, source + steps) for source in range(fi...  14.7 us
    unnamed x34, local copies, waits for them, and re-layouts  11.6 us
    all_to_all x1, starting transfers between devices, on_device(): lax.all_to_all(partial.reshape(64, 80, HEAD_DIM), CHIPS, 0, 0, tiled=True)  11.5 us
    all_to_all x1, starting transfers between devices, on_device(): lax.all_to_all(chips_call(parts, grad_normed, sent_a), CHIPS, 0, 0, tiled...  10.3 us
    all_to_all x1, waiting for transfers between devices, on_device(): lax.all_to_all(partial.reshape(64, 80, HEAD_DIM), CHIPS, 0, 0, tiled=True)  9.4 us
    ppermute x1, starting transfers between devices, on_device(): other = lax.ppermute(totals, 'core', SWAP)  9.01 us
  transfers between devices with their start and end apart: 12, of which 6 were waited for; matrix products, arithmetic and copies ran while one was open for 0% of the time, Pallas kernels for 7%

profile of v5, /device:TPU:39, one launch (start us, length us, event | category | flops | bytes accessed | tf_op | source)
XLA Modules:
  0.0 149.9 jit_solution(10578069443128254725)
XLA Ops:
  0.6 2.7 %collective-permute-start.2 = (bf16[768,512]{1,0:T(8,128)(2,1)}, bf16[768,512]{1,0:T(8,128)(2,1)S(1)}, u32[]{:S(2)}, u32[]{:S(2)}) collective-permute-start(bf16[768,512]{1,0:T(8,128)(2,1)} %tokens.3), channel_id=1, source_target_pairs={{0,2},{1,3},{2,4},{3,5},{4,6},{5,7},{6,8},{7,9},{8,10},{9,11},{10,... | collective-permute-start | bytes 2359304 | tf_op jit(solution)/shard_map/ppermute | solution.py:619
  3.3 0.7 reshape.35.own_ids
  4.0 3.9 %collective-permute-start.1 = (s32[1,768]{1,0:T(1,128)S(1)}, s32[1,768]{1,0:T(1,128)S(1)}, u32[]{:S(2)}, u32[]{:S(2)}) collective-permute-start(s32[1,768]{1,0:T(1,128)S(1)} %reshape.35.own_ids), channel_id=1, source_target_pairs={{0,1},{1,2},{2,3},{3,4},{4,5},{5,6},{6,7},{7,8},{8,9},{9,10},{10,1... | collective-permute-start | bytes 9224 | tf_op jit(solution)/shard_map/ppermute | solution.py:619
  8.0 3.1 %collective-permute-start = (s32[1,768]{1,0:T(1,128)S(1)}, s32[1,768]{1,0:T(1,128)S(1)}, u32[]{:S(2)}, u32[]{:S(2)}) collective-permute-start(s32[1,768]{1,0:T(1,128)S(1)} %reshape.35.own_ids), channel_id=1, source_target_pairs={{0,2},{1,3},{2,4},{3,5},{4,6},{5,7},{6,8},{7,9},{8,10},{9,11},{10,... | collective-permute-start | bytes 9224 | tf_op jit(solution)/shard_map/ppermute | solution.py:619
  11.1 1.3 collective-permute-start.3
  12.4 7.8 %own_projection.1 = (bf16[512,768]{1,0:T(8,128)(2,1)}, bf16[8,768,128]{2,1,0:T(8,128)(2,1)}, bf16[8,128,768]{2,1,0:T(8,128)(2,1)}, bf16[2,768,512]{2,1,0:T(8,128...) custom-call(bf16[768,512]{1,0:T(8,128)(2,1)} %tokens.3, f32[1,512]{1,0:T(1,128)} %bitcast.11, ...), custom_call_target="tpu_custom_call" | custom-call | flops 1610612736 | bytes 12582912 | tf_op jit(solution)/shard_map/own_projection/pallas_call | solution.py:145
  20.2 0.0 collective-permute-done.1.refs_3_.near_ids
  20.2 1.0 collective-permute-done.refs_2_.far_ids
  21.3 0.0 collective-permute-done.2.refs_0_
  21.3 0.6 copy-done.14
  21.9 0.3 copy-done.10
  22.2 3.5 %collective-permute-start.4 = (bf16[768,512]{1,0:T(8,128)(2,1)}, bf16[768,512]{1,0:T(8,128)(2,1)S(1)}, u32[]{:S(2)}, u32[]{:S(2)}) collective-permute-start(bf16[768,512]{1,0:T(8,128)(2,1)} %relay.1.far), channel_id=1, source_target_pairs={{1,0},{3,2},{5,4},{7,6},{9,8},{11,10},{13,12},{15,14},{17,16},{19,... | collective-permute-start | bytes 2359304 | tf_op jit(solution)/shard_map/ppermute | solution.py:636
  25.6 0.0 collective-permute-done.3.near_a
  25.7 2.0 %collective-permute-done.4.near_b = bf16[768,512]{1,0:T(8,128)(2,1)S(1)} collective-permute-done((bf16[768,512]{1,0:T(8,128)(2,1)}, bf16[768,512]{1,0:T(8,128)(2,1)S(1)}, u32[]{:S(2)}, u32[]{:S(2)}) %collective-permute-start.4) | collective-permute-done | bytes 786464 | tf_op jit(solution)/shard_map/ppermute | solution.py:636
  27.7 0.9 copy-done.16
  28.6 33.4 %attention.1 = (bf16[768,512]{1,0:T(8,128)(2,1)}, bf16[2,768,512]{2,1,0:T(8,128)(2,1)}, bf16[8,128,768]{2,1,0:T(8,128)(2,1)}, bf16[768,512]{1,0:T(8,128)(2,1)}, ...) custom-call(s32[1]{0:T(128)} %bitcast.core, f32[1,512]{1,0:T(1,128)} %bitcast.12, ...), custom_call_target="tpu_custom_call" | custom-call | flops 20000000000 | bytes 25165824 | tf_op jit(solution)/shard_map/attention/pallas_call | solution.py:416
  62.1 0.5 collective-permute-start.5
  62.5 0.1 collective-permute-start.6
  62.6 3.9 %collective-permute-done.6.swapped = bf16[768,512]{1,0:T(8,128)(2,1)S(1)} collective-permute-done((bf16[768,512]{1,0:T(8,128)(2,1)}, bf16[768,512]{1,0:T(8,128)(2,1)S(1)}, u32[]{:S(2)}, u32[]{:S(2)}) %collective-permute-start.6) | collective-permute-done | bytes 786464 | tf_op jit(solution)/shard_map/ppermute | solution.py:644
  66.5 0.0 collective-permute-done.5
  66.5 0.9 copy-done.9
  67.4 3.1 %pair_sum.1 = (bf16[5120,128]{1,0:T(8,128)(2,1)}, bf16[384,512]{1,0:T(8,128)(2,1)}, bf16[384,512]{1,0:T(8,128)(2,1)}) custom-call(s32[1]{0:T(128)} %bitcast.core, bf16[5120,128]{1,0:T(8,128)(2,1)} %bitcast.9, bf16[5120,128]{1,0:T(8,128)(2,1)} %bitcast.4.arrived, bf16[768,512]{1,0:T(8,128)(2,1)} %get-tuple-element.35.far_grad, bf16[768,512]{1,0:T(8,128)(2,1)} %copy-done.9), custom_call_target="tpu_custom_call" | custom-call | tf_op jit(solution)/shard_map/pair_sum/pallas_call | solution.py:496
  70.6 2.4 %collective-permute-start.7 = (bf16[384,512]{1,0:T(8,128)(2,1)}, bf16[384,512]{1,0:T(8,128)(2,1)S(1)}, u32[]{:S(2)}, u32[]{:S(2)}) collective-permute-start(bf16[384,512]{1,0:T(8,128)(2,1)} %get-tuple-element.38), channel_id=1, source_target_pairs={{2,0},{3,1},{4,2},{5,3},{6,4},{7,5},{8,6},{9,7},{10,8},{11,9},{12,... | collective-permute-start | bytes 1179656 | tf_op jit(solution)/shard_map/ppermute | solution.py:619
  73.0 11.5 %all-to-all-start = ((bf16[64,80,128]{2,1,0:T(8,128)(2,1)}), bf16[64,80,128]{2,1,0:T(8,128)(2,1)S(1)}, u32[]{:S(2)}, u32[]{:S(2)}) async-start(bf16[64,80,128]{2,1,0:T(8,128)(2,1)} %bitcast.10), calls=%async_computation | async-start | bytes 2621440 | tf_op jit(solution)/shard_map/all_to_all | solution.py:650
  84.5 0.0 copy-start.2
  84.5 1.6 %copy-done.2 = bf16[512,2048]{1,0:T(8,128)(2,1)S(1)} copy-done((bf16[512,2048]{1,0:T(8,128)(2,1)S(1)}, bf16[512,2048]{1,0:T(8,128)(2,1)}, u32[]{:S(2)}) %copy-start.2) | copy-done | bytes 2097176
  86.1 1.4 copy-done.3
  87.5 1.4 copy-done.4
  88.9 1.0 copy-done.7
  89.9 1.8 %projection_gradient.1.refs_0_.grad_normed = f32[768,512]{1,0:T(8,128)S(1)} custom-call(bf16[2,768,512]{2,1,0:T(8,128)(2,1)S(1)} %copy-done.3, bf16[8,128,768]{2,1,0:T(8,128)(2,1)S(1)} %copy-done.4, bf16[512,2048]{1,0:T(8,128)(2,1)S(1)} %copy-done.2, bf16[384,512]{1,0:T(8,128)(2,1)S(1)} %copy-done.7), custom_call_target="tpu_custom_call" | custom-call | flops 1600000000 | bytes 8388608 | tf_op jit(solution)/shard_map/projection_gradient/pallas_call | solution.py:439
  91.7 0.0 collective-permute-done.7.refs_0_
  91.7 0.8 copy-done.5
  92.5 9.4 %all-to-all-done.parts = bf16[64,80,128]{2,1,0:T(8,128)(2,1)S(1)} async-done(((bf16[64,80,128]{2,1,0:T(8,128)(2,1)}), bf16[64,80,128]{2,1,0:T(8,128)(2,1)S(1)}, u32[]{:S(2)}, u32[]{:S(2)}) %all-to-all-start) | async-done | bytes 1310752 | tf_op jit(solution)/shard_map/all_to_all | solution.py:650
  101.9 0.0 copy-done
  101.9 1.0 copy-done.6
  102.9 0.2 chip_sum.1
  103.1 0.0 copy-start.1
  103.1 1.0 copy-done.1
  104.2 10.3 %all-to-all-start.1 = ((bf16[64,80,128]{2,1,0:T(8,128)(2,1)}), bf16[64,80,128]{2,1,0:T(8,128)(2,1)S(1)}, u32[]{:S(2)}, u32[]{:S(2)}) async-start(bf16[64,80,128]{2,1,0:T(8,128)(2,1)} %copy-done.1), calls=%async_computation.1 | async-start | bytes 2621440 | tf_op jit(solution)/shard_map/all_to_all | solution.py:651
  114.5 2.5 %collective-permute-start.8 = (bf16[384,512]{1,0:T(8,128)(2,1)S(1)}, bf16[384,512]{1,0:T(8,128)(2,1)S(1)}, u32[]{:S(2)}, u32[]{:S(2)}) collective-permute-start(bf16[384,512]{1,0:T(8,128)(2,1)S(1)} %copy-done.8), channel_id=1, source_target_pairs={{2,0},{3,1},{4,2},{5,3},{6,4},{7,5},{8,6},{9,7},{10,8},{11,9},{12,... | collective-permute-start | bytes 1179656 | tf_op jit(solution)/shard_map/ppermute | solution.py:619
  117.0 15.2 %all-to-all-done.1 = bf16[64,80,128]{2,1,0:T(8,128)(2,1)S(1)} async-done(((bf16[64,80,128]{2,1,0:T(8,128)(2,1)}), bf16[64,80,128]{2,1,0:T(8,128)(2,1)S(1)}, u32[]{:S(2)}, u32[]{:S(2)}) %all-to-all-start.1) | async-done | bytes 1310752 | tf_op jit(solution)/shard_map/all_to_all | solution.py:651
  132.2 9.0 %collective-permute-start.9 = (bf16[10,512,128]{2,1,0:T(8,128)(2,1)S(1)}, bf16[10,512,128]{2,1,0:T(8,128)(2,1)S(1)}, u32[]{:S(2)}, u32[]{:S(2)}) collective-permute-start(bf16[10,512,128]{2,1,0:T(8,128)(2,1)S(1)} %bitcast.7), channel_id=1, source_target_pairs={{0,1},{1,0},{2,3},{3,2},{4,5},{5,4},{6,7},{7,6},{8,9},{9,8},{10,11... | collective-permute-start | bytes 3932168 | tf_op jit(solution)/shard_map/ppermute | solution.py:653
  141.2 0.0 collective-permute-done.8.refs_0_
  141.2 0.7 copy-done.11
  142.0 1.6 %unpack.2 = (f32[512,2048]{1,0:T(8,128)}, f32[512,512]{1,0:T(8,128)}) custom-call(s32[1]{0:T(128)} %bitcast.core, bf16[10,512,128]{2,1,0:T(8,128)(2,1)S(1)} %bitcast.8), custom_call_target="tpu_custom_call" | custom-call | tf_op jit(solution)/shard_map/unpack/pallas_call | solution.py:546
  143.6 0.3 collective-permute-done.9.blocks
  143.9 1.6 %unpack.3 = (f32[512,2048]{1,0:T(8,128)}, f32[512,512]{1,0:T(8,128)}) custom-call(s32[1]{0:T(128)} %bitcast.core, bf16[10,512,128]{2,1,0:T(8,128)(2,1)S(1)} %collective-permute-done.9.blocks, f32[512,2048]{1,0:T(8,128)} %get-tuple-element.40.refs_0_, f32[512,512]{1,0:T(8,128)} %get-tuple-element.41.refs_1_), custom_call_target="tpu_custom_call", output_to_operand_aliasing={{0}: (2, {}), {1}: (3, {})} | custom-call | tf_op jit(solution)/shard_map/unpack/pallas_call | solution.py:546
  145.5 4.3 %input_norm_gradient.1 = bf16[768,512]{1,0:T(8,128)(2,1)} custom-call(s32[1]{0:T(128)} %bitcast.core, f32[1,512]{1,0:T(1,128)} %bitcast.13, bf16[768,512]{1,0:T(8,128)(2,1)} %tokens.3, bf16[768,512]{1,0:T(8,128)(2,1)} %cotangent.1, f32[768,512]{1,0:T(8,128)} %copy-done, bf16[384,512]{1,0:T(8,128)(2,1)} %relay_home.2.refs_1_.sent_a, ...), custom_call_target="tpu_custom_call" | custom-call | tf_op jit(solution)/shard_map/input_norm_gradient/pallas_call | solution.py:604
  (22 shorter events, 0.0 us)
Async XLA Ops:
  0.6 20.7 %collective-permute-start.2 = (bf16[768,512]{1,0:T(8,128)(2,1)}, bf16[768,512]{1,0:T(8,128)(2,1)S(1)}, u32[]{:S(2)}, u32[]{:S(2)}) collective-permute-start(bf16[768,512]{1,0:T(8,128)(2,1)} %tokens.3), channel_id=1, source_target_pairs={{0,2},{1,3},{2,4},{3,5},{4,6},{5,7},{6,8},{7,9},{8,10},{9,11},{10,... | collective-permute-start | bytes 2359304 | tf_op jit(solution)/shard_map/ppermute | solution.py:619
  4.0 16.2 %copy-start.12 = (s32[1,768]{1,0:T(1,128)}, s32[1,768]{1,0:T(1,128)S(1)}, u32[]{:S(2)}) copy-start(s32[1,768]{1,0:T(1,128)S(1)} %reshape.35.own_ids) | copy-start | bytes 9220
  4.0 16.2 %collective-permute-start.1 = (s32[1,768]{1,0:T(1,128)S(1)}, s32[1,768]{1,0:T(1,128)S(1)}, u32[]{:S(2)}, u32[]{:S(2)}) collective-permute-start(s32[1,768]{1,0:T(1,128)S(1)} %reshape.35.own_ids), channel_id=1, source_target_pairs={{0,1},{1,2},{2,3},{3,4},{4,5},{5,6},{6,7},{7,8},{8,9},{9,10},{10,1... | collective-permute-start | bytes 9224 | tf_op jit(solution)/shard_map/ppermute | solution.py:619
  8.0 13.3 %collective-permute-start = (s32[1,768]{1,0:T(1,128)S(1)}, s32[1,768]{1,0:T(1,128)S(1)}, u32[]{:S(2)}, u32[]{:S(2)}) collective-permute-start(s32[1,768]{1,0:T(1,128)S(1)} %reshape.35.own_ids), channel_id=1, source_target_pairs={{0,2},{1,3},{2,4},{3,5},{4,6},{5,7},{6,8},{7,9},{8,10},{9,11},{10,... | collective-permute-start | bytes 9224 | tf_op jit(solution)/shard_map/ppermute | solution.py:619
  11.1 14.6 %collective-permute-start.3 = (bf16[768,512]{1,0:T(8,128)(2,1)}, bf16[768,512]{1,0:T(8,128)(2,1)S(1)}, u32[]{:S(2)}, u32[]{:S(2)}) collective-permute-start(bf16[768,512]{1,0:T(8,128)(2,1)} %tokens.3), channel_id=1, source_target_pairs={{0,1},{2,3},{4,5},{6,7},{8,9},{10,11},{12,13},{14,15},{16,17},{18,... | collective-permute-start | bytes 2359304 | tf_op jit(solution)/shard_map/ppermute | solution.py:631
  20.2 1.1 copy-start.13
  21.3 0.6 copy-start.14
  21.3 0.9 copy-start.10
  22.2 5.5 %collective-permute-start.4 = (bf16[768,512]{1,0:T(8,128)(2,1)}, bf16[768,512]{1,0:T(8,128)(2,1)S(1)}, u32[]{:S(2)}, u32[]{:S(2)}) collective-permute-start(bf16[768,512]{1,0:T(8,128)(2,1)} %relay.1.far), channel_id=1, source_target_pairs={{1,0},{3,2},{5,4},{7,6},{9,8},{11,10},{13,12},{15,14},{17,16},{19,... | collective-permute-start | bytes 2359304 | tf_op jit(solution)/shard_map/ppermute | solution.py:636
  25.6 2.0 %copy-start.15 = (bf16[768,512]{1,0:T(8,128)(2,1)}, bf16[768,512]{1,0:T(8,128)(2,1)S(1)}, u32[]{:S(2)}) copy-start(bf16[768,512]{1,0:T(8,128)(2,1)S(1)} %collective-permute-done.3.near_a) | copy-start | bytes 2359300
  27.7 0.9 copy-start.16
  62.1 4.5 %collective-permute-start.5 = (bf16[10,512,128]{2,1,0:T(8,128)(2,1)}, bf16[10,512,128]{2,1,0:T(8,128)(2,1)}, u32[]{:S(2)}, u32[]{:S(2)}) collective-permute-start(bf16[10,512,128]{2,1,0:T(8,128)(2,1)} %get-tuple-element.34), channel_id=1, source_target_pairs={{0,1},{1,0},{2,3},{3,2},{4,5},{5,4},{6,7},{7,6},{8,9},{9,8},{10,11... | collective-permute-start | bytes 3932168 | tf_op jit(solution)/shard_map/ppermute | solution.py:643
  62.5 4.0 %collective-permute-start.6 = (bf16[768,512]{1,0:T(8,128)(2,1)}, bf16[768,512]{1,0:T(8,128)(2,1)S(1)}, u32[]{:S(2)}, u32[]{:S(2)}) collective-permute-start(bf16[768,512]{1,0:T(8,128)(2,1)} %get-tuple-element.36), channel_id=1, source_target_pairs={{0,1},{1,0},{2,3},{3,2},{4,5},{5,4},{6,7},{7,6},{8,9},{9,8},{10,11... | collective-permute-start | bytes 2359304 | tf_op jit(solution)/shard_map/ppermute | solution.py:644
  66.5 0.9 copy-start.9
  70.6 21.2 %collective-permute-start.7 = (bf16[384,512]{1,0:T(8,128)(2,1)}, bf16[384,512]{1,0:T(8,128)(2,1)S(1)}, u32[]{:S(2)}, u32[]{:S(2)}) collective-permute-start(bf16[384,512]{1,0:T(8,128)(2,1)} %get-tuple-element.38), channel_id=1, source_target_pairs={{2,0},{3,1},{4,2},{5,3},{6,4},{7,5},{8,6},{9,7},{10,8},{11,9},{12,... | collective-permute-start | bytes 1179656 | tf_op jit(solution)/shard_map/ppermute | solution.py:619
  73.0 28.9 %all-to-all-start = ((bf16[64,80,128]{2,1,0:T(8,128)(2,1)}), bf16[64,80,128]{2,1,0:T(8,128)(2,1)S(1)}, u32[]{:S(2)}, u32[]{:S(2)}) async-start(bf16[64,80,128]{2,1,0:T(8,128)(2,1)} %bitcast.10), calls=%async_computation | async-start | bytes 2621440 | tf_op jit(solution)/shard_map/all_to_all | solution.py:650
  84.5 1.6 %copy-start.2 = (bf16[512,2048]{1,0:T(8,128)(2,1)S(1)}, bf16[512,2048]{1,0:T(8,128)(2,1)}, u32[]{:S(2)}) copy-start(bf16[512,2048]{1,0:T(8,128)(2,1)} %w_in.5) | copy-start | bytes 6291460
  86.1 1.4 copy-start.3
  87.5 1.4 copy-start.4
  88.9 1.0 copy-start.7
  91.7 10.2 %copy-start = (f32[768,512]{1,0:T(8,128)}, f32[768,512]{1,0:T(8,128)S(1)}, u32[]{:S(2)}) copy-start(f32[768,512]{1,0:T(8,128)S(1)} %projection_gradient.1.refs_0_.grad_normed) | copy-start | bytes 4718596
  91.7 0.8 copy-start.5
  101.9 1.0 copy-start.6
  103.1 1.1 copy-start.1
  104.2 10.3 %copy-start.8 = (bf16[384,512]{1,0:T(8,128)(2,1)S(1)}, bf16[384,512]{1,0:T(8,128)(2,1)}, u32[]{:S(2)}) copy-start(bf16[384,512]{1,0:T(8,128)(2,1)} %get-tuple-element.37.after) | copy-start | bytes 1179652
  104.2 28.0 %all-to-all-start.1 = ((bf16[64,80,128]{2,1,0:T(8,128)(2,1)}), bf16[64,80,128]{2,1,0:T(8,128)(2,1)S(1)}, u32[]{:S(2)}, u32[]{:S(2)}) async-start(bf16[64,80,128]{2,1,0:T(8,128)(2,1)} %copy-done.1), calls=%async_computation.1 | async-start | bytes 2621440 | tf_op jit(solution)/shard_map/all_to_all | solution.py:651
  114.5 26.7 %collective-permute-start.8 = (bf16[384,512]{1,0:T(8,128)(2,1)S(1)}, bf16[384,512]{1,0:T(8,128)(2,1)S(1)}, u32[]{:S(2)}, u32[]{:S(2)}) collective-permute-start(bf16[384,512]{1,0:T(8,128)(2,1)S(1)} %copy-done.8), channel_id=1, source_target_pairs={{2,0},{3,1},{4,2},{5,3},{6,4},{7,5},{8,6},{9,7},{10,8},{11,9},{12,... | collective-permute-start | bytes 1179656 | tf_op jit(solution)/shard_map/ppermute | solution.py:619
  132.2 11.7 %collective-permute-start.9 = (bf16[10,512,128]{2,1,0:T(8,128)(2,1)S(1)}, bf16[10,512,128]{2,1,0:T(8,128)(2,1)S(1)}, u32[]{:S(2)}, u32[]{:S(2)}) collective-permute-start(bf16[10,512,128]{2,1,0:T(8,128)(2,1)S(1)} %bitcast.7), channel_id=1, source_target_pairs={{0,1},{1,0},{2,3},{3,2},{4,5},{5,4},{6,7},{7,6},{8,9},{9,8},{10,11... | collective-permute-start | bytes 3932168 | tf_op jit(solution)/shard_map/ppermute | solution.py:653
  141.2 0.7 copy-start.11
